TPU v7x, 128 devices: a whole 4x4x4 slice. The times are simulated.
128 devices in a mesh: ctx: 8 (over z, y_lo), fsdp: 16 (over y_hi, x, core).
Axes of the slice: x: 4, y: 4 (y_hi: 2, y_lo: 2; y = y_hi * 2 + y_lo), z: 4, core: 2. Of those that a mesh axis runs over, the one named last changes fastest.
Arguments:
- tokens: bfloat16 [2, 16, 1024, 1024], P(None, 'fsdp', 'ctx'), may hold values from -6 to 6
- cotangent: bfloat16 [2, 16, 1024, 1024], P(None, 'fsdp', 'ctx'), may hold values from -6 to 6
- block_table: int32 [2, 16], replicated, may hold values from 0 to 15, as said below
- segment_ids: int32 [2, 16, 1024], P(None, 'fsdp'), may hold values from 0 to 2, as said below
- positions: int32 [2, 16, 1024], P(None, 'fsdp', 'ctx'), may hold values from 0 to 895, as said below
- gain_attn: bfloat16 [1024], P('fsdp'), may hold values from 0.5 to 1.5
- w_query: bfloat16 [1024, 2048], P('fsdp'), may hold values from -0.1875 to 0.1875
- key_projection: bfloat16 [1024, 1024], P('fsdp'), may hold values from -0.1875 to 0.1875
- value_projection: bfloat16 [1024, 1024], P('fsdp'), may hold values from -0.1875 to 0.1875
- query_norm_gain: bfloat16 [128], P('fsdp'), may hold values from 0.099609375 to 1.8984375
- key_norm_gain: bfloat16 [128], P('fsdp'), may hold values from 0.099609375 to 1.8984375
- w_out: bfloat16 [2048, 1024], P('fsdp'), may hold values from -4 to 4
- gain_ffn: bfloat16 [1024], P('fsdp'), may hold values from 0.5 to 1.5
- w_gate: bfloat16 [1024, 3072], P('fsdp'), may hold values from -0.1875 to 0.1875
- w_up: bfloat16 [1024, 3072], P('fsdp'), may hold values from -0.1875 to 0.1875
- w_down: bfloat16 [3072, 1024], P('fsdp'), may hold values from -0.109375 to 0.109375
Outputs:
- output: bfloat16 [2, 16, 1024, 1024], P(None, 'fsdp', 'ctx')
- grad_tokens: float32 [2, 16, 1024, 1024], P(None, 'fsdp', 'ctx')
- grad_gain_attn: float32 [1024], P('fsdp')
- grad_w_query: float32 [1024, 2048], P('fsdp')
- grad_w_key: float32 [1024, 1024], P('fsdp')
- grad_w_value: float32 [1024, 1024], P('fsdp')
- grad_gain_query: float32 [128], P('fsdp')
- grad_gain_key: float32 [128], P('fsdp')
- grad_w_out: float32 [2048, 1024], P('fsdp')
- grad_gain_ffn: float32 [1024], P('fsdp')
- grad_w_gate: float32 [1024, 3072], P('fsdp')
- grad_w_up: float32 [1024, 3072], P('fsdp')
- grad_w_down: float32 [3072, 1024], P('fsdp')
Inputs may be any that keep to these rules, and one draw needn't show every extreme that they name: `block_table`: each row is a permutation of the 16 logical blocks of 64 tokens; storage blocks 2c and 2c + 1 lie on context index c, and one of the two is among the first 8 logical blocks (the prompt), the other among the last. `segment_ids`: in logical order the ids never fall: 512 tokens of 0, then continuation k of 128 to 384 tokens of k, for k = 1 to 2; stored in the tokens' order. In logical order the prompt stands at 0 to 511 and each continuation at consecutive positions that end at 895; stored in the tokens' order.
All inputs are finite; a program needn't handle non-finite values.
Results may differ from a plain program's by a relative error of at most 0.02.
Values may be sent and summed in bfloat16 or wider, within the bound.
A program may use at most 256 MiB of HBM per device.

v0:
```python
import math

import jax
import jax.numpy as jnp
from jax import lax
from jax.sharding import PartitionSpec as P


def rms_gain(value_rows, gain_vec):
    return (
        value_rows
        * lax.rsqrt(jnp.mean(value_rows * value_rows, axis=-1, keepdims=True) + 1e-06)
        * gain_vec
    )


def rope_tables(where_at, head_width):
    frequency = jnp.exp(
        jnp.arange(0, head_width // 2, dtype=jnp.float32)
        * (-2.0 * math.log(1000000.0) / head_width)
    )
    angles = where_at.astype(jnp.float32)[:, None] * frequency[None, :]
    rotary_cosines = jnp.concatenate([jnp.cos(angles), jnp.cos(angles)], axis=-1)
    rotary_sines = jnp.concatenate([jnp.sin(angles), jnp.sin(angles)], axis=-1)
    return (rotary_cosines, rotary_sines)


def prepare_heads(raw_rows, gain_vec, rotary_cosines, rotary_sines):
    head_width = gain_vec.shape[0]
    per_head = raw_rows.reshape(raw_rows.shape[0], raw_rows.shape[1] // head_width, head_width)
    normed = rms_gain(per_head, gain_vec)
    half_width = head_width // 2
    turned = jnp.concatenate([-normed[..., half_width:], normed[..., :half_width]], axis=-1)
    rotated = normed * rotary_cosines[:, None, :] + turned * rotary_sines[:, None, :]
    return rotated.reshape(raw_rows.shape)


def swiglu(gate_pre, up_proj):
    return jax.nn.silu(gate_pre) * up_proj


def across_rows(first_arr, second_arr):
    return lax.dot_general(
        first_arr, second_arr, (((0,), (0,)), ((), ())), preferred_element_type=jnp.float32
    )


def against_cols(first_arr, second_arr):
    return lax.dot_general(
        first_arr, second_arr, (((1,), (1,)), ((), ())), preferred_element_type=jnp.float32
    )


def forward_dot(first_arr, second_arr):
    return jnp.dot(first_arr, second_arr, preferred_element_type=jnp.float32)


def micro_batch(tokens_rows, cot_rows, table_row, segment_all, where_rows, gathered, ctx_index):
    (
        gain_attn,
        w_query,
        key_projection,
        value_projection,
        query_norm_gain,
        key_norm_gain,
        w_out,
        gain_ffn,
        w_gate,
        w_up,
        w_down,
    ) = gathered
    rows_here = tokens_rows.shape[0]
    sequence_length = segment_all.shape[0]
    block_len = rows_here // 2
    head_dim = query_norm_gain.shape[0]
    kv_heads = key_projection.shape[1] // head_dim
    query_group_width = w_query.shape[1] // key_projection.shape[1]
    score_scale = head_dim ** (-0.5)
    slots = jnp.arange(sequence_length, dtype=jnp.int32)
    hits = (slots // block_len)[:, None] == jnp.arange(table_row.shape[0], dtype=jnp.int32)[None, :]
    logical = (
        jnp.sum(jnp.where(hits, table_row[None, :], 0), axis=1) * block_len + slots % block_len
    )
    start_row = ctx_index * rows_here
    logical_here = lax.dynamic_slice_in_dim(logical, start_row, rows_here)
    segment_here = lax.dynamic_slice_in_dim(segment_all, start_row, rows_here)
    visible = (logical[None, :] <= logical_here[:, None]) & (
        (segment_all[None, :] == 0) | (segment_all[None, :] == segment_here[:, None])
    )
    rotary_cosines, rotary_sines = rope_tables(where_rows, head_dim)

    def prep_rows(raw_rows, gain_vec):
        return prepare_heads(raw_rows, gain_vec, rotary_cosines, rotary_sines)

    inputs = tokens_rows.astype(jnp.float32)
    normed_full, back_in = jax.vjp(rms_gain, inputs, gain_attn.astype(jnp.float32))
    normalized_input = normed_full.astype(jnp.bfloat16)
    projected_queries = forward_dot(normalized_input, w_query)
    projected_keys = forward_dot(normalized_input, key_projection)
    value_raw = forward_dot(normalized_input, value_projection)
    query_full, back_query = jax.vjp(
        prep_rows, projected_queries, query_norm_gain.astype(jnp.float32)
    )
    key_full, back_key = jax.vjp(prep_rows, projected_keys, key_norm_gain.astype(jnp.float32))
    query_rows = query_full.astype(jnp.bfloat16)
    keys_low = key_full.astype(jnp.bfloat16)
    values_low = value_raw.astype(jnp.bfloat16)
    keys_all, values_all = (
        lax.all_gather(keys_low, "ctx", axis=0, tiled=True),
        lax.all_gather(values_low, "ctx", axis=0, tiled=True),
    )
    query_heads = query_rows.reshape(rows_here, kv_heads, query_group_width, head_dim)
    key_heads = keys_all.reshape(sequence_length, kv_heads, head_dim)
    value_heads = values_all.reshape(sequence_length, kv_heads, head_dim)

    def masked_scores():
        raw_scores = (
            jnp.einsum("qkgd,pkd->kgqp", query_heads, key_heads, preferred_element_type=jnp.float32)
            * score_scale
        )
        return jnp.where(visible[None, None], raw_scores, -1e30)

    scores = masked_scores()
    row_peak = jnp.max(scores, axis=-1, keepdims=True)
    shifted = jnp.exp(scores - row_peak)
    row_total = jnp.sum(shifted, axis=-1, keepdims=True)
    attn_probs = shifted / row_total
    log_total = row_peak + jnp.log(row_total)
    probs_low = attn_probs.astype(jnp.bfloat16)
    mixed = jnp.einsum("kgqp,pkd->qkgd", probs_low, value_heads, preferred_element_type=jnp.float32)
    mixed = mixed.reshape(rows_here, -1).astype(jnp.bfloat16)
    attended = inputs + forward_dot(mixed, w_out)
    normed_mid_full, back_mid = jax.vjp(rms_gain, attended, gain_ffn.astype(jnp.float32))
    normed_mid = normed_mid_full.astype(jnp.bfloat16)
    gate_pre = forward_dot(normed_mid, w_gate)
    up_proj = forward_dot(normed_mid, w_up)
    swiglu_out, back_act = jax.vjp(swiglu, gate_pre, up_proj)
    hidden = swiglu_out.astype(jnp.bfloat16)
    output_rows = (attended + forward_dot(hidden, w_down)).astype(jnp.bfloat16)
    cot_full = cot_rows.astype(jnp.float32)
    grad_down = across_rows(hidden, cot_rows)
    g_hidden = against_cols(cot_rows, w_down)
    g_gate_full, g_up_full = back_act(g_hidden)
    g_gate = g_gate_full.astype(jnp.bfloat16)
    g_up = g_up_full.astype(jnp.bfloat16)
    grad_gate = across_rows(normed_mid, g_gate)
    grad_up = across_rows(normed_mid, g_up)
    g_mid = against_cols(g_gate, w_gate) + against_cols(g_up, w_up)
    g_att_norm, grad_ffn_gain = back_mid(g_mid)
    g_attended = cot_full + g_att_norm
    g_attn = g_attended.astype(jnp.bfloat16)
    grad_out = across_rows(mixed, g_attn)
    g_mixed = (
        against_cols(g_attn, w_out)
        .astype(jnp.bfloat16)
        .reshape(rows_here, kv_heads, query_group_width, head_dim)
    )
    again_probs = jnp.exp(masked_scores() - log_total)
    again_low = again_probs.astype(jnp.bfloat16)
    g_probs = jnp.einsum("qkgd,pkd->kgqp", g_mixed, value_heads, preferred_element_type=jnp.float32)
    row_inner = jnp.sum(again_probs * g_probs, axis=-1, keepdims=True)
    g_scores = (again_probs * (g_probs - row_inner)).astype(jnp.bfloat16)
    g_queries = (
        jnp.einsum("kgqp,pkd->qkgd", g_scores, key_heads, preferred_element_type=jnp.float32)
        * score_scale
    )
    g_keys_part = (
        jnp.einsum("kgqp,qkgd->pkd", g_scores, query_heads, preferred_element_type=jnp.float32)
        * score_scale
    )
    g_values_part = jnp.einsum(
        "kgqp,qkgd->pkd", again_low, g_mixed, preferred_element_type=jnp.float32
    )
    g_keys, g_values = (
        lax.psum_scatter(
            g_keys_part.reshape(sequence_length, -1).astype(jnp.bfloat16),
            "ctx",
            scatter_dimension=0,
            tiled=True,
        ).astype(jnp.float32),
        lax.psum_scatter(
            g_values_part.reshape(sequence_length, -1).astype(jnp.bfloat16),
            "ctx",
            scatter_dimension=0,
            tiled=True,
        ).astype(jnp.float32),
    )
    g_query_full, grad_query_gain = back_query(g_queries.reshape(rows_here, -1))
    g_key_full, grad_key_gain = back_key(g_keys)
    g_query_raw = g_query_full.astype(jnp.bfloat16)
    g_key_raw = g_key_full.astype(jnp.bfloat16)
    g_value_raw = g_values.astype(jnp.bfloat16)
    grad_query = across_rows(normalized_input, g_query_raw)
    grad_key = across_rows(normalized_input, g_key_raw)
    grad_value = across_rows(normalized_input, g_value_raw)
    g_in = (
        against_cols(g_query_raw, w_query)
        + against_cols(g_key_raw, key_projection)
        + against_cols(g_value_raw, value_projection)
    )
    g_input_norm, grad_attn_gain = back_in(g_in)
    grad_rows = g_attended + g_input_norm
    term_list = (
        grad_attn_gain,
        grad_query,
        grad_key,
        grad_value,
        grad_query_gain,
        grad_key_gain,
        grad_out,
        grad_ffn_gain,
        grad_gate,
        grad_up,
        grad_down,
    )
    return (output_rows, grad_rows, term_list)


def per_device(
    tokens,
    cotangent,
    block_table,
    segment_ids,
    positions,
    gain_attn,
    w_query,
    key_projection,
    value_projection,
    query_norm_gain,
    key_norm_gain,
    w_out,
    gain_ffn,
    w_gate,
    w_up,
    w_down,
):
    ctx_index = lax.axis_index("ctx")
    outputs_all = []
    input_grads = []
    totals = None
    for batch_index in range(tokens.shape[0]):
        gathered = (
            lax.all_gather(gain_attn, "fsdp", axis=0, tiled=True),
            lax.all_gather(w_query, "fsdp", axis=0, tiled=True),
            lax.all_gather(key_projection, "fsdp", axis=0, tiled=True),
            lax.all_gather(value_projection, "fsdp", axis=0, tiled=True),
            lax.all_gather(query_norm_gain, "fsdp", axis=0, tiled=True),
            lax.all_gather(key_norm_gain, "fsdp", axis=0, tiled=True),
            lax.all_gather(w_out, "fsdp", axis=0, tiled=True),
            lax.all_gather(gain_ffn, "fsdp", axis=0, tiled=True),
            lax.all_gather(w_gate, "fsdp", axis=0, tiled=True),
            lax.all_gather(w_up, "fsdp", axis=0, tiled=True),
            lax.all_gather(w_down, "fsdp", axis=0, tiled=True),
        )
        output_rows, grad_rows, term_list = micro_batch(
            tokens[batch_index, 0],
            cotangent[batch_index, 0],
            block_table[batch_index],
            segment_ids[batch_index, 0],
            positions[batch_index, 0],
            gathered,
            ctx_index,
        )
        outputs_all.append(output_rows)
        input_grads.append(grad_rows)
        totals = (
            term_list
            if totals is None
            else tuple((earlier + latest for earlier, latest in zip(totals, term_list)))
        )
    shares = (
        lax.psum_scatter(totals[0], "fsdp", scatter_dimension=0, tiled=True),
        lax.psum_scatter(totals[1], "fsdp", scatter_dimension=0, tiled=True),
        lax.psum_scatter(totals[2], "fsdp", scatter_dimension=0, tiled=True),
        lax.psum_scatter(totals[3], "fsdp", scatter_dimension=0, tiled=True),
        lax.psum_scatter(totals[4], "fsdp", scatter_dimension=0, tiled=True),
        lax.psum_scatter(totals[5], "fsdp", scatter_dimension=0, tiled=True),
        lax.psum_scatter(totals[6], "fsdp", scatter_dimension=0, tiled=True),
        lax.psum_scatter(totals[7], "fsdp", scatter_dimension=0, tiled=True),
        lax.psum_scatter(totals[8], "fsdp", scatter_dimension=0, tiled=True),
        lax.psum_scatter(totals[9], "fsdp", scatter_dimension=0, tiled=True),
        lax.psum_scatter(totals[10], "fsdp", scatter_dimension=0, tiled=True),
    )
    summed = (
        lax.psum(shares[0].astype(jnp.bfloat16), "ctx").astype(jnp.float32),
        lax.psum(shares[1].astype(jnp.bfloat16), "ctx").astype(jnp.float32),
        lax.psum(shares[2].astype(jnp.bfloat16), "ctx").astype(jnp.float32),
        lax.psum(shares[3].astype(jnp.bfloat16), "ctx").astype(jnp.float32),
        lax.psum(shares[4].astype(jnp.bfloat16), "ctx").astype(jnp.float32),
        lax.psum(shares[5].astype(jnp.bfloat16), "ctx").astype(jnp.float32),
        lax.psum(shares[6].astype(jnp.bfloat16), "ctx").astype(jnp.float32),
        lax.psum(shares[7].astype(jnp.bfloat16), "ctx").astype(jnp.float32),
        lax.psum(shares[8].astype(jnp.bfloat16), "ctx").astype(jnp.float32),
        lax.psum(shares[9].astype(jnp.bfloat16), "ctx").astype(jnp.float32),
        lax.psum(shares[10].astype(jnp.bfloat16), "ctx").astype(jnp.float32),
    )
    return (
        jnp.stack(outputs_all)[:, None],
        jnp.stack(input_grads)[:, None],
        summed[0],
        summed[1],
        summed[2],
        summed[3],
        summed[4],
        summed[5],
        summed[6],
        summed[7],
        summed[8],
        summed[9],
        summed[10],
    )


def solution(mesh):
    placed = (
        P(None, "fsdp", "ctx", None),
        P(None, "fsdp", "ctx", None),
        P(),
        P(None, "fsdp", None),
        P(None, "fsdp", "ctx"),
        P("fsdp"),
        P("fsdp", None),
        P("fsdp", None),
        P("fsdp", None),
        P("fsdp"),
        P("fsdp"),
        P("fsdp", None),
        P("fsdp"),
        P("fsdp", None),
        P("fsdp", None),
        P("fsdp", None),
    )
    return jax.shard_map(
        per_device,
        mesh=mesh,
        in_specs=placed,
        out_specs=(
            P(None, "fsdp", "ctx", None),
            P(None, "fsdp", "ctx", None),
            P("fsdp"),
            P("fsdp", None),
            P("fsdp", None),
            P("fsdp", None),
            P("fsdp"),
            P("fsdp"),
            P("fsdp", None),
            P("fsdp"),
            P("fsdp", None),
            P("fsdp", None),
            P("fsdp", None),
        ),
        check_vma=False,
    )
```

profile of v0, /device:TPU:1, one launch (start us, length us, event | category | flops | bytes accessed | tf_op | source)
XLA Modules:
  0.0 1782.7 jit_solution(12070386807545801654)
XLA Ops:
  14.7 34.8 %all-reduce.17 = (bf16[1024]{0:T(1024)(128)(2,1)S(1)}, bf16[128]{0:T(256)(128)(2,1)S(1)}, bf16[128]{0:T(256)(128)(2,1)S(1)}, bf16[1024]{0:T(1024)(128)(2,1)S(1)}) all-reduce(bf16[1024]{0:T(1024)(128)(2,1)S(1)} %dynamic-update-slice, bf16[128]{0:T(256)(128)(2,1)S(1)} %dynamic-update-slice.1, ...), channel_id=1, replica_groups=mesh['ctx'=8,'fsdp'=16] {'fsdp'}, use_global_device_ids=true, to_apply=%add.8 | all-reduce | flops 2304 | bytes 9216
  50.8 11.7 all-gather.12.cloned.1.call-done
  69.6 42.7 %all-gather.16.cloned.1.call-done = bf16[1024,1024]{1,0:T(8,128)(2,1)} async-done(((bf16[64,1024]{1,0:T(8,128)(2,1)}), bf16[1024,1024]{1,0:T(8,128)(2,1)}) %all-gather.16.cloned.1.call-update) | async-done | bytes 2097168 | tf_op jit(solution)/shard_map/all_gather | solution.py:245
  125.4 39.7 %all-gather.30.cloned.1.call-done = bf16[1024,1024]{1,0:T(8,128)(2,1)} async-done(((bf16[128,1024]{1,0:T(8,128)(2,1)}), bf16[1024,1024]{1,0:T(8,128)(2,1)}) %all-gather.30.cloned.1.call-update) | async-done | bytes 2097168 | tf_op jit(solution)/shard_map/all_gather | solution.py:110
  167.3 51.3 %all-gather.14.cloned.1.call-done = bf16[1024,1024]{1,0:T(8,128)(2,1)} async-done(((bf16[128,1024]{1,0:T(8,128)(2,1)}), bf16[1024,1024]{1,0:T(8,128)(2,1)}) %all-gather.14.cloned.1.call-update) | async-done | bytes 2097168 | tf_op jit(solution)/shard_map/all_gather | solution.py:110
  222.2 54.5 %all-gather.20.cloned.1.call-done = bf16[1024,2048]{1,0:T(8,128)(2,1)} async-done(((bf16[64,2048]{1,0:T(8,128)(2,1)}), bf16[1024,2048]{1,0:T(8,128)(2,1)}) %all-gather.20.cloned.1.call-update) | async-done | bytes 4194320 | tf_op jit(solution)/shard_map/all_gather | solution.py:244
  276.7 6.4 copy.102
  283.1 3.7 multiply_reduce_fusion.5
  289.8 37.6 %all-gather.18.cloned.1.call-done = bf16[1024,1024]{0,1:T(8,128)(2,1)} async-done(((bf16[128,1024]{0,1:T(8,128)(2,1)}), bf16[1024,1024]{0,1:T(8,128)(2,1)}) %all-gather.18.cloned.1.call-update) | async-done | bytes 2097168 | tf_op jit(solution)/shard_map/all_gather | solution.py:109
  334.2 14.2 fusion.41
  348.4 39.7 %all-gather.22.cloned.1.call-done = bf16[2048,1024]{1,0:T(8,128)(2,1)} async-done(((bf16[128,1024]{1,0:T(8,128)(2,1)}), bf16[2048,1024]{1,0:T(8,128)(2,1)}) %all-gather.22.cloned.1.call-update) | async-done | bytes 4194320 | tf_op jit(solution)/shard_map/all_gather | solution.py:249
  393.0 46.0 %all-gather.32.cloned.1.call-done = bf16[1024,1024]{0,1:T(8,128)(2,1)} async-done(((bf16[128,1024]{0,1:T(8,128)(2,1)}), bf16[1024,1024]{0,1:T(8,128)(2,1)}) %all-gather.32.cloned.1.call-update) | async-done | bytes 2097168 | tf_op jit(solution)/shard_map/all_gather | solution.py:109
  450.1 57.8 %all-gather.24.cloned.1.call-done = bf16[1024,3072]{1,0:T(8,128)(2,1)} async-done(((bf16[64,3072]{1,0:T(8,128)(2,1)}), bf16[1024,3072]{1,0:T(8,128)(2,1)}) %all-gather.24.cloned.1.call-update) | async-done | bytes 6291472 | tf_op jit(solution)/shard_map/all_gather | solution.py:251
  507.9 4.9 fusion.170
  512.8 60.0 %all-gather.26.cloned.1.call-done = bf16[1024,3072]{1,0:T(8,128)(2,1)} async-done(((bf16[64,3072]{1,0:T(8,128)(2,1)}), bf16[1024,3072]{1,0:T(8,128)(2,1)}) %all-gather.26.cloned.1.call-update) | async-done | bytes 6291472 | tf_op jit(solution)/shard_map/all_gather | solution.py:252
  572.8 4.9 fusion.171
  577.8 60.2 %all-gather.28.cloned.1.call-done = bf16[3072,1024]{1,0:T(8,128)(2,1)} async-done(((bf16[192,1024]{1,0:T(8,128)(2,1)}), bf16[3072,1024]{1,0:T(8,128)(2,1)}) %all-gather.28.cloned.1.call-update) | async-done | bytes 6291472 | tf_op jit(solution)/shard_map/all_gather | solution.py:253
  637.9 7.2 multiply_convert_fusion.1
  645.2 5.6 fusion.174
  671.6 6.1 fusion.3
  684.7 4.0 copy.159
  690.1 4.5 convolution_convert_fusion
  696.7 5.0 fusion
  710.7 5.2 bitcast_convert_fusion.1
  718.6 5.2 bitcast_convert_fusion
  726.4 13.0 reduce-scatter.34.cloned.1.call-done
  740.6 53.1 %reduce-scatter.38.cloned.1.call-done = bf16[128,1024]{1,0:T(8,128)(2,1)} async-done(((bf16[1024,1024]{1,0:T(8,128)(2,1)}), bf16[128,1024]{1,0:T(8,128)(2,1)}) %reduce-scatter.38.cloned.1.call-update) | async-done | bytes 262160
  805.2 42.5 %reduce-scatter.36.cloned.1.call-done = bf16[128,1024]{1,0:T(8,128)(2,1)} async-done(((bf16[1024,1024]{1,0:T(8,128)(2,1)}), bf16[128,1024]{1,0:T(8,128)(2,1)}) %reduce-scatter.36.cloned.1.call-update) | async-done | bytes 262160
  847.8 3.7 fusion.130
  851.5 50.4 %reduce-scatter.40.cloned.1.call-done = bf16[128,1024]{1,0:T(8,128)(2,1)} async-done(((bf16[1024,1024]{1,0:T(8,128)(2,1)}), bf16[128,1024]{1,0:T(8,128)(2,1)}) %reduce-scatter.40.cloned.1.call-update) | async-done | bytes 262160
  901.8 5.0 convolution_add_fusion.5
  920.3 4.7 convolution_add_fusion.4
  927.5 4.5 convolution_add_fusion.3
  935.0 6.6 convolution_add_fusion.2
  944.5 6.4 convolution_add_fusion.1
  954.0 6.4 convolution_add_fusion
  962.2 3.8 fusion.48
  966.0 4.2 fusion.49
  974.3 9.7 reduce-scatter.22.cloned.1.call-done
  985.6 82.0 %reduce-scatter.24.cloned.1.call-done = f32[64,1024]{1,0:T(8,128)} async-done(((f32[1024,1024]{1,0:T(8,128)}), f32[64,1024]{1,0:T(8,128)}) %reduce-scatter.24.cloned.1.call-update) | async-done | bytes 262160 | tf_op jit(solution)/shard_map/reduce_scatter | solution.py:275
  1069.2 104.3 %reduce-scatter.20.cloned.1.call-done = f32[64,2048]{1,0:T(8,128)} async-done(((f32[1024,2048]{1,0:T(8,128)}), f32[64,2048]{1,0:T(8,128)}) %reduce-scatter.20.cloned.1.call-update) | async-done | bytes 524304 | tf_op jit(solution)/shard_map/reduce_scatter | solution.py:273
  1175.3 103.9 %reduce-scatter.26.cloned.1.call-done = f32[128,1024]{1,0:T(8,128)} async-done(((f32[2048,1024]{1,0:T(8,128)}), f32[128,1024]{1,0:T(8,128)}) %reduce-scatter.26.cloned.1.call-update) | async-done | bytes 524304 | tf_op jit(solution)/shard_map/reduce_scatter | solution.py:278
  1281.0 123.9 %reduce-scatter.28.cloned.1.call-done = f32[64,3072]{1,0:T(8,128)} async-done(((f32[1024,3072]{1,0:T(8,128)}), f32[64,3072]{1,0:T(8,128)}) %reduce-scatter.28.cloned.1.call-update) | async-done | bytes 786448 | tf_op jit(solution)/shard_map/reduce_scatter | solution.py:280
  1406.9 123.8 %reduce-scatter.30.cloned.1.call-done = f32[64,3072]{1,0:T(8,128)} async-done(((f32[1024,3072]{1,0:T(8,128)}), f32[64,3072]{1,0:T(8,128)}) %reduce-scatter.30.cloned.1.call-update) | async-done | bytes 786448 | tf_op jit(solution)/shard_map/reduce_scatter | solution.py:281
  1532.6 123.1 %reduce-scatter.32.cloned.1.call-done = f32[192,1024]{1,0:T(8,128)} async-done(((f32[3072,1024]{1,0:T(8,128)}), f32[192,1024]{1,0:T(8,128)}) %reduce-scatter.32.cloned.1.call-update) | async-done | bytes 786448 | tf_op jit(solution)/shard_map/reduce_scatter | solution.py:282
  1665.6 61.4 %all-reduce.16 = (bf16[1024]{0:T(1024)(128)(2,1)S(1)}, bf16[128]{0:T(256)(128)(2,1)S(1)}, bf16[128]{0:T(256)(128)(2,1)S(1)}, bf16[1024]{0:T(1024)(128)(2,1)S(1)}) all-reduce(f32[1024]{0:T(1024)S(1)} %add.334, f32[128]{0:T(128)S(1)} %add.338, f32[128]{0:T(128)S(1)} %add.339, ...), channel_id=6, replica_groups=mesh['ctx'=8,'fsdp'=16] {'fsdp'}, use_global_device_ids=true, to_apply=%region_30.31.clone | all-reduce | flops 2304 | bytes 13824
  1727.3 16.9 all-reduce.18
  1747.6 16.7 all-reduce.22.cloned.1.call-done
  (459 shorter events, 181.0 us)
Async XLA Ops:
  7.2 62.0 %copy-start.110 = (s32[2,1,128]{2,1,0:T(1,128)S(1)}, s32[2,1,128]{2,1,0:T(1,128)}, u32[]{:S(2)}) copy-start(s32[2,1,128]{2,1,0:T(1,128)} %param.20) | copy-start | bytes 3076
  7.2 55.4 %all-gather.12.cloned.1.call-start = ((), (), s32[]{:S(2)}) async-start(), calls=%async_computation.11 | async-start | bytes 2228224 | tf_op jit(solution)/shard_map/all_gather | solution.py:246
  7.9 104.3 %all-gather.16.cloned.1.call-start = ((), (), s32[]{:S(2)}) async-start(), calls=%async_computation.13 | async-start | bytes 2228224 | tf_op jit(solution)/shard_map/all_gather | solution.py:245
  8.7 156.4 %all-gather.30.cloned.1.call-start = ((), (), s32[]{:S(2)}) async-start(), calls=%async_computation.20 | async-start | bytes 2359296 | tf_op jit(solution)/shard_map/all_gather | solution.py:110
  50.8 18.4 %copy-start.108 = (f32[128]{0:T(128)}, f32[128]{0:T(128)S(1)}, u32[]{:S(2)}) copy-start(f32[128]{0:T(128)S(1)} %get-tuple-element.84) | copy-start | bytes 1540
  50.8 236.0 %copy-start.93 = (f32[128]{0:T(128)}, f32[128]{0:T(128)S(1)}, u32[]{:S(2)}) copy-start(f32[128]{0:T(128)S(1)} %fusion.150) | copy-start | bytes 1540
  65.4 49.7 %copy-start.5 = (bf16[2,1,128,1024]{3,2,1,0:T(8,128)(2,1)S(1)}, bf16[2,1,128,1024]{3,2,1,0:T(8,128)(2,1)}, u32[]{:S(2)}) copy-start(bf16[2,1,128,1024]{3,2,1,0:T(8,128)(2,1)} %param.16) | copy-start | bytes 1572868
  65.5 153.2 %all-gather.14.cloned.1.call-start = ((), (), s32[]{:S(2)}) async-start(), calls=%async_computation.12 | async-start | bytes 2359296 | tf_op jit(solution)/shard_map/all_gather | solution.py:110
  65.5 217.6 %copy-start.88 = (f32[128]{0:T(128)}, f32[128]{0:T(128)S(1)}, u32[]{:S(2)}) copy-start(f32[128]{0:T(128)S(1)} %fusion.148) | copy-start | bytes 1540
  68.5 208.2 %all-gather.20.cloned.1.call-start = ((), (), s32[]{:S(2)}) async-start(), calls=%async_computation.15 | async-start | bytes 4456448 | tf_op jit(solution)/shard_map/all_gather | solution.py:244
  69.1 258.3 %all-gather.18.cloned.1.call-start = ((), (), s32[]{:S(2)}) async-start(), calls=%async_computation.14 | async-start | bytes 2359296 | tf_op jit(solution)/shard_map/all_gather | solution.py:109
  69.2 47.7 %copy-start.100 = (f32[128]{0:T(128)}, f32[128]{0:T(128)S(1)}, u32[]{:S(2)}) copy-start(f32[128]{0:T(128)S(1)} %convert_element_type.342) | copy-start | bytes 1540
  69.6 48.1 %copy-start.65 = (f32[128,128]{0,1:T(8,128)}, f32[128,128]{0,1:T(8,128)S(1)}, u32[]{:S(2)}) copy-start(f32[128,128]{0,1:T(8,128)S(1)} %pad_maximum_fusion.1) | copy-start | bytes 196612
  118.5 269.6 %all-gather.22.cloned.1.call-start = ((), (), s32[]{:S(2)}) async-start(), calls=%async_computation.16 | async-start | bytes 4456448 | tf_op jit(solution)/shard_map/all_gather | solution.py:249
  119.2 319.8 %all-gather.32.cloned.1.call-start = ((), (), s32[]{:S(2)}) async-start(), calls=%async_computation.21 | async-start | bytes 2359296 | tf_op jit(solution)/shard_map/all_gather | solution.py:109
  119.3 45.8 %copy-start.68 = (f32[128,128]{0,1:T(8,128)}, f32[128,128]{0,1:T(8,128)S(1)}, u32[]{:S(2)}) copy-start(f32[128,128]{0,1:T(8,128)S(1)} %pad_maximum_fusion.3) | copy-start | bytes 196612
  120.2 387.7 %all-gather.24.cloned.1.call-start = ((), (), s32[]{:S(2)}) async-start(), calls=%async_computation.17 | async-start | bytes 6684672 | tf_op jit(solution)/shard_map/all_gather | solution.py:251
  120.9 451.9 %all-gather.26.cloned.1.call-start = ((), (), s32[]{:S(2)}) async-start(), calls=%async_computation.18 | async-start | bytes 6684672 | tf_op jit(solution)/shard_map/all_gather | solution.py:252
  121.5 516.4 %all-gather.28.cloned.1.call-start = ((), (), s32[]{:S(2)}) async-start(), calls=%async_computation.19 | async-start | bytes 6684672 | tf_op jit(solution)/shard_map/all_gather | solution.py:253
  122.3 617.2 %reduce-scatter.34.cloned.1.call-start = ((), (), s32[]{:S(2)}) async-start(), calls=%async_computation.29 | async-start | bytes 2359296
  122.7 165.6 %copy-start.101 = (f32[128]{0:T(128)}, f32[128]{0:T(128)S(1)}, u32[]{:S(2)}) copy-start(f32[128]{0:T(128)S(1)} %convert_element_type.347) | copy-start | bytes 1540
  289.8 40.8 %copy-start.41 = (bf16[128,16,128]{0,2,1:T(8,128)(2,1)}, bf16[128,16,128]{0,2,1:T(8,128)(2,1)S(1)}, u32[]{:S(2)}) copy-start(bf16[128,16,128]{0,2,1:T(8,128)(2,1)S(1)} %fusion.53) | copy-start | bytes 1572868
  348.4 43.7 %copy-start.69 = (f32[128,128]{0,1:T(8,128)S(1)}, f32[128,128]{0,1:T(8,128)}, u32[]{:S(2)}) copy-start(f32[128,128]{0,1:T(8,128)} %copy-done.68) | copy-start | bytes 196612
  391.4 50.9 %copy-start.116 = (f32[128]{0:T(128)}, f32[128]{0:T(128)S(1)}, u32[]{:S(2)}) copy-start(f32[128]{0:T(128)S(1)} %get-tuple-element.174) | copy-start | bytes 1540
  391.4 274.7 %copy-start.18 = (f32[128,1024]{1,0:T(8,128)}, f32[128,1024]{1,0:T(8,128)S(1)}, u32[]{:S(2)}) copy-start(f32[128,1024]{1,0:T(8,128)S(1)} %get-tuple-element.175) | copy-start | bytes 1572868
  450.0 122.8 %copy-start.22 = (bf16[128,1024]{1,0:T(8,128)(2,1)}, bf16[128,1024]{1,0:T(8,128)(2,1)S(1)}, u32[]{:S(2)}) copy-start(bf16[128,1024]{1,0:T(8,128)(2,1)S(1)} %multiply_convert_fusion.5) | copy-start | bytes 786436
  688.7 104.9 %reduce-scatter.38.cloned.1.call-start = ((), (), s32[]{:S(2)}) async-start(), calls=%async_computation.31 | async-start | bytes 2359296
  710.6 137.1 %reduce-scatter.36.cloned.1.call-start = ((), (), s32[]{:S(2)}) async-start(), calls=%async_computation.30 | async-start | bytes 2359296
  718.5 183.3 %reduce-scatter.40.cloned.1.call-start = ((), (), s32[]{:S(2)}) async-start(), calls=%async_computation.32 | async-start | bytes 2359296
  726.3 70.4 %copy-start.28 = (f32[128,8,128]{0,2,1:T(8,128)S(1)}, f32[128,8,128]{0,2,1:T(8,128)}, u32[]{:S(2)}) copy-start(f32[128,8,128]{0,2,1:T(8,128)} %copy-done.27) | copy-start | bytes 1572868
  726.3 70.4 %copy-start.30 = (f32[128,8,128]{0,2,1:T(8,128)S(1)}, f32[128,8,128]{0,2,1:T(8,128)}, u32[]{:S(2)}) copy-start(f32[128,8,128]{0,2,1:T(8,128)} %copy-done.29) | copy-start | bytes 1572868
  726.3 70.4 %copy-start.85 = (f32[128,8]{0,1:T(8,128)S(1)}, f32[128,8]{0,1:T(8,128)}, u32[]{:S(2)}) copy-start(f32[128,8]{0,1:T(8,128)} %copy-done.84) | copy-start | bytes 12292
  726.3 70.4 %copy-start.87 = (f32[128,8]{0,1:T(8,128)S(1)}, f32[128,8]{0,1:T(8,128)}, u32[]{:S(2)}) copy-start(f32[128,8]{0,1:T(8,128)} %copy-done.86) | copy-start | bytes 12292
  726.4 257.6 %reduce-scatter.22.cloned.1.call-start = ((), (), s32[]{:S(2)}) async-start(), calls=%async_computation.23 | async-start | bytes 4456448 | tf_op jit(solution)/shard_map/reduce_scatter | solution.py:274
  805.2 96.7 %copy-start.95 = (f32[128]{0:T(128)S(1)}, f32[128]{0:T(128)}, u32[]{:S(2)}) copy-start(f32[128]{0:T(128)} %copy-done.93) | copy-start | bytes 1540
  805.2 262.4 %reduce-scatter.24.cloned.1.call-start = ((), (), s32[]{:S(2)}) async-start(), calls=%async_computation.24 | async-start | bytes 4456448 | tf_op jit(solution)/shard_map/reduce_scatter | solution.py:275
  906.9 266.6 %reduce-scatter.20.cloned.1.call-start = ((), (), s32[]{:S(2)}) async-start(), calls=%async_computation.22 | async-start | bytes 8912896 | tf_op jit(solution)/shard_map/reduce_scatter | solution.py:273
  925.0 354.2 %reduce-scatter.26.cloned.1.call-start = ((), (), s32[]{:S(2)}) async-start(), calls=%async_computation.25 | async-start | bytes 8912896 | tf_op jit(solution)/shard_map/reduce_scatter | solution.py:278
  932.0 473.0 %reduce-scatter.28.cloned.1.call-start = ((), (), s32[]{:S(2)}) async-start(), calls=%async_computation.26 | async-start | bytes 13369344 | tf_op jit(solution)/shard_map/reduce_scatter | solution.py:280
  941.6 589.1 %reduce-scatter.30.cloned.1.call-start = ((), (), s32[]{:S(2)}) async-start(), calls=%async_computation.27 | async-start | bytes 13369344 | tf_op jit(solution)/shard_map/reduce_scatter | solution.py:281
  950.9 704.8 %reduce-scatter.32.cloned.1.call-start = ((), (), s32[]{:S(2)}) async-start(), calls=%async_computation.28 | async-start | bytes 13369344 | tf_op jit(solution)/shard_map/reduce_scatter | solution.py:282
  960.5 803.8 %all-reduce.22.cloned.1.call-start = ((), (), s32[]{:S(2)}) async-start(), calls=%async_computation.33 | async-start | bytes 3932160 | tf_op jit(solution)/shard_map/psum | solution.py:286
  1281.0 378.6 %copy-start.56 = (bf16[128,8,128]{0,2,1:T(8,128)(2,1)S(1)}, bf16[128,8,128]{0,2,1:T(8,128)(2,1)}, u32[]{:S(2)}) copy-start(bf16[128,8,128]{0,2,1:T(8,128)(2,1)} %copy-done.55) | copy-start | bytes 786436
  1532.6 129.6 %copy-start.39 = (bf16[128,16,128]{0,2,1:T(8,128)(2,1)S(1)}, bf16[128,16,128]{0,2,1:T(8,128)(2,1)}, u32[]{:S(2)}) copy-start(bf16[128,16,128]{0,2,1:T(8,128)(2,1)} %copy-done.38) | copy-start | bytes 1572868
  1663.7 82.4 %copy-start.107 = (f32[128]{0:T(128)S(1)}, f32[128]{0:T(128)}, u32[]{:S(2)}) copy-start(f32[128]{0:T(128)} %copy-done.106) | copy-start | bytes 1540
  1663.8 82.4 %copy-start.109 = (f32[128]{0:T(128)S(1)}, f32[128]{0:T(128)}, u32[]{:S(2)}) copy-start(f32[128]{0:T(128)} %copy-done.108) | copy-start | bytes 1540
  1663.8 82.4 %copy-start.33 = (f32[128,1024]{1,0:T(8,128)S(1)}, f32[128,1024]{1,0:T(8,128)}, u32[]{:S(2)}) copy-start(f32[128,1024]{1,0:T(8,128)} %copy-done.31) | copy-start | bytes 1572868
  1663.8 82.4 %copy-start.35 = (f32[128,1024]{1,0:T(8,128)S(1)}, f32[128,1024]{1,0:T(8,128)}, u32[]{:S(2)}) copy-start(f32[128,1024]{1,0:T(8,128)} %get-tuple-element.125) | copy-start | bytes 1572868
  (103 other events, 347.4 us)
Sparse Core Ops, SparseCore 0:
  10.5 52.0 all-gather.11
  65.0 47.2 all-gather.15
  114.5 50.5 all-gather.29
  167.2 51.4 all-gather.13
  220.9 55.7 all-gather.19
  278.7 48.7 all-gather.17
  329.9 58.1 all-gather.21
  390.2 48.7 all-gather.31
  441.5 66.3 all-gather.23
  510.2 62.6 all-gather.25
  575.3 62.6 all-gather.27
  688.9 50.5 reduce-scatter.33
  741.8 51.8 reduce-scatter.37
  795.9 51.7 reduce-scatter.35
  850.0 51.7 reduce-scatter.39
  905.7 78.1 reduce-scatter.21
  988.4 79.1 reduce-scatter.23
  1071.8 101.6 reduce-scatter.19
  1177.8 101.3 reduce-scatter.25
  1283.4 121.4 reduce-scatter.27
  1409.9 120.6 reduce-scatter.29
  1535.0 120.6 reduce-scatter.31
  1660.3 103.9 all-reduce.21
where the time goes:
time: 1790 us; the launch traced here: 1780 us
  waiting for transfers between devices  1350 us (75%)
  matrix products  181 us (10%)
  blocking collectives  113 us (6%)
  local copies, waits for them, and re-layouts  60.6 us (3%)
  other arithmetic  55 us (3%)
  between operations  18.8 us (1%)
    unnamed x27, waiting for transfers between devices  164 us
    reduce_scatter x1, waiting for transfers between devices, per_device(): lax.psum_scatter(totals[8], 'fsdp', scatter_dimension=0, tiled=True)  124 us
    reduce_scatter x1, waiting for transfers between devices, per_device(): lax.psum_scatter(totals[9], 'fsdp', scatter_dimension=0, tiled=True)  124 us
    reduce_scatter x1, waiting for transfers between devices, per_device(): lax.psum_scatter(totals[10], 'fsdp', scatter_dimension=0, tiled=True)  123 us
    reduce_scatter x1, waiting for transfers between devices, per_device(): lax.psum_scatter(totals[1], 'fsdp', scatter_dimension=0, tiled=True)  104 us
    reduce_scatter x1, waiting for transfers between devices, per_device(): lax.psum_scatter(totals[6], 'fsdp', scatter_dimension=0, tiled=True)  104 us
    unnamed x2, blocking collectives  96.2 us
    all_gather x2, waiting for transfers between devices, micro_batch(): lax.all_gather(values_low, 'ctx', axis=0, tiled=True)  91 us
  transfers between devices with their start and end apart: 23, of which 23 were waited for; matrix products, arithmetic and copies ran while one was open for 12% of the time, Pallas kernels for 0%

commit v1 on v0

v1 whole, which is shorter than its diff:
```python
import functools
import math

import jax
import jax.numpy as jnp
from jax import lax
from jax.experimental import pallas as pl
from jax.experimental.pallas import tpu as pltpu
from jax.sharding import PartitionSpec as P

MESH = pl.DeviceIdType.MESH
SIZES = {"z": 4, "yl": 2, "yh": 2, "x": 4, "core": 2}
BF = jnp.bfloat16
F32 = jnp.float32
HEAD = 128


def my_place():
    c = lax.axis_index("ctx")
    f = lax.axis_index("fsdp")
    return {"z": c // 2, "yl": c % 2, "yh": f // 8, "x": (f // 2) % 4, "core": f % 2}


def moved(me, shift):
    to = dict(me)
    for axis, step in shift.items():
        to[axis] = (me[axis] + (step % SIZES[axis])) % SIZES[axis]
    return to


def ctx_of(place):
    return place["z"] * 2 + place["yl"]


def tp_of(place):
    return place["x"] * 2 + place["core"]


def chip_of(place):
    return place["yh"] * 4 + place["x"]


def fsdp_of(place):
    return chip_of(place) * 2 + place["core"]


def device_of(place):
    return (ctx_of(place), fsdp_of(place))


CTX_SHIFTS = [{"z": a, "yl": b} for a in range(4) for b in range(2) if a or b]
PLANE_SHIFTS = [
    {"yh": a, "x": b, "core": d}
    for a in range(2)
    for b in range(4)
    for d in range(2)
    if a or b or d
]
CHIP_SHIFTS = [{"yh": a, "x": b} for a in range(2) for b in range(4) if a or b]
TP_SHIFTS = [{"x": b, "core": d} for b in range(4) for d in range(2) if b or d]
COPY_SHIFTS = [
    {"z": a, "yl": b, "yh": d}
    for a in range(4)
    for b in range(2)
    for d in range(2)
    if a or b or d
]
RING_Z = [{"z": 1}, {"z": 3}, {"yl": 1}]
RING_X = [{"x": 1}, {"x": 3}, {"core": 1}]


class Net:
    def __init__(self, send_sems, recv_sems, local_sems):
        self.me = my_place()
        self.send_sems, self.recv_sems, self.local_sems = send_sems, recv_sems, local_sems
        self.count = 0
        self.locals = 0
        self.pending = []

    def enter(self, shifts):
        barrier = pltpu.get_barrier_semaphore()
        for shift in shifts:
            pl.semaphore_signal(
                barrier, inc=1, device_id=device_of(moved(self.me, shift)), device_id_type=MESH
            )
        pl.semaphore_wait(barrier, len(shifts))

    def send(self, src, dst, **shift):
        at = self.count
        self.count += 1
        copy = pltpu.make_async_remote_copy(
            src_ref=src,
            dst_ref=dst,
            send_sem=self.send_sems.at[at],
            recv_sem=self.recv_sems.at[at],
            device_id=device_of(moved(self.me, shift)),
            device_id_type=MESH,
        )
        copy.start()
        self.pending.append(copy.wait_send)
        return copy

    def local(self, src, dst):
        copy = pltpu.make_async_copy(src, dst, self.local_sems.at[self.locals])
        self.locals += 1
        copy.start()
        self.pending.append(copy.wait)
        return copy

    def finish(self):
        for wait in self.pending:
            wait()


def run_tasks(tasks):
    tasks = list(tasks)
    while tasks:
        left = []
        for task in tasks:
            try:
                next(task)
                left.append(task)
            except StopIteration:
                pass
        tasks = left


def unique(shifts):
    seen, out = set(), []
    for shift in shifts:
        key = tuple(sorted((k, v) for k, v in shift.items() if v))
        if key not in seen:
            seen.add(key)
            out.append(shift)
    return out


def comm_call(body, shifts, outs, scratch, cid, in_vmem, out_vmem, n_remote, n_local=1):
    shifts = unique(shifts)

    def kernel(*refs):
        refs, sems = refs[:-3], refs[-3:]
        net = Net(*sems)
        net.enter(shifts)
        run_tasks(body(net, *refs))
        net.finish()

    vm = pl.BlockSpec(memory_space=pltpu.VMEM)
    hb = pl.BlockSpec(memory_space=pl.ANY)
    return pl.pallas_call(
        kernel,
        out_shape=[jax.ShapeDtypeStruct(s, d) for s, d in outs],
        in_specs=[vm if v else hb for v in in_vmem],
        out_specs=[vm if v else hb for v in out_vmem],
        scratch_shapes=list(scratch)
        + [
            pltpu.SemaphoreType.DMA((n_remote,)),
            pltpu.SemaphoreType.DMA((n_remote,)),
            pltpu.SemaphoreType.DMA((n_local,)),
        ],
        compiler_params=pltpu.CompilerParams(
            collective_id=cid, has_side_effects=True, vmem_limit_bytes=50 << 20
        ),
    )


def gather_ctx(net, src, out):
    me = net.me

    def at(dz, dy, lo, rows):
        return out.at[:, ctx_of(moved(me, {"z": dz, "yl": dy})), pl.ds(lo, rows)]

    net.local(src, out.at[:, ctx_of(me)])
    src_a, src_b = src.at[:, pl.ds(0, 64)], src.at[:, pl.ds(64, 64)]
    b_y = net.send(src_b, at(0, 0, 64, 64), yl=1)
    a_r = net.send(src_a, at(0, 0, 0, 64), z=1)
    a_l = net.send(src_a, at(0, 0, 0, 64), z=-1)
    b_r = net.send(src_b, at(0, 0, 64, 64), z=1)
    b_l = net.send(src_b, at(0, 0, 64, 64), z=-1)
    a_y = net.send(src_a, at(0, 0, 0, 64), yl=1)
    yield
    b_y.wait_recv()
    c_r = net.send(at(0, 1, 64, 64), at(0, 1, 64, 64), z=1)
    c_l = net.send(at(0, 1, 64, 64), at(0, 1, 64, 64), z=-1)
    yield
    a_r.wait_recv()
    fa_r = net.send(at(-1, 0, 0, 32), at(-1, 0, 0, 32), z=1)
    ya_r = net.send(at(-1, 0, 0, 64), at(-1, 0, 0, 64), yl=1)
    a_l.wait_recv()
    fa_l = net.send(at(1, 0, 32, 32), at(1, 0, 32, 32), z=-1)
    ya_l = net.send(at(1, 0, 0, 64), at(1, 0, 0, 64), yl=1)
    yield
    b_r.wait_recv()
    fb_r = net.send(at(-1, 0, 64, 32), at(-1, 0, 64, 32), z=1)
    b_l.wait_recv()
    fb_l = net.send(at(1, 0, 96, 32), at(1, 0, 96, 32), z=-1)
    yield
    c_r.wait_recv()
    fc_r = net.send(at(-1, 1, 64, 32), at(-1, 1, 64, 32), z=1)
    c_l.wait_recv()
    fc_l = net.send(at(1, 1, 96, 32), at(1, 1, 96, 32), z=-1)
    yield
    fa_r.wait_recv()
    yb_r = net.send(at(2, 0, 0, 32), at(2, 0, 0, 32), yl=1)
    fa_l.wait_recv()
    yb_l = net.send(at(2, 0, 32, 32), at(2, 0, 32, 32), yl=1)
    yield
    for copy in (a_y, ya_r, ya_l, fb_r, fb_l, fc_r, fc_l, yb_r, yb_l):
        copy.wait_recv()


def gather_tp(net, src, out):
    me = net.me

    def at(dx, lo=0, rows=256):
        return out.at[tp_of(moved(me, {"x": dx})), pl.ds(lo, rows)]

    net.local(src, out.at[tp_of(me)])
    r = net.send(src, at(0), x=1)
    l = net.send(src, at(0), x=-1)
    own = net.send(src, at(0), core=1)
    yield
    r.wait_recv()
    fr = net.send(at(-1, 0, 128), at(-1, 0, 128), x=1)
    cr = net.send(at(-1), at(-1), core=1)
    l.wait_recv()
    fl = net.send(at(1, 128, 128), at(1, 128, 128), x=-1)
    cl = net.send(at(1), at(1), core=1)
    yield
    fr.wait_recv()
    c2r = net.send(at(2, 0, 128), at(2, 0, 128), core=1)
    fl.wait_recv()
    c2l = net.send(at(2, 128, 128), at(2, 128, 128), core=1)
    yield
    for copy in (own, cr, cl, c2r, c2l):
        copy.wait_recv()


def add_rows(dst, terms, rows, step=32):
    def one(i, carry):
        at = pl.ds(pl.multiple_of(i * step, step), step)
        total = terms[0][..., at, :].astype(F32)
        for term in terms[1:]:
            total = total + term[..., at, :].astype(F32)
        dst[..., at, :] = total.astype(dst.dtype)
        return carry

    lax.fori_loop(0, rows // step, one, 0)


def reduce_ctx(net, part, total, ry, sa, rha, ra, rhb, sb, rb, su, ru):
    me = net.me

    def at(dz, dy, lo, rows):
        return part.at[:, ctx_of(moved(me, {"z": dz, "yl": dy})), pl.ds(lo, rows)]

    cy = {}
    for dz in (2, 1, 3, 0):
        cy[dz] = net.send(at(dz, 1, 0, 64), ry.at[dz], yl=1)
    hb = {}
    for q in (1, 0):
        hb[q, 0] = net.send(at(2, q, 64, 32), rhb.at[q, 0], z=1)
        hb[q, 1] = net.send(at(2, q, 96, 32), rhb.at[q, 1], z=-1)
    yield
    cy[2].wait_recv()
    add_rows(sa.at[2], [at(2, 0, 0, 64), ry.at[2]], 64)
    ha_r = net.send(sa.at[2, :, pl.ds(0, 32)], rha.at[0], z=1)
    ha_l = net.send(sa.at[2, :, pl.ds(32, 32)], rha.at[1], z=-1)
    yield
    cb = {}
    for q in (1, 0):
        hb[q, 0].wait_recv()
        add_rows(sb.at[q, 0, :, pl.ds(0, 32)], [at(1, q, 64, 32), rhb.at[q, 0]], 32)
        add_rows(sb.at[q, 0, :, pl.ds(32, 32)], [at(1, q, 96, 32)], 32)
        cb[q, 0] = net.send(sb.at[q, 0], rb.at[q, 0], z=1)
        hb[q, 1].wait_recv()
        add_rows(sb.at[q, 1, :, pl.ds(0, 32)], [at(3, q, 64, 32)], 32)
        add_rows(sb.at[q, 1, :, pl.ds(32, 32)], [at(3, q, 96, 32), rhb.at[q, 1]], 32)
        cb[q, 1] = net.send(sb.at[q, 1], rb.at[q, 1], z=-1)
        yield
    cy[1].wait_recv()
    ha_r.wait_recv()
    add_rows(sa.at[1, :, pl.ds(0, 32)], [at(1, 0, 0, 32), ry.at[1, :, pl.ds(0, 32)], rha.at[0]], 32)
    add_rows(sa.at[1, :, pl.ds(32, 32)], [at(1, 0, 32, 32), ry.at[1, :, pl.ds(32, 32)]], 32)
    ca_r = net.send(sa.at[1], ra.at[0], z=1)
    cy[3].wait_recv()
    ha_l.wait_recv()
    add_rows(sa.at[3, :, pl.ds(0, 32)], [at(3, 0, 0, 32), ry.at[3, :, pl.ds(0, 32)]], 32)
    add_rows(sa.at[3, :, pl.ds(32, 32)], [at(3, 0, 32, 32), ry.at[3, :, pl.ds(32, 32)], rha.at[1]], 32)
    ca_l = net.send(sa.at[3], ra.at[1], z=-1)
    yield
    cb[1, 0].wait_recv()
    cb[1, 1].wait_recv()
    add_rows(su, [at(0, 1, 64, 64), rb.at[1, 0], rb.at[1, 1]], 64)
    cu = net.send(su, ru, yl=1)
    yield
    cy[0].wait_recv()
    ca_r.wait_recv()
    ca_l.wait_recv()
    add_rows(total.at[:, pl.ds(0, 64)], [at(0, 0, 0, 64), ry.at[0], ra.at[0], ra.at[1]], 64)
    yield
    cb[0, 0].wait_recv()
    cb[0, 1].wait_recv()
    cu.wait_recv()
    add_rows(total.at[:, pl.ds(64, 64)], [at(0, 0, 64, 64), rb.at[0, 0], rb.at[0, 1], ru], 64)


def reduce_ctx_scratch(width):
    def buf(*lead, rows=64):
        return pltpu.VMEM(lead + (2, rows, width), BF)

    return [
        buf(4),
        buf(4),
        buf(2, rows=32),
        buf(2),
        buf(2, 2, rows=32),
        buf(2, 2),
        buf(2, 2),
        buf(),
        buf(),
    ]


def reduce_tp(net, part, total, rc, s, rh, r):
    me = net.me

    def at(dx, dc, lo=0, rows=256):
        return part.at[tp_of(moved(me, {"x": dx, "core": dc})), pl.ds(lo, rows)]

    cc = {}
    for dx in (2, 1, 3, 0):
        cc[dx] = net.send(at(dx, 1), rc.at[dx], core=1)
    yield
    cc[2].wait_recv()
    add_rows(s.at[2], [at(2, 0), rc.at[2]], 256)
    h_r = net.send(s.at[2, pl.ds(0, 128)], rh.at[0], x=1)
    h_l = net.send(s.at[2, pl.ds(128, 128)], rh.at[1], x=-1)
    cc[1].wait_recv()
    add_rows(s.at[1, pl.ds(128, 128)], [at(1, 0, 128, 128), rc.at[1, pl.ds(128, 128)]], 128)
    cc[3].wait_recv()
    add_rows(s.at[3, pl.ds(0, 128)], [at(3, 0, 0, 128), rc.at[3, pl.ds(0, 128)]], 128)
    yield
    h_r.wait_recv()
    add_rows(s.at[1, pl.ds(0, 128)], [at(1, 0, 0, 128), rc.at[1, pl.ds(0, 128)], rh.at[0]], 128)
    c_r = net.send(s.at[1], r.at[0], x=1)
    h_l.wait_recv()
    add_rows(
        s.at[3, pl.ds(128, 128)], [at(3, 0, 128, 128), rc.at[3, pl.ds(128, 128)], rh.at[1]], 128
    )
    c_l = net.send(s.at[3], r.at[1], x=-1)
    yield
    cc[0].wait_recv()
    c_r.wait_recv()
    c_l.wait_recv()
    add_rows(total, [at(0, 0), rc.at[0], r.at[0], r.at[1]], 256)


def reduce_tp_scratch(width):
    return [
        pltpu.VMEM((4, 256, width), BF),
        pltpu.VMEM((4, 256, width), BF),
        pltpu.VMEM((2, 128, width), BF),
        pltpu.VMEM((2, 256, width), BF),
    ]


def gather_heads_weights(net, src, out):
    me = net.me
    net.local(src, out.at[fsdp_of(me)])
    copies = [net.send(src, out.at[fsdp_of(me)], **shift) for shift in CHIP_SHIFTS]
    passed = [net.send(src, out.at[fsdp_of(me)], core=1)]
    yield
    for shift, copy in zip(CHIP_SHIFTS, copies):
        copy.wait_recv()
        back = {k: -v for k, v in shift.items()}
        slot = out.at[fsdp_of(moved(me, back))]
        passed.append(net.send(slot, slot, core=1))
    yield
    for copy in passed:
        copy.wait_recv()


def gather_out_weights(net, src, mid, out):
    me = net.me
    mine = chip_of(me)
    stay = net.local(src.at[mine], mid.at[mine])
    first = [
        net.send(src.at[chip_of(moved(me, shift))], mid.at[mine], **shift) for shift in CHIP_SHIFTS
    ]
    yield
    for copy in first:
        copy.wait_recv()
    stay.wait()
    net.pending.remove(stay.wait)
    slot = mid.at[ctx_of(me)]
    place = out.at[me["core"], mine]
    net.local(slot, place)
    copies = [net.send(slot, place, **shift) for shift in CHIP_SHIFTS]
    passed = [net.send(slot, place, core=1)]
    yield
    for shift, copy in zip(CHIP_SHIFTS, copies):
        copy.wait_recv()
        back = {k: -v for k, v in shift.items()}
        there = out.at[me["core"], chip_of(moved(me, back))]
        passed.append(net.send(there, there, core=1))
    yield
    for copy in passed:
        copy.wait_recv()


def gather_ff_weights(net, src, down, out, down_out):
    me = net.me
    net.local(src.at[tp_of(me)], out.at[fsdp_of(me)])
    net.local(down, down_out.at[me["yh"]])
    copies = [
        net.send(src.at[tp_of(moved(me, shift))], out.at[fsdp_of(me)], **shift)
        for shift in PLANE_SHIFTS
    ]
    copies.append(net.send(down, down_out.at[me["yh"]], yh=1))
    yield
    for copy in copies:
        copy.wait_recv()


def scatter_plane(net, src, out):
    me = net.me
    net.local(src.at[fsdp_of(me)], out.at[fsdp_of(me)])
    copies = [
        net.send(src.at[fsdp_of(moved(me, shift))], out.at[fsdp_of(me)], **shift)
        for shift in PLANE_SHIFTS
    ]
    yield
    for copy in copies:
        copy.wait_recv()


def copy_index(place):
    return place["yh"] * 8 + ctx_of(place)


def scatter_copies(net, src, down, out, down_out):
    me = net.me

    def piece(place):
        return down.at[place["yh"], :, pl.ds(pl.multiple_of(ctx_of(place) * 128, 128), 128)]

    mine = copy_index(me)
    net.local(src.at[mine], out.at[mine])
    net.local(piece(me), down_out.at[mine])
    copies = []
    for shift in COPY_SHIFTS:
        to = moved(me, shift)
        copies.append(net.send(src.at[copy_index(to)], out.at[mine], **shift))
        copies.append(net.send(piece(to), down_out.at[mine], **shift))
    yield
    for copy in copies:
        copy.wait_recv()


def spread_ctx(net, src, out, after=None):
    me = net.me
    kept = net.local(src, out.at[ctx_of(me)])
    copies = [net.send(src, out.at[ctx_of(me)], **shift) for shift in CTX_SHIFTS]
    yield
    for copy in copies:
        copy.wait_recv()
    if after is None:
        return
    kept.wait()
    net.pending.remove(kept.wait)
    yield
    yield from after()


def exchange_chips(net, src, out):
    me = net.me
    mine = chip_of(me)
    net.local(src.at[mine], out.at[mine])
    copies = [
        net.send(src.at[chip_of(moved(me, shift))], out.at[mine], **shift) for shift in CHIP_SHIFTS
    ]
    yield
    for copy in copies:
        copy.wait_recv()


def exchange_tp(net, src, out):
    me = net.me
    mine = tp_of(me)
    net.local(src.at[mine], out.at[mine])
    copies = [
        net.send(src.at[tp_of(moved(me, shift))], out.at[mine], **shift) for shift in TP_SHIFTS
    ]
    yield
    for copy in copies:
        copy.wait_recv()


def rms_gain(value_rows, gain_vec):
    return (
        value_rows
        * lax.rsqrt(jnp.mean(value_rows * value_rows, axis=-1, keepdims=True) + 1e-06)
        * gain_vec
    )


def rope_tables(where_at):
    frequency = jnp.exp(
        jnp.arange(0, HEAD // 2, dtype=F32) * (-2.0 * math.log(1000000.0) / HEAD)
    )
    angles = where_at.astype(F32)[..., None] * frequency
    cos, sin = jnp.cos(angles), jnp.sin(angles)
    return jnp.concatenate([cos, cos], axis=-1), jnp.concatenate([sin, sin], axis=-1)


def prepare_heads(raw, gain_vec, cos, sin):
    normed = rms_gain(raw, gain_vec)
    half = HEAD // 2
    turned = jnp.concatenate([-normed[..., half:], normed[..., :half]], axis=-1)
    return normed * cos[:, :, None, :] + turned * sin[:, :, None, :]


def across_rows(a, b):
    return lax.dot_general(a, b, (((0,), (0,)), ((), ())), preferred_element_type=F32)


def against_cols(a, b):
    return lax.dot_general(a, b, (((1,), (1,)), ((), ())), preferred_element_type=F32)


def forward_dot(a, b):
    return jnp.dot(a, b, preferred_element_type=F32)


def token_places(block_table, segment_ids):
    mb, blocks = block_table.shape
    seq = segment_ids.shape[-1]
    block = seq // blocks
    logical = (
        jnp.repeat(block_table, block, axis=1) * block + jnp.arange(seq, dtype=jnp.int32) % block
    )
    first = jnp.sum((segment_ids == 1).astype(jnp.int32), axis=1, keepdims=True)
    prompt = seq // 2
    end = jnp.where(segment_ids == 1, prompt - 1 + first, seq - 1)
    position = jnp.where(segment_ids == 0, logical, 895 - (end - logical))
    return logical, position


def per_device(
    tokens,
    cotangent,
    block_table,
    segment_ids,
    positions,
    gain_attn,
    w_query,
    key_projection,
    value_projection,
    query_norm_gain,
    key_norm_gain,
    w_out,
    gain_ffn,
    w_gate,
    w_up,
    w_down,
):
    ctx = lax.axis_index("ctx")
    mbs, width = tokens.shape[0], tokens.shape[-1]
    tok = tokens[:, 0]
    cot = cotangent[:, 0].reshape(256, width)

    def columns(w, n):
        return lax.dynamic_slice_in_dim(w, ctx * n, n, axis=1)

    small = jnp.concatenate(
        [gain_attn, gain_ffn, query_norm_gain, key_norm_gain, jnp.zeros((512 - 144,), BF)]
    )
    wqkv_mine = jnp.concatenate(
        [
            jnp.concatenate(
                [columns(w_query, 256), columns(key_projection, 128), columns(value_projection, 128)],
                axis=1,
            ),
            jnp.broadcast_to(small[None], (16, 512)),
        ],
        axis=0,
    )

    def by_tp(w):
        return w.reshape(64, 2, 8, 192).transpose(2, 0, 1, 3).reshape(8, 64, 384)

    wgu_mine = jnp.concatenate([by_tp(w_gate), by_tp(w_up)], axis=2)

    def first_body(net, tok, cot, wqkv, wo, wgu, wd, xs, cots, wqkvs, mid, wos, wgus, wds):
        return [
            gather_ctx(net, tok, xs),
            gather_heads_weights(net, wqkv, wqkvs),
            gather_out_weights(net, wo, mid, wos),
            gather_tp(net, cot, cots),
            gather_ff_weights(net, wgu, wd, wgus, wds),
        ]

    x_all, cot_all, wqkv_all, _, wo_all, wgu_all, wd_all = comm_call(
        first_body,
        RING_Z + RING_X + PLANE_SHIFTS,
        [
            ((2, 8, 128, width), BF),
            ((8, 256, width), BF),
            ((16, 80, 512), BF),
            ((8, 16, width), BF),
            ((2, 8, 16, width), BF),
            ((16, 64, 768), BF),
            ((2, 192, width), BF),
        ],
        [],
        0,
        [False] * 6,
        [False] * 7,
        100,
        16,
    )(tok, cot, wqkv_mine, w_out.reshape(8, 16, width), wgu_mine, w_down)

    smalls = wqkv_all[:, 64].astype(F32)
    g_attn_gain = smalls[:, :64].reshape(-1)
    g_ffn_gain = smalls[:, 64:128].reshape(-1)
    g_query_gain = smalls[:, 128:136].reshape(-1)
    g_key_gain = smalls[:, 136:144].reshape(-1)
    wqkv = wqkv_all[:, :64].reshape(width, 512)
    wo = wo_all.reshape(256, width)
    wgu = wgu_all.reshape(width, 768)
    wd = wd_all.reshape(384, width)
    wg, wu = wgu[:, :384], wgu[:, 384:]

    logical, where_at = token_places(block_table, segment_ids[:, 0])
    seg = segment_ids[:, 0]
    visible = (logical[:, None, :] <= logical[:, :, None]) & (
        (seg[:, None, :] == 0) | (seg[:, None, :] == seg[:, :, None])
    )
    cos, sin = rope_tables(where_at)

    x = x_all.reshape(mbs, 1024, width).astype(F32)
    normed_in = rms_gain(x, g_attn_gain).astype(BF).reshape(2048, width)
    raw = forward_dot(normed_in, wqkv).reshape(mbs, 1024, 4, HEAD)
    q_full, back_q = jax.vjp(lambda r, g: prepare_heads(r, g, cos, sin), raw[:, :, :2], g_query_gain)
    k_full, back_k = jax.vjp(lambda r, g: prepare_heads(r, g, cos, sin), raw[:, :, 2:3], g_key_gain)
    q = q_full.astype(BF)
    k = k_full.astype(BF)[:, :, 0]
    v = raw[:, :, 3].astype(BF)
    scale = HEAD ** (-0.5)
    scores = jnp.einsum("mqhd,mpd->mhqp", q, k, preferred_element_type=F32) * scale
    scores = jnp.where(visible[:, None], scores, -1e30)
    peak = jnp.max(scores, axis=-1, keepdims=True)
    shifted = jnp.exp(scores - peak)
    row_total = jnp.sum(shifted, axis=-1, keepdims=True)
    probs = shifted / row_total
    probs_low = probs.astype(BF)
    mixed = jnp.einsum("mhqp,mpd->mqhd", probs_low, v, preferred_element_type=F32)
    mixed = mixed.astype(BF).reshape(2048, 256)
    att_part = forward_dot(mixed, wo).astype(BF).reshape(2, 8, 128, width)

    def reduce_ctx_body(net, part, total, *bufs):
        return [reduce_ctx(net, part, total, *bufs)]

    (att_sum,) = comm_call(
        reduce_ctx_body,
        RING_Z,
        [((2, 128, width), F32)],
        reduce_ctx_scratch(width),
        1,
        [True],
        [True],
        32,
    )(att_part)
    attended = tok.reshape(256, width).astype(F32) + att_sum.reshape(256, width)
    r2 = lax.rsqrt(jnp.mean(attended * attended, axis=-1, keepdims=True) + 1e-06)
    normed_mid = (attended * r2 * g_ffn_gain).astype(BF)

    def gather_tp_body(net, src, out):
        return [gather_tp(net, src, out)]

    (mid_all,) = comm_call(
        gather_tp_body, RING_X, [((8, 256, width), BF)], [], 2, [False], [False], 16
    )(normed_mid)
    nm = mid_all.reshape(2048, width)
    ct = cot_all.reshape(2048, width)
    gate_up = forward_dot(nm, wgu)
    gate, up = gate_up[:, :384], gate_up[:, 384:]
    sig = jax.nn.sigmoid(gate)
    silu = gate * sig
    hidden = (silu * up).astype(BF)
    out_part = forward_dot(hidden, wd).astype(BF).reshape(8, 256, width)
    g_hidden = against_cols(ct, wd)
    g_gate = (g_hidden * up * sig * (1.0 + gate * (1.0 - sig))).astype(BF)
    g_up = (g_hidden * silu).astype(BF)
    g_gu = jnp.concatenate([g_gate, g_up], axis=1)
    grad_down_part = across_rows(hidden, ct).astype(BF)
    grad_gu_part = across_rows(nm, g_gu).astype(BF)
    mid_part = against_cols(g_gu, wgu).astype(BF).reshape(8, 256, width)

    def reduce_tp_body(net, a, b, ta, tb, *bufs):
        return [reduce_tp(net, a, ta, *bufs[:4]), reduce_tp(net, b, tb, *bufs[4:])]

    g_mid, out_sum = comm_call(
        reduce_tp_body,
        RING_X,
        [((256, width), F32), ((256, width), F32)],
        reduce_tp_scratch(width) * 2,
        3,
        [True, True],
        [True, True],
        32,
    )(mid_part, out_part)
    output = (attended + out_sum).astype(BF)
    n2 = g_mid * g_ffn_gain
    grad_ffn_gain = jnp.sum(g_mid * attended * r2, axis=0)
    g_attended = (
        cot.astype(F32)
        + r2 * n2
        - attended * (r2 * r2 * r2) * jnp.mean(n2 * attended, axis=-1, keepdims=True)
    )
    g_attn = g_attended.astype(BF)

    def gather_ctx_body(net, src, out):
        return [gather_ctx(net, src, out)]

    (g_attn_all,) = comm_call(
        gather_ctx_body, RING_Z, [((2, 8, 128, width), BF)], [], 4, [False], [False], 32
    )(g_attn.reshape(2, 128, width))
    ga = g_attn_all.reshape(2048, width)
    g_mixed = against_cols(ga, wo).astype(BF).reshape(2, 1024, 2, HEAD)
    grad_out_part = across_rows(mixed, ga).astype(BF)
    g_probs = jnp.einsum("mqhd,mpd->mhqp", g_mixed, v, preferred_element_type=F32)
    inner = jnp.sum(probs * g_probs, axis=-1, keepdims=True)
    g_scores = (probs * (g_probs - inner)).astype(BF)
    g_q = jnp.einsum("mhqp,mpd->mqhd", g_scores, k, preferred_element_type=F32) * scale
    g_k = jnp.einsum("mhqp,mqhd->mpd", g_scores, q, preferred_element_type=F32) * scale
    g_v = jnp.einsum("mhqp,mqhd->mpd", probs_low, g_mixed, preferred_element_type=F32)
    g_q_raw, grad_query_gain = back_q(g_q)
    g_k_raw, grad_key_gain = back_k(g_k[:, :, None])
    g_raw = (
        jnp.concatenate([g_q_raw, g_k_raw, g_v[:, :, None]], axis=2).astype(BF).reshape(2048, 512)
    )
    grad_qkv_part = across_rows(normed_in, g_raw).astype(BF)
    in_part = against_cols(g_raw, wqkv).astype(BF).reshape(2, 8, 128, width)
    (in_sum,) = comm_call(
        reduce_ctx_body,
        RING_Z,
        [((2, 128, width), F32)],
        reduce_ctx_scratch(width),
        5,
        [True],
        [True],
        32,
    )(in_part)
    g_in = in_sum.reshape(256, width)
    x_own = tok.reshape(256, width).astype(F32)
    r1 = lax.rsqrt(jnp.mean(x_own * x_own, axis=-1, keepdims=True) + 1e-06)
    n1 = g_in * g_attn_gain
    grad_attn_gain = jnp.sum(g_in * x_own * r1, axis=0)
    grad_tokens = (
        g_attended
        + r1 * n1
        - x_own * (r1 * r1 * r1) * jnp.mean(n1 * x_own, axis=-1, keepdims=True)
    )

    small_terms = jnp.concatenate(
        [
            grad_attn_gain.reshape(16, 64),
            grad_ffn_gain.reshape(16, 64),
            grad_query_gain.reshape(16, 8),
            grad_key_gain.reshape(16, 8),
            jnp.zeros((16, 512 - 144), F32),
        ],
        axis=1,
    ).astype(BF)
    qkv_terms = jnp.concatenate(
        [grad_qkv_part.reshape(16, 64, 512), jnp.broadcast_to(small_terms[:, None], (16, 16, 512))],
        axis=1,
    )
    wo_terms = grad_out_part.reshape(2, 8, 16, width).transpose(1, 0, 2, 3).reshape(16, 16, width)

    def terms_body(net, a, b, g, d, oa, ob, og, od):
        return [
            scatter_plane(net, a, oa),
            scatter_plane(net, b, ob),
            scatter_copies(net, g, d, og, od),
        ]

    ta, tb, tg, td = comm_call(
        terms_body,
        PLANE_SHIFTS + COPY_SHIFTS,
        [
            ((16, 80, 512), BF),
            ((16, 16, width), BF),
            ((16, 64, 768), BF),
            ((16, 192, 128), BF),
        ],
        [],
        6,
        [False] * 4,
        [False] * 4,
        60,
        4,
    )(qkv_terms, wo_terms, grad_gu_part.reshape(16, 64, 768), grad_down_part.reshape(2, 192, width))

    def summed(t):
        return jnp.sum(t.astype(F32), axis=0).astype(BF)

    def spread_body(net, a, b, g, d, oa, ob, og, od, mb_, mg):
        return [
            spread_ctx(net, b, mb_, lambda: exchange_chips(net, mb_, ob)),
            spread_ctx(net, g, mg, lambda: exchange_tp(net, mg, og)),
            spread_ctx(net, a, oa),
            spread_ctx(net, d, od),
        ]

    sa_, sb_, sg_, sd_, _, _ = comm_call(
        spread_body,
        CTX_SHIFTS + PLANE_SHIFTS,
        [
            ((8, 80, 512), BF),
            ((8, 16, width), BF),
            ((8, 64, 768), BF),
            ((8, 192, 128), BF),
            ((8, 16, width), BF),
            ((8, 64, 768), BF),
        ],
        [],
        7,
        [False] * 4,
        [False] * 6,
        48,
        6,
    )(summed(ta), summed(tb), summed(tg), summed(td))

    qkv_grad = sa_[:, :64].astype(F32)
    grad_w_query = qkv_grad[:, :, :256].transpose(1, 0, 2).reshape(64, 2048)
    grad_w_key = qkv_grad[:, :, 256:384].transpose(1, 0, 2).reshape(64, 1024)
    grad_w_value = qkv_grad[:, :, 384:].transpose(1, 0, 2).reshape(64, 1024)
    gains = jnp.sum(sa_[:, 64].astype(F32), axis=0)
    grad_w_out = sb_.astype(F32).reshape(128, width)

    def from_tp(g):
        return g.reshape(8, 64, 2, 192).transpose(1, 2, 0, 3).reshape(64, 3072)

    gu_grad = sg_.astype(F32)
    grad_w_gate = from_tp(gu_grad[:, :, :384])
    grad_w_up = from_tp(gu_grad[:, :, 384:])
    grad_w_down = sd_.astype(F32).transpose(1, 0, 2).reshape(192, width)
    return (
        output.reshape(2, 1, 128, width),
        grad_tokens.reshape(2, 1, 128, width),
        gains[:64],
        grad_w_query,
        grad_w_key,
        grad_w_value,
        gains[128:136],
        gains[136:144],
        grad_w_out,
        gains[64:128],
        grad_w_gate,
        grad_w_up,
        grad_w_down,
    )


def solution(mesh):
    placed = (
        P(None, "fsdp", "ctx", None),
        P(None, "fsdp", "ctx", None),
        P(),
        P(None, "fsdp", None),
        P(None, "fsdp", "ctx"),
        P("fsdp"),
        P("fsdp", None),
        P("fsdp", None),
        P("fsdp", None),
        P("fsdp"),
        P("fsdp"),
        P("fsdp", None),
        P("fsdp"),
        P("fsdp", None),
        P("fsdp", None),
        P("fsdp", None),
    )
    return jax.shard_map(
        per_device,
        mesh=mesh,
        in_specs=placed,
        out_specs=(
            P(None, "fsdp", "ctx", None),
            P(None, "fsdp", "ctx", None),
            P("fsdp"),
            P("fsdp", None),
            P("fsdp", None),
            P("fsdp", None),
            P("fsdp"),
            P("fsdp"),
            P("fsdp", None),
            P("fsdp"),
            P("fsdp", None),
            P("fsdp", None),
            P("fsdp", None),
        ),
        check_vma=False,
    )
```

time: 1790 us -> 554 us (0.31)
  waiting for transfers between devices: 1350 us -> 0 us
  Pallas kernels: 0 us -> 351 us
  blocking collectives: 113 us -> 0 us
  matrix products: 181 us -> 98.3 us
  local copies, waits for them, and re-layouts: 60.6 us -> 38.2 us
    reduce_scatter x7 -> x0, waiting for transfers between devices: 671 us -> none  [the longest x1 124 us: per_device(): lax.psum_scatter(totals[8], 'fsdp', scatter_dimension=0, tiled=True)]
    all_gather x11 -> x0, waiting for transfers between devices: 501 us -> none  [the longest x2 91 us: micro_batch(): lax.all_gather(values_low, 'ctx', axis=0, tiled=True)]
    pallas_call x0 -> x8, Pallas kernels: none -> 351 us  [the longest x1 76.3 us: per_device(): comm_call(first_body, RING_Z + RING_X + PLANE_SHIFTS, [((2, 8, 128, width...]
    unnamed x27 -> x0, waiting for transfers between devices: 164 us -> none
    unnamed x2 -> x0, blocking collectives: 96.2 us -> none
    dot_general x54 -> x17, matrix products: 181 us -> 86.8 us  [the longest x4 19.2 us: forward_dot(): return jnp.dot(a, b, preferred_element_type=F32)]
    unnamed x277 -> x81, local copies, waits for them, and re-layouts: 47.7 us -> 7.1 us
  transfers between devices with their start and end apart: 23 -> 0, of which waited for: 23 -> 0; matrix products, arithmetic and copies ran while one was open for 12% -> 0% of each run, Pallas kernels for 0% -> 0%
where the time goes in v1:
time: 554 us; the launch traced here: 550 us
  Pallas kernels  351 us (63%)
  matrix products  98.3 us (18%)
  other arithmetic  60.1 us (11%)
  local copies, waits for them, and re-layouts  38.2 us (7%)
    pallas_call x1, Pallas kernels, per_device(): comm_call(first_body, RING_Z + RING_X + PLANE_SHIFTS, [((2, 8, 128, width...  76.3 us
    pallas_call x2, Pallas kernels, per_device(): comm_call(reduce_ctx_body, RING_Z, [((2, 128, width), F32)], reduce_ctx_s...  67.2 us
    pallas_call x1, Pallas kernels, per_device(): comm_call(terms_body, PLANE_SHIFTS + COPY_SHIFTS, [((16, 80, 512), BF), (...  62.2 us
    pallas_call x1, Pallas kernels, per_device(): comm_call(spread_body, CTX_SHIFTS + PLANE_SHIFTS, [((8, 80, 512), BF), ((...  46.9 us
    pallas_call x1, Pallas kernels, per_device(): comm_call(reduce_tp_body, RING_X, [((256, width), F32), ((256, width), F3...  43.7 us
    pallas_call x1, Pallas kernels, per_device(): comm_call(gather_ctx_body, RING_Z, [((2, 8, 128, width), BF)], [], 4, [Fa...  30.2 us
    pallas_call x1, Pallas kernels, per_device(): comm_call(gather_tp_body, RING_X, [((8, 256, width), BF)], [], 2, [False]...  24.9 us
    dot_general x4, matrix products, forward_dot(): return jnp.dot(a, b, preferred_element_type=F32)  19.2 us

profile of v1, /device:TPU:1, one launch (start us, length us, event | category | flops | bytes accessed | tf_op | source)
XLA Modules:
  0.0 549.8 jit_solution(8992854713660037178)
XLA Ops:
  4.0 2.8 concatenate.70
  10.6 1.6 reshape.556
  15.1 2.9 fusion.81
  18.0 3.6 or_and_fusion
  21.6 1.9 broadcast_multiply_fusion.1
  23.5 76.3 %shard_map.246 = (bf16[2,8,128,1024]{3,2,1,0:T(8,128)(2,1)}, bf16[8,256,1024]{2,1,0:T(8,128)(2,1)}, bf16[16,80,512]{2,1,0:T(8,128)(2,1)}, bf16[8,16,1024]{2,1,0:...) custom-call(bf16[2,128,1024]{2,1,0:T(8,128)(2,1)S(1)} %bitcast.284, ...), custom_call_target="tpu_custom_call" | custom-call | tf_op jit(solution)/shard_map/pallas_call | solution.py:604
  99.8 3.4 fusion.5
  104.5 4.2 fusion.7
  109.0 2.3 copy.50
  111.2 4.9 fusion.107
  120.8 1.8 fusion.21
  122.6 11.5 %fusion.102 = (f32[2,2,1024]{2,1,0:T(2,128)S(1)}, f32[2,2,1024,1024]{2,3,1,0:T(8,128)}) fusion(pred[2,1024,1024]{1,2,0:T(8,128)(4,1)} %or_and_fusion, bf16[2,1024,2,128]{1,3,2,0:T(8,128)(2,1)} %fusion.21, bf16[2,1024,1,128]{1,3,2,0:T(8,128)(2,1)S(1)} %fusion.58), kind=kOutput, calls=%fused_computation.189 | convolution fusion | flops 1090520064 | bytes 20463616 | tf_op jit(solution)/shard_map/sub | solution.py:654
  134.1 8.4 %fusion.36 = bf16[2,1024,2,128]{1,3,2,0:T(8,128)(2,1)} fusion(f32[2,1024,4,128]{1,3,2,0:T(8,128)} %copy-done.9, f32[2,2,1024,1024]{2,3,1,0:T(8,128)} %get-tuple-element.119, f32[2,2,1024]{2,1,0:T(2,128)S(1)} %get-tuple-element.118), kind=kOutput, calls=%fused_computation.63 | convolution fusion | flops 1082654720 | bytes 18366464 | tf_op jit(solution)/shard_map/mhqp,mpd->mqhd/dot_general | solution.py:658
  142.5 3.7 copy.55
  146.2 4.4 convolution_convert_fusion.2
  150.6 34.4 %shard_map.247 = f32[2,128,1024]{2,1,0:T(8,128)S(1)} custom-call(bf16[2,8,128,1024]{3,2,1,0:T(8,128)(2,1)} %bitcast.294), custom_call_target="tpu_custom_call" | custom-call | tf_op jit(solution)/shard_map/pallas_call | solution.py:665
  185.5 24.9 %shard_map.248 = bf16[8,256,1024]{2,1,0:T(8,128)(2,1)} custom-call(bf16[256,1024]{1,0:T(8,128)(2,1)S(1)} %multiply_convert_fusion.3.refs_0_), custom_call_target="tpu_custom_call" | custom-call | tf_op jit(solution)/shard_map/pallas_call | solution.py:682
  210.4 5.5 %fusion.108 = f32[2048,768]{0,1:T(8,128)S(1)} fusion(bf16[2048,1024]{1,0:T(8,128)(2,1)} %bitcast.298, bf16[1024,768]{1,0:T(8,128)(2,1)S(1)} %bitcast.329), kind=kOutput, calls=%fused_computation.191 | convolution fusion | flops 3221225472 | bytes 12058624 | tf_op jit(solution)/shard_map/dot_general | solution.py:533
  215.9 3.6 multiply_convert_fusion.2
  219.5 1.8 convolution_convert_fusion.5
  221.7 4.8 fusion.29
  226.5 5.2 convolution_convert_fusion.3
  231.6 4.3 convolution_convert_fusion
  236.0 43.7 %shard_map.249 = (f32[256,1024]{1,0:T(8,128)S(1)}, f32[256,1024]{1,0:T(8,128)S(1)}) custom-call(bf16[8,256,1024]{2,1,0:T(8,128)(2,1)} %bitcast.306, bf16[8,256,1024]{2,1,0:T(8,128)(2,1)} %bitcast.307), custom_call_target="tpu_custom_call" | custom-call | tf_op jit(solution)/shard_map/pallas_call | solution.py:704
  280.0 1.6 fusion.94
  281.7 30.2 %shard_map.250 = bf16[2,8,128,1024]{3,2,1,0:T(8,128)(2,1)} custom-call(bf16[2,128,1024]{2,1,0:T(8,128)(2,1)S(1)} %bitcast.286), custom_call_target="tpu_custom_call" | custom-call | tf_op jit(solution)/shard_map/pallas_call | solution.py:727
  311.8 4.7 convolution_convert_fusion.6
  316.6 2.3 convolution_convert_fusion.4
  318.9 1.5 reshape.574
  321.5 9.5 %fusion.46 = bf16[2,1024,1,128]{1,3,2,0:T(8,128)(2,1)} fusion(bf16[2,1024,2,128]{3,2,1,0:T(2,128)(2,1)S(1)} %reshape.574, f32[2,2,1024,1024]{2,3,1,0:T(8,128)} %get-tuple-element.119, f32[2,2,1024]{2,1,0:T(2,128)S(1)} %get-tuple-element.118), kind=kOutput, calls=%fused_computation.70 | convolution fusion | flops 1082392576 | bytes 18366464 | tf_op jit(solution)/shard_map/mhqp,mqhd->mpd/dot_general | solution.py:738
  330.9 11.0 %fusion.1 = (f32[2,2,1024]{2,1,0:T(2,128)S(1)}, f32[2,1024,1024,2]{2,1,3,0:T(8,128)}) fusion(f32[2,2,1024,1024]{2,3,1,0:T(8,128)} %get-tuple-element.119, f32[2,2,1024]{2,1,0:T(2,128)S(1)} %get-tuple-element.118, bf16[2,1024,2,128]{3,2,1,0:T(2,128)(2,1)S(1)} %reshape.574, f32[2,1024,4,128]{1,3,2,0:T(8,128)} %copy-done.9), kind=kOutput, calls=%fused_computation.3 | convolution fusion | flops 1086320640 | bytes 35160064 | tf_op jit(solution)/shard_map/mqhd,mpd->mhqp/dot_general | solution.py:733
  342.0 12.1 %fusion.3 = bf16[2,2,1024,1024]{2,3,1,0:T(8,128)(2,1)S(1)} fusion(f32[2,1024,1024,2]{2,1,3,0:T(8,128)} %get-tuple-element.121, f32[2,2,1024]{2,1,0:T(2,128)S(1)} %get-tuple-element.120, f32[2,2,1024,1024]{2,3,1,0:T(8,128)} %get-tuple-element.119, f32[2,2,1024]{2,1,0:T(2,128)S(1)} %get-tuple-element.118), kind=kLoop, calls=%fused_computation.5 | loop fusion | flops 16777216 | bytes 41975808 | tf_op jit(solution)/shard_map/convert_element_type | solution.py:735
  354.1 2.9 fusion.42
  358.2 1.4 bitcast_multiply_fusion.1
  359.7 2.0 copy-done.10
  363.0 1.6 fusion.16
  364.7 1.3 fusion.96
  366.0 2.1 multiply_reduce_fusion.3
  368.2 1.5 fusion.54
  369.7 1.6 pad_maximum_fusion.1
  371.3 4.4 copy.64
  375.8 6.3 %fusion.33 = bf16[1024,512]{1,0:T(8,128)(2,1)} fusion(bf16[2048,1024]{1,0:T(8,128)(2,1)} %bitcast.305, bf16[256,8,4,128]{3,2,1,0:T(4,128)(2,1)} %bitcast.312), kind=kOutput, calls=%fused_computation.61 | convolution fusion | flops 2148007936 | bytes 7340032 | tf_op jit(solution)/shard_map/dot_general | solution.py:525
  382.2 5.9 %convolution_convert_fusion.1 = bf16[2048,1024]{1,0:T(8,128)(2,1)} fusion(bf16[1024,512]{1,0:T(8,128)(2,1)S(1)} %bitcast.309, bf16[256,8,4,128]{3,2,1,0:T(4,128)(2,1)} %bitcast.313), kind=kOutput, calls=%fused_computation.24 | convolution fusion | flops 2149580800 | bytes 7340032 | tf_op jit(solution)/shard_map/dot_general | solution.py:529
  388.1 32.8 %shard_map.251 = f32[2,128,1024]{2,1,0:T(8,128)S(1)} custom-call(bf16[2,8,128,1024]{3,2,1,0:T(8,128)(2,1)} %bitcast.297), custom_call_target="tpu_custom_call" | custom-call | tf_op jit(solution)/shard_map/pallas_call | solution.py:746
  422.8 2.4 pad_maximum_fusion.6.refs_0_
  425.2 62.2 %shard_map.252 = (bf16[16,80,512]{2,1,0:T(8,128)(2,1)S(1)}, bf16[16,16,1024]{2,1,0:T(8,128)(2,1)S(1)}, bf16[16,64,768]{2,1,0:T(8,128)(2,1)}, bf16[16,192,128]{2,1,0:T(8,128)(2,1)S(1)}) custom-call(bf16[16,80,512]{2,1,0:T(8,128)(2,1)} %pad_maximum_fusion.6.refs_0_, bf16[16,16,1024]{2,1,0:T(8,128)(2,1)S(1)} %bitcast.287, bf16[16,64,768]{2,1,0:T(8,128)(2,1)} %bitcast.314, ...), custom_call_target="tpu_custom_call" | custom-call | tf_op jit(solution)/shard_map/pallas_call | solution.py:790
  489.9 1.6 reduce_sum.235.refs_2_
  491.5 46.9 %shard_map.253 = (bf16[8,80,512]{2,1,0:T(8,128)(2,1)S(1)}, bf16[8,16,1024]{2,1,0:T(8,128)(2,1)S(1)}, bf16[8,64,768]{2,1,0:T(8,128)(2,1)S(1)}, bf16[8,192,128]{2,...) custom-call(bf16[80,512]{1,0:T(8,128)(2,1)S(1)} %reduce_sum.233.refs_0_, ...), custom_call_target="tpu_custom_call" | custom-call | tf_op jit(solution)/shard_map/pallas_call | solution.py:818
  (162 shorter events, 36.5 us)
Async XLA Ops:
  0.6 9.1 %copy-start = (bf16[64,2048]{1,0:T(8,128)(2,1)S(1)}, bf16[64,2048]{1,0:T(8,128)(2,1)}, u32[]{:S(2)}) copy-start(bf16[64,2048]{1,0:T(8,128)(2,1)} %param.21) | copy-start | bytes 786436
  0.7 12.2 %copy-start.28 = (bf16[64,3072]{1,0:T(8,128)(2,1)S(1)}, bf16[64,3072]{1,0:T(8,128)(2,1)}, u32[]{:S(2)}) copy-start(bf16[64,3072]{1,0:T(8,128)(2,1)} %param.29) | copy-start | bytes 1179652
  18.0 5.5 %copy-start.12 = (f32[2,1024,64]{1,2,0:T(8,128)}, f32[2,1024,64]{1,2,0:T(8,128)S(1)}, u32[]{:S(2)}) copy-start(f32[2,1024,64]{1,2,0:T(8,128)S(1)} %get-tuple-element.110) | copy-start | bytes 1572868
  18.0 99.5 %copy-start.11 = (f32[2,1024,64]{1,2,0:T(8,128)}, f32[2,1024,64]{1,2,0:T(8,128)S(1)}, u32[]{:S(2)}) copy-start(f32[2,1024,64]{1,2,0:T(8,128)S(1)} %get-tuple-element.111) | copy-start | bytes 1572868
  18.0 5.5 %copy-start.2 = (bf16[2,1,128,1024]{3,2,1,0:T(8,128)(2,1)S(1)}, bf16[2,1,128,1024]{3,2,1,0:T(8,128)(2,1)}, u32[]{:S(2)}) copy-start(bf16[2,1,128,1024]{3,2,1,0:T(8,128)(2,1)} %param.16) | copy-start | bytes 1572868
  18.0 5.5 %copy-start.3 = (bf16[2,1,128,1024]{3,2,1,0:T(8,128)(2,1)S(1)}, bf16[2,1,128,1024]{3,2,1,0:T(8,128)(2,1)}, u32[]{:S(2)}) copy-start(bf16[2,1,128,1024]{3,2,1,0:T(8,128)(2,1)} %param.17) | copy-start | bytes 1572868
  18.0 5.5 %copy-start.5 = (bf16[192,1024]{1,0:T(8,128)(2,1)S(1)}, bf16[192,1024]{1,0:T(8,128)(2,1)}, u32[]{:S(2)}) copy-start(bf16[192,1024]{1,0:T(8,128)(2,1)} %refs_5_.1) | copy-start | bytes 1179652
  18.0 5.5 %copy-start.6 = (bf16[128,1024]{1,0:T(8,128)(2,1)S(1)}, bf16[128,1024]{1,0:T(8,128)(2,1)}, u32[]{:S(2)}) copy-start(bf16[128,1024]{1,0:T(8,128)(2,1)} %param.26) | copy-start | bytes 786436
  99.8 116.1 %copy-start.7 = (bf16[2,192,1024]{2,1,0:T(8,128)(2,1)}, bf16[2,192,1024]{2,1,0:T(8,128)(2,1)S(1)}, u32[]{:S(2)}) copy-start(bf16[2,192,1024]{2,1,0:T(8,128)(2,1)S(1)} %get-tuple-element.33) | copy-start | bytes 2359300
  99.8 3.4 copy-start.26
  104.5 4.2 copy-start.31
  116.1 3.3 copy-start.9
  116.2 0.7 copy-start.29
  116.9 1.4 copy-start.25
  118.8 3.8 copy-start.23
  119.2 1.2 copy-start.21
  119.2 1.5 copy-start.22
  185.3 25.1 %copy-start.37 = (bf16[16,64,768]{2,1,0:T(8,128)(2,1)S(1)}, bf16[16,64,768]{2,1,0:T(8,128)(2,1)}, u32[]{:S(2)}) copy-start(bf16[16,64,768]{2,1,0:T(8,128)(2,1)} %get-tuple-element.34) | copy-start | bytes 4718596
  210.3 5.6 %copy-start.36 = (bf16[8,256,1024]{2,1,0:T(8,128)(2,1)S(1)}, bf16[8,256,1024]{2,1,0:T(8,128)(2,1)}, u32[]{:S(2)}) copy-start(bf16[8,256,1024]{2,1,0:T(8,128)(2,1)} %get-tuple-element.32) | copy-start | bytes 12582916
  219.5 2.2 copy-start.14
  226.5 5.2 copy-start.8
  311.8 4.7 copy-start.15
  341.9 12.1 %copy-start.19 = (bf16[2,1024,2,128]{1,3,2,0:T(8,128)(2,1)S(1)}, bf16[2,1024,2,128]{1,3,2,0:T(8,128)(2,1)}, u32[]{:S(2)}) copy-start(bf16[2,1024,2,128]{1,3,2,0:T(8,128)(2,1)} %fusion.21) | copy-start | bytes 3145732
  354.1 2.9 copy-start.13
  357.0 1.2 copy-start.24
  358.1 1.5 copy-start.17
  359.5 2.2 copy-start.10
  364.7 3.5 copy-start.30
  366.0 3.7 copy-start.20
  366.0 3.7 copy-start.27
  375.8 6.4 %copy-start.16 = (bf16[16,64,512]{2,1,0:T(8,128)(2,1)S(1)}, bf16[16,64,512]{2,1,0:T(8,128)(2,1)}, u32[]{:S(2)}) copy-start(bf16[16,64,512]{2,1,0:T(8,128)(2,1)} %slice.81) | copy-start | bytes 3145732
  388.1 32.8 %copy-start.32 = (f32[1024]{0:T(1024)S(1)}, f32[1024]{0:T(1024)}, u32[]{:S(2)}) copy-start(f32[1024]{0:T(1024)} %copy-done.31) | copy-start | bytes 12292
  388.1 32.8 %copy-start.34 = (f32[2,128]{1,0:T(2,128)S(1)}, f32[2,128]{1,0:T(2,128)}, u32[]{:S(2)}) copy-start(f32[2,128]{1,0:T(2,128)} %get-tuple-element.117) | copy-start | bytes 3076
  388.1 33.2 %copy-start.18 = (f32[256,1024]{1,0:T(8,128)S(1)}, f32[256,1024]{1,0:T(8,128)}, u32[]{:S(2)}) copy-start(f32[256,1024]{1,0:T(8,128)} %get-tuple-element.82) | copy-start | bytes 3145732
  388.1 33.2 %copy-start.33 = (f32[256]{0:T(256)S(1)}, f32[256]{0:T(256)}, u32[]{:S(2)}) copy-start(f32[256]{0:T(256)} %get-tuple-element.116) | copy-start | bytes 3076
  388.1 33.2 %copy-start.35 = (f32[256]{0:T(256)S(1)}, f32[256]{0:T(256)}, u32[]{:S(2)}) copy-start(f32[256]{0:T(256)} %multiply_multiply_fusion.4) | copy-start | bytes 3076
  487.4 0.9 copy-start.4
  545.5 3.9 copy-start.1

commit v2 on v1

v2 whole, which is shorter than its diff:
```python
import functools
import math

import jax
import jax.numpy as jnp
from jax import lax
from jax.experimental import pallas as pl
from jax.experimental.pallas import tpu as pltpu
from jax.sharding import PartitionSpec as P

MESH = pl.DeviceIdType.MESH
SIZES = {"z": 4, "yl": 2, "yh": 2, "x": 4, "core": 2}
BF = jnp.bfloat16
F32 = jnp.float32
HEAD = 128


def my_place():
    c = lax.axis_index("ctx")
    f = lax.axis_index("fsdp")
    return {"z": c // 2, "yl": c % 2, "yh": f // 8, "x": (f // 2) % 4, "core": f % 2}


def moved(me, shift):
    to = dict(me)
    for axis, step in shift.items():
        to[axis] = (me[axis] + (step % SIZES[axis])) % SIZES[axis]
    return to


def ctx_of(place):
    return place["z"] * 2 + place["yl"]


def tp_of(place):
    return place["x"] * 2 + place["core"]


def chip_of(place):
    return place["yh"] * 4 + place["x"]


def head_of(place):
    return place["z"] * 2 + place["core"]


def fsdp_of(place):
    return chip_of(place) * 2 + place["core"]


def device_of(place):
    return (ctx_of(place), fsdp_of(place))


CTX_SHIFTS = [{"z": a, "yl": b} for a in range(4) for b in range(2) if a or b]
PLANE_SHIFTS = [
    {"yh": a, "x": b, "core": d}
    for a in range(2)
    for b in range(4)
    for d in range(2)
    if a or b or d
]
CHIP_SHIFTS = [{"yh": a, "x": b} for a in range(2) for b in range(4) if a or b]
TP_SHIFTS = [{"x": b, "core": d} for b in range(4) for d in range(2) if b or d]
COPY_SHIFTS = [
    {"z": a, "yl": b, "yh": d}
    for a in range(4)
    for b in range(2)
    for d in range(2)
    if a or b or d
]
WEIGHT_PLANE = [
    {"yh": a, "yl": a, "x": b, "core": d}
    for a in range(2)
    for b in range(4)
    for d in range(2)
    if a or b or d
]
WEIGHT_CHIPS = [{"yh": a, "yl": a, "x": b} for a in range(2) for b in range(4) if a or b]
SAMPLE_SHIFTS = [
    {"yh": a, "yl": b, "x": d}
    for a in range(2)
    for b in range(2)
    for d in range(4)
    if a or b or d
]
HEAD_SHIFTS = [{"z": a, "core": b} for a in range(4) for b in range(2) if a or b]
RING_Z = [{"z": 1}, {"z": 3}, {"core": 1}, {"yl": 1, "core": 1}]
RING_X = [{"x": 1}, {"x": 3}, {"core": 1}]


def back(shift):
    return {axis: -step for axis, step in shift.items()}


class Net:
    def __init__(self, send_sems, recv_sems, local_sems, pair_sems):
        self.me = my_place()
        self.send_sems, self.recv_sems, self.local_sems = send_sems, recv_sems, local_sems
        self.pair_sems = pair_sems
        self.count = 0
        self.locals = 0
        self.pending = []

    def enter(self, shifts):
        barrier = pltpu.get_barrier_semaphore()
        for shift in shifts:
            pl.semaphore_signal(
                barrier, inc=1, device_id=device_of(moved(self.me, shift)), device_id_type=MESH
            )
        pl.semaphore_wait(barrier, len(shifts))

    def send(self, src, dst, **shift):
        at = self.count
        self.count += 1
        copy = pltpu.make_async_remote_copy(
            src_ref=src,
            dst_ref=dst,
            send_sem=self.send_sems.at[at],
            recv_sem=self.recv_sems.at[at],
            device_id=device_of(moved(self.me, shift)),
            device_id_type=MESH,
        )
        copy.start()
        self.pending.append(copy.wait_send)
        return copy

    def pair(self, src, dst, place, recv, new=True):
        if new:
            self.count += 1
        return pltpu.make_async_remote_copy(
            src_ref=src,
            dst_ref=dst,
            send_sem=self.send_sems.at[self.count - 1],
            recv_sem=self.pair_sems.at[recv],
            device_id=device_of(place),
            device_id_type=MESH,
        )

    def spare(self):
        self.locals += 1
        return self.local_sems.at[self.locals - 1]

    def settle(self, copy):
        copy.wait()
        self.pending.remove(copy.wait)

    def local(self, src, dst):
        copy = pltpu.make_async_copy(src, dst, self.local_sems.at[self.locals])
        self.locals += 1
        copy.start()
        self.pending.append(copy.wait)
        return copy

    def swap(self, src, dst):
        return Swap(self, src, dst)

    def finish(self):
        for wait in self.pending:
            wait()


class Swap:
    def __init__(self, net, src, dst):
        me = net.me
        self.away = me["yl"] != me["core"]
        at = net.count
        net.count += 1
        self.remote = pltpu.make_async_remote_copy(
            src_ref=src,
            dst_ref=dst,
            send_sem=net.send_sems.at[at],
            recv_sem=net.recv_sems.at[at],
            device_id=device_of(moved(me, {"yl": 1, "core": 1})),
            device_id_type=MESH,
        )
        self.near = pltpu.make_async_copy(src, dst, net.spare())
        pl.when(self.away)(self.remote.start)
        pl.when(jnp.logical_not(self.away))(self.near.start)

    def wait(self):
        pl.when(self.away)(self.remote.wait)
        pl.when(jnp.logical_not(self.away))(self.near.wait)


def run_tasks(tasks):
    tasks = list(tasks)
    while tasks:
        left = []
        for task in tasks:
            try:
                next(task)
                left.append(task)
            except StopIteration:
                pass
        tasks = left


def unique(shifts):
    seen, out = set(), []
    for shift in shifts:
        key = tuple(sorted((k, v) for k, v in shift.items() if v))
        if key not in seen:
            seen.add(key)
            out.append(shift)
    return out


def comm_call(body, shifts, outs, scratch, cid, in_vmem, out_vmem, n_remote, n_local=1):
    shifts = unique(shifts)

    def kernel(*refs):
        refs, sems = refs[:-4], refs[-4:]
        net = Net(*sems)
        net.enter(shifts)
        drain(*(body(net, *refs) or ()))
        net.finish()

    vm = pl.BlockSpec(memory_space=pltpu.VMEM)
    hb = pl.BlockSpec(memory_space=pl.ANY)
    return pl.pallas_call(
        kernel,
        out_shape=[jax.ShapeDtypeStruct(s, d) for s, d in outs],
        in_specs=[vm if v else hb for v in in_vmem],
        out_specs=[vm if v else hb for v in out_vmem],
        scratch_shapes=list(scratch)
        + [
            pltpu.SemaphoreType.DMA((n_remote,)),
            pltpu.SemaphoreType.DMA((n_remote,)),
            pltpu.SemaphoreType.DMA((n_local,)),
            pltpu.SemaphoreType.DMA((2,)),
        ],
        compiler_params=pltpu.CompilerParams(
            collective_id=cid, has_side_effects=True, vmem_limit_bytes=60 << 20
        ),
    )


def drain(*tasks):
    run_tasks(tasks)


def step(task):
    next(task, None)


class Weave:
    def __init__(self):
        self.tasks = []

    def add(self, task):
        next(task)
        self.tasks.append(task)
        return task

    def tick(self, count=1):
        for _ in range(count):
            if self.tasks:
                self.step(self.tasks.pop(0))

    def step(self, task):
        try:
            next(task)
            self.tasks.append(task)
        except StopIteration:
            pass

    def finish(self, task):
        if task in self.tasks:
            self.tasks.remove(task)
            for _ in task:
                pass

    def finish_all(self):
        drain(*self.tasks)
        self.tasks = []


def gather_ring(net, axis, src, block, rows):
    me = net.me
    half = rows // 2
    low, high = (0, half), (half, half)

    def at(step, part=(0, rows)):
        return block(moved(me, {axis: step}), *part)

    def cut(part):
        return src.at[..., pl.ds(*part), :]

    def send(step, part, shift):
        here = cut(part) if step == 0 else at(step, part)
        return net.send(here, at(step, part), **shift)

    right, left, other = {axis: 1}, {axis: -1}, {"core": 1}
    r0 = send(0, low, right)
    l1 = send(0, high, left)
    r1 = send(0, high, right)
    l0 = send(0, low, left)
    own = send(0, (0, rows), other)
    yield
    r0.wait_recv()
    fr = send(-1, low, right)
    l1.wait_recv()
    fl = send(1, high, left)
    yield
    r1.wait_recv()
    cr = send(-1, (0, rows), other)
    l0.wait_recv()
    cl = send(1, (0, rows), other)
    yield
    fr.wait_recv()
    c2r = send(2, low, other)
    fl.wait_recv()
    c2l = send(2, high, other)
    yield
    for copy in (own, cr, cl, c2r, c2l):
        copy.wait_recv()


def add_rows(dst, terms, rows, step=32):
    def one(i, carry):
        at = pl.ds(pl.multiple_of(i * step, step), step)
        total = terms[0][at, :].astype(F32)
        for term in terms[1:]:
            total = total + term[at, :].astype(F32)
        dst[at, :] = total.astype(dst.dtype)
        return carry

    lax.fori_loop(0, rows // step, one, 0)


def reduce_ring(net, axis, part, index, total, rc, s, rh, r):
    me = net.me
    low, high = pl.ds(0, 64), pl.ds(64, 64)
    right, left, other = {axis: 1}, {axis: -1}, {"core": 1}

    def at(step, core, rows=pl.ds(0, 128)):
        return part.at[index(moved(me, {axis: step, "core": core})), rows]

    cc = {}
    for step in (2, 1, 3, 0):
        cc[step] = net.send(at(step, 1), rc.at[step], **other)
    yield
    cc[2].wait_recv()
    add_rows(s.at[2], [at(2, 0), rc.at[2]], 128)
    h_r = net.send(s.at[2, low], rh.at[0], **right)
    h_l = net.send(s.at[2, high], rh.at[1], **left)
    cc[1].wait_recv()
    add_rows(s.at[1, high], [at(1, 0, high), rc.at[1, high]], 64)
    r_high = net.send(s.at[1, high], r.at[0, high], **right)
    cc[3].wait_recv()
    add_rows(s.at[3, low], [at(3, 0, low), rc.at[3, low]], 64)
    l_low = net.send(s.at[3, low], r.at[1, low], **left)
    yield
    h_r.wait_recv()
    add_rows(s.at[1, low], [at(1, 0, low), rc.at[1, low], rh.at[0]], 64)
    r_low = net.send(s.at[1, low], r.at[0, low], **right)
    h_l.wait_recv()
    add_rows(s.at[3, high], [at(3, 0, high), rc.at[3, high], rh.at[1]], 64)
    l_high = net.send(s.at[3, high], r.at[1, high], **left)
    yield
    for copy in (cc[0], r_high, l_low, r_low, l_high):
        copy.wait_recv()
    add_rows(total, [at(0, 0), rc.at[0], r.at[0], r.at[1]], 128)


def reduce_ring_scratch(width):
    return [
        pltpu.VMEM((4, 128, width), BF),
        pltpu.VMEM((4, 128, width), BF),
        pltpu.VMEM((2, 64, width), BF),
        pltpu.VMEM((2, 128, width), BF),
    ]


def gather_heads_weights(net, wq, wk, wv, small, stage, out):
    me = net.me
    mine = fsdp_of(me)
    staged = []
    for core in range(2):
        h = me["z"] * 2 + core
        place = stage.at[core]
        for src, dst in (
            (wq.at[:, pl.ds(pl.multiple_of(h * 256, 256), 256)], place.at[pl.ds(0, 64), pl.ds(0, 256)]),
            (wk.at[:, pl.ds(pl.multiple_of(h * 128, 128), 128)], place.at[pl.ds(0, 64), pl.ds(256, 128)]),
            (wv.at[:, pl.ds(pl.multiple_of(h * 128, 128), 128)], place.at[pl.ds(0, 64), pl.ds(384, 128)]),
            (small, place.at[pl.ds(64, 16)]),
        ):
            staged.append(net.local(src, dst))
    yield
    for copy in staged:
        net.settle(copy)
    kept = net.local(stage.at[me["core"]], out.at[mine])
    copies = [
        net.send(stage.at[moved(me, shift)["core"]], out.at[mine], **shift)
        for shift in WEIGHT_PLANE
    ]
    yield
    for copy in copies:
        copy.wait_recv()
    net.settle(kept)


def gather_out_weights(net, src, mid, out):
    me = net.me
    mine = chip_of(me)
    stay = net.local(src.at[mine], mid.at[mine])
    first = [
        net.send(src.at[chip_of(moved(me, shift))], mid.at[mine], **shift) for shift in WEIGHT_CHIPS
    ]
    yield
    for copy in first:
        copy.wait_recv()
    net.settle(stay)
    place = out.at[me["core"], mine]
    kept = net.local(mid.at[head_of(me)], place)
    copies = [
        net.send(mid.at[head_of(moved(me, shift))], place, **shift) for shift in WEIGHT_PLANE
    ]
    yield
    for copy in copies:
        copy.wait_recv()
    net.settle(kept)


def gather_ff_weights(net, gate, up, down, gate_stage, up_stage, gate_out, up_out, down_out):
    me = net.me
    mine = fsdp_of(me)
    staged = []
    for j in range(8):
        at = pl.ds(j * 384, 384)
        staged.append(net.local(gate.at[:, at], gate_stage.at[j]))
        staged.append(net.local(up.at[:, at], up_stage.at[j]))
    chip = chip_of(me)
    near = dict(me, x=chip // 2, core=chip % 2)
    far = dict(near, yh=(me["yh"] + 1) % 2, yl=(me["yl"] + 1) % 2)
    half = me["core"]
    here = tp_of(me) == chip
    away = jnp.logical_not(here)
    one = net.pair(down, down_out.at[half], near, half)
    two = net.pair(down, down_out.at[half], far, half)
    stay = pltpu.make_async_copy(down, down_out.at[half], net.spare())
    yield
    for copy in staged:
        net.settle(copy)

    def pieces(place):
        j = tp_of(place)
        return [(gate_stage.at[j], gate_out.at[mine]), (up_stage.at[j], up_out.at[mine])]

    kept = [net.local(src, dst) for src, dst in pieces(me)]
    copies = [
        net.send(src, dst, **shift)
        for shift in WEIGHT_PLANE
        for src, dst in pieces(moved(me, shift))
    ]
    two.start()
    pl.when(here)(stay.start)
    pl.when(away)(one.start)
    yield
    for copy in copies:
        copy.wait_recv()
    for copy in kept:
        net.settle(copy)
    for h in (0, 1):
        arrived = net.pair(down, down_out.at[h], near, h, new=False)
        pl.when(jnp.logical_not(here & (half == h)))(arrived.wait_recv)
    two.wait_send()
    pl.when(here)(stay.wait)
    pl.when(away)(one.wait_send)


def chunk_of(place):
    return chip_of(place) * 2 + place["yl"]


def scatter_samples(net, pick, out):
    me = net.me
    mine = chunk_of(me)
    kept = net.local(pick(me), out.at[mine])
    copies = [net.send(pick(moved(me, shift)), out.at[mine], **shift) for shift in SAMPLE_SHIFTS]
    yield
    for copy in copies:
        copy.wait_recv()
    net.settle(kept)


def copy_index(place):
    return place["yh"] * 8 + ctx_of(place)


def scatter_copies(net, gate, up, down, gate_out, up_out, down_out):
    me = net.me

    def piece(place):
        return down.at[place["yh"], :, pl.ds(pl.multiple_of(ctx_of(place) * 128, 128), 128)]

    mine = copy_index(me)

    def pieces(place):
        at = copy_index(place)
        return [
            (gate.at[at], gate_out.at[mine]),
            (up.at[at], up_out.at[mine]),
            (piece(place), down_out.at[mine]),
        ]

    for src, dst in pieces(me):
        net.local(src, dst)
    copies = [
        net.send(src, dst, **shift) for shift in COPY_SHIFTS for src, dst in pieces(moved(me, shift))
    ]
    yield
    for copy in copies:
        copy.wait_recv()


def spread(net, src, out, shifts, index, after=None):
    me = net.me
    mine = out.at[index(me)]
    kept = net.local(src, mine)
    copies = [net.send(src, mine, **shift) for shift in shifts]
    yield
    for copy in copies:
        copy.wait_recv()
    net.settle(kept)
    if after is not None:
        yield
        yield from after()


def swap_task(net, src, out):
    swapped = net.swap(src, out)
    yield
    swapped.wait()


def exchange_chips(net, src, out, after):
    me = net.me
    mine = chip_of(me)
    kept = net.local(src.at[mine], out.at[mine])
    copies = [
        net.send(src.at[chip_of(moved(me, shift))], out.at[mine], **shift) for shift in CHIP_SHIFTS
    ]
    yield
    for copy in copies:
        copy.wait_recv()
    net.settle(kept)
    yield from after()


def exchange_tp(net, src, out):
    me = net.me
    mine = tp_of(me)
    place = out.at[:, pl.ds(pl.multiple_of(mine * 384, 128), 384)]
    net.local(src.at[mine], place)
    copies = [net.send(src.at[tp_of(moved(me, shift))], place, **shift) for shift in TP_SHIFTS]
    yield
    for copy in copies:
        copy.wait_recv()


def spread_down(net, src, mid, out):
    me = net.me
    j = tp_of(me)
    goal = dict(me, yh=j // 4, x=j % 4, core=me["yh"])
    stays = (j == chip_of(me)) & (me["yh"] == me["core"])
    sent = net.pair(src, mid, goal, 0)
    kept = pltpu.make_async_copy(src, mid, net.spare())

    @pl.when(stays)
    def _():
        kept.start()
        kept.wait()

    @pl.when(jnp.logical_not(stays))
    def _():
        sent.start()

    yield

    @pl.when(jnp.logical_not(stays))
    def _():
        sent.wait()

    place = out.at[:, pl.ds(pl.multiple_of(ctx_of(me) * 128, 128), 128)]
    net.local(mid, place)
    copies = [net.send(mid, place, **shift) for shift in CTX_SHIFTS]
    yield
    for copy in copies:
        copy.wait_recv()


def rope_tables(where_at):
    frequency = jnp.exp(
        jnp.arange(0, HEAD // 2, dtype=F32) * (-2.0 * math.log(1000000.0) / HEAD)
    )
    angles = where_at.astype(F32)[..., None] * frequency
    cos, sin = jnp.cos(angles), jnp.sin(angles)
    return jnp.concatenate([cos, cos], axis=-1), jnp.concatenate([-sin, sin], axis=-1)


def across_rows(a, b):
    return lax.dot_general(a, b, (((0,), (0,)), ((), ())), preferred_element_type=F32)


def against_cols(a, b):
    return lax.dot_general(a, b, (((1,), (1,)), ((), ())), preferred_element_type=F32)


def forward_dot(a, b):
    return jnp.dot(a, b, preferred_element_type=F32)


EXP2_SCALE = HEAD ** (-0.5) * math.log2(math.e)


def norm_scale(v):
    return lax.rsqrt(jnp.mean(v * v, axis=-1, keepdims=True) + 1e-06)


def visible_tile(lk, lk2, lq, sq):
    lk, lk2 = jnp.concatenate([lk, lk], axis=1), jnp.concatenate([lk2, lk2], axis=1)
    return (lk <= lq) & (lk2 >= sq)


def half_loop(body, part, parts, count):
    lax.fori_loop(part * count // parts, (part + 1) * count // parts, body, 0)


class Front:
    def __init__(self, m, gains, wqkv, wo, xs, tables, saved, part, mixed, vt):
        self.gains, self.wqkv, self.wo, self.xs = gains, wqkv, wo, xs.at[m]
        self.cos, self.sin, self.lk, self.lk2, self.lq, self.sq = (t.at[m] for t in tables)
        self.xn, self.raw, self.q, self.k, self.v, self.mixt, self.rl = (t.at[m] for t in saved)
        self.part, self.mixed, self.vt = part.at[m], mixed, vt

    def project(self, i, carry):
        rows = pl.ds(pl.multiple_of(i * 256, 256), 256)
        x = self.xs[pl.ds(i * 2, 2)].reshape(256, 1024).astype(F32)
        low = (x * norm_scale(x) * self.gains[0:1, :]).astype(BF)
        self.xn[rows, :] = low
        y = forward_dot(low, self.wqkv[:, pl.ds(0, 64), :].reshape(1024, 512))
        self.raw[rows, :] = y[:, :384]
        c, s = self.cos[rows, :], self.sin[rows, :]
        for head in range(3):
            u = y[:, head * HEAD : (head + 1) * HEAD]
            lane = HEAD * (head // 2)
            n = u * norm_scale(u) * self.gains[2:3, lane : lane + HEAD]
            turned = (n * c + pltpu.roll(n, HEAD // 2, 1) * s).astype(BF)
            if head < 2:
                self.q[head, rows, :] = turned
            else:
                self.k[rows, :] = turned
        value = y[:, 384:]
        self.v[rows, :] = value.astype(BF)
        self.vt[:, rows] = value.T.astype(BF)
        return carry

    def attend(self, head, i, carry):
        rows = pl.ds(pl.multiple_of(i * 256, 256), 256)
        s = against_cols(self.k[...], self.q[head, rows, :])
        seen = visible_tile(self.lk[...], self.lk2[...], self.lq[:, rows], self.sq[:, rows])
        e = jnp.where(seen, jnp.exp2(s * EXP2_SCALE), 0.0)
        inv = 1.0 / jnp.sum(e, axis=0, keepdims=True)
        self.rl[head, :, rows] = inv
        m = forward_dot(self.vt[...], e.astype(BF)) * inv
        self.mixt[head * HEAD : (head + 1) * HEAD, rows] = m.astype(BF)
        self.mixed[rows, head * HEAD : (head + 1) * HEAD] = m.T.astype(BF)
        return carry

    def project_out(self, i, carry):
        rows = pl.ds(pl.multiple_of(i * 256, 256), 256)
        y = forward_dot(self.mixed[rows, :], self.wo[...].reshape(256, 1024)).astype(BF)
        self.part[pl.ds(i * 2, 2)] = y.reshape(2, 128, 1024)
        return carry

    def pieces(self):
        return (
            [functools.partial(half_loop, self.project, p, 2, 4) for p in range(2)]
            + [
                functools.partial(half_loop, functools.partial(self.attend, head), p, 2, 4)
                for head in range(2)
                for p in range(2)
            ]
            + [functools.partial(half_loop, self.project_out, 0, 1, 4)]
        )


def sequence_block(out):
    def block(place, lo, n):
        return out.at[head_of(place), pl.ds(lo, n)]

    return block


def front_body(
    net,
    tok, cot, small, wq, wk, wv, wo_in, wg, wu, wd, cos, sin, lk, lk2, lq, sq,
    attended, normed, gains, wqkv, wo, cots, wgs, wus, wds, mid,
    xn_out, raw_out, q_out, k_out, v_out, mixt_out, rl_out,
    xn, raw, q, k, v, mixt, rl,
    xs, part, mixed, vt, stage, gate_stage, up_stage, outbox, inbox, *bufs,
):
    me = net.me
    heads = gather_heads_weights(net, wq, wk, wv, small, stage, wqkv)
    next(heads)
    swaps = [net.swap(tok.at[m], xs.at[m, ctx_of(me)]) for m in range(2)]
    gather = [
        gather_ring(net, "z", xs.at[m, head_of(me)], sequence_block(xs.at[m]), 128)
        for m in range(2)
    ]
    outs = gather_out_weights(net, wo_in, mid, wo)
    feed = gather_ff_weights(net, wg, wu, wd, gate_stage, up_stage, wgs, wus, wds)

    def cot_block(place, lo, n):
        return cots.at[:, tp_of(place), pl.ds(lo, n)]

    cots_in = gather_ring(net, "x", cot, cot_block, 128)
    own_cot = net.local(cot, cots.at[:, tp_of(me)])
    next(heads)
    swaps[0].wait()
    next(gather[0])
    next(outs)
    next(feed)
    next(gather[0])
    swaps[1].wait()
    next(gather[1])
    next(gather[0])
    drain(gather[0])
    next(outs)
    drain(heads)
    next(cots_in)
    sums = jnp.sum(wqkv[:, pl.ds(64, 16), :].astype(F32), axis=0)
    gains[...] = jnp.zeros_like(gains)
    gains[0:1, :] = jnp.concatenate([sums[0:1], sums[1:2]], axis=1)
    gains[1:2, :] = jnp.concatenate([sums[2:3], sums[3:4]], axis=1)
    gains[2:3, :512] = sums[4:5]
    tables = (cos, sin, lk, lk2, lq, sq)
    saved = (xn, raw, q, k, v, mixt, rl)
    work = [
        Front(m, gains, wqkv, wo, xs, tables, saved, part, mixed, vt).pieces() for m in range(2)
    ]

    def save(m):
        for src, dst in zip(saved, (xn_out, raw_out, q_out, k_out, v_out, mixt_out, rl_out)):
            net.local(src.at[m], dst.at[m])

    def settle(m):
        x = tok[m].astype(F32) + inbox[m].astype(F32)
        attended[m] = x
        normed[m] = (x * norm_scale(x) * gains[1:2, :]).astype(BF)

    for at, piece in enumerate(work[0][:-1]):
        piece()
        step(gather[1])
        if at == 1:
            drain(outs)
        if at == 4:
            step(cots_in)
    drain(gather[1])
    work[0][-1]()
    reduce0 = reduce_ring(net, "z", part.at[0], head_of, outbox.at[0], *bufs[:4])
    next(reduce0)
    step(cots_in)
    next(feed)
    save(0)
    for at, piece in enumerate(work[1]):
        piece()
        if at in (0, 2, 4):
            step(reduce0)
        if at == 5:
            step(cots_in)
    drain(reduce0)
    back0 = net.swap(outbox.at[0], inbox.at[0])
    reduce1 = reduce_ring(net, "z", part.at[1], head_of, outbox.at[1], *bufs[4:])
    next(reduce1)
    save(1)
    next(reduce1)
    drain(cots_in)
    next(reduce1)
    back0.wait()
    settle(0)
    drain(reduce1)
    back1 = net.swap(outbox.at[1], inbox.at[1])
    drain(feed)
    back1.wait()
    settle(1)


class Back:
    def __init__(self, m, gains, wqkv, wo, g, tables, saved, part, graw, dwqkv, dwo, sums, work):
        self.m, self.gains, self.wqkv, self.wo, self.g = m, gains, wqkv, wo, g.at[m]
        self.cos, self.sin, self.lk, self.lk2, self.lq, self.sq = (t.at[m] for t in tables)
        self.xn, self.raw, self.q, self.k, self.v, self.mixt, self.rl = (t.at[m] for t in saved)
        self.part, self.graw = part.at[m], graw.at[m]
        self.dwqkv, self.dwo, self.sums = dwqkv, dwo, sums
        self.kt, self.dk, self.dv, self.dq = work

    def begin(self):
        self.kt[...] = self.k[...].astype(F32).T.astype(BF)
        self.dk[...] = jnp.zeros_like(self.dk)
        self.dv[...] = jnp.zeros_like(self.dv)

    def attend(self, head, i, carry):
        rows = pl.ds(pl.multiple_of(i * 256, 256), 256)
        at = slice(head * HEAD, (head + 1) * HEAD)
        g = self.g[pl.ds(i * 2, 2)].reshape(256, 1024)
        wo = self.wo[head].reshape(HEAD, 1024)
        gm = against_cols(g, wo).astype(BF)
        gmt = against_cols(wo, g).astype(BF)
        delta = jnp.sum(
            gmt.astype(F32) * self.mixt[at, rows].astype(F32), axis=0, keepdims=True
        )
        qt = self.q[head, rows, :]
        s = against_cols(self.k[...], qt)
        seen = visible_tile(self.lk[...], self.lk2[...], self.lq[:, rows], self.sq[:, rows])
        p = jnp.where(seen, jnp.exp2(s * EXP2_SCALE), 0.0) * self.rl[head, :, rows]
        dp = forward_dot(self.v[...], gmt)
        ds = (p * (dp - delta)).astype(BF)
        self.dv[...] += forward_dot(p.astype(BF), gm)
        self.dk[...] += forward_dot(ds, qt)
        self.dq[head, rows, :] = forward_dot(self.kt[...], ds).T
        return carry

    def unproject(self, i, carry):
        rows = pl.ds(pl.multiple_of(i * 256, 256), 256)
        c, s = self.cos[rows, :], self.sin[rows, :]
        for head in range(3):
            lane = head // 2
            at = slice(head * HEAD, (head + 1) * HEAD)
            gr = (self.dq[head, rows, :] if head < 2 else self.dk[rows, :]) * HEAD ** (-0.5)
            gu = gr * c - pltpu.roll(gr, HEAD // 2, 1) * s
            u = self.raw[rows, at]
            r = norm_scale(u)
            self.sums[lane : lane + 1, :] += jnp.sum(gu * (u * r), axis=0, keepdims=True)
            n = gu * self.gains[2:3, lane * HEAD : (lane + 1) * HEAD]
            d = r * n - u * (r * r * r) * jnp.mean(n * u, axis=-1, keepdims=True)
            self.graw[rows, at] = d.astype(BF)
        self.graw[rows, 384:] = self.dv[rows, :].astype(BF)
        y = against_cols(self.graw[rows, :], self.wqkv[:, pl.ds(0, 64), :].reshape(1024, 512))
        self.part[pl.ds(i * 2, 2)] = y.astype(BF).reshape(2, 128, 1024)
        return carry

    def pieces(self):
        return (
            [self.begin]
            + [
                functools.partial(half_loop, functools.partial(self.attend, head), p, 2, 4)
                for head in range(2)
                for p in range(2)
            ]
            + [functools.partial(half_loop, self.unproject, p, 2, 4) for p in range(2)]
        )

    def out_weights(self):
        def some(i, carry):
            at = pl.ds(pl.multiple_of(i * 256, 256), 256)
            y = forward_dot(self.mixt[...], self.g[:, :, at].reshape(1024, 256))
            self.dwo[:, at] = y if self.m == 0 else self.dwo[:, at] + y
            return carry

        lax.fori_loop(0, 4, some, 0)

    def head_weights(self):
        def some(i, carry):
            at = pl.ds(pl.multiple_of(i * 256, 256), 256)
            y = across_rows(self.xn[:, at], self.graw[...])
            self.dwqkv[at, :] = y if self.m == 0 else self.dwqkv[at, :] + y
            return carry

        lax.fori_loop(0, 4, some, 0)


def back_body(
    net,
    g_own, out_part_in, xn_in, raw_in, q_in, k_in, v_in, mixt_in, rl_in,
    wqkv, wo, gains, cos, sin, lk, lk2, lq, sq,
    in_sum, out_sum, dwqkv_low, dwo_low, sums,
    xn, raw, q, k, v, mixt, rl,
    g, out_part, part, graw, dwqkv, dwo, kt, dk, dv, dq, outbox, *bufs,
):
    me = net.me
    swaps = [net.swap(g_own.at[m], g.at[m, ctx_of(me)]) for m in range(2)]
    fetched = [net.local(out_part_in.at[0], out_part.at[0])]
    saved = (xn, raw, q, k, v, mixt, rl)
    needed = [
        net.local(src.at[m], dst.at[m])
        for m in range(2)
        for src, dst in zip((xn_in, raw_in, q_in, k_in, v_in, mixt_in, rl_in), saved)
    ]
    fetched.append(net.local(out_part_in.at[1], out_part.at[1]))
    sums[...] = jnp.zeros_like(sums)
    gather = [
        gather_ring(net, "z", g.at[m, head_of(me)], sequence_block(g.at[m]), 128) for m in range(2)
    ]
    outs = [
        reduce_ring(net, "x", out_part.at[m], tp_of, out_sum.at[m], *bufs[4 * m + 8 : 4 * m + 12])
        for m in range(2)
    ]
    swaps[0].wait()
    next(gather[0])
    net.settle(fetched[0])
    next(outs[0])
    next(gather[0])
    swaps[1].wait()
    next(gather[1])
    next(gather[0])
    drain(gather[0])
    for copy in needed:
        net.settle(copy)
    net.settle(fetched[1])
    tables = (cos, sin, lk, lk2, lq, sq)
    work = [
        Back(m, gains, wqkv, wo, g, tables, saved, part, graw, dwqkv, dwo, sums, (kt, dk, dv, dq))
        for m in range(2)
    ]
    for at, piece in enumerate(work[0].pieces()):
        piece()
        step(gather[1])
        if at in (1, 3, 5):
            step(outs[0])
    drain(gather[1])
    reduce0 = reduce_ring(net, "z", part.at[0], head_of, outbox.at[0], *bufs[:4])
    next(reduce0)
    drain(outs[0])
    next(outs[1])
    for at, piece in enumerate(work[1].pieces()):
        piece()
        if at in (1, 2, 3):
            step(reduce0)
        if at in (2, 4, 6):
            step(outs[1])
    drain(reduce0)
    back0 = net.swap(outbox.at[0], in_sum.at[0])
    reduce1 = reduce_ring(net, "z", part.at[1], head_of, outbox.at[1], *bufs[4:8])
    next(reduce1)
    work[0].out_weights()
    next(reduce1)
    work[0].head_weights()
    next(reduce1)
    work[1].out_weights()
    drain(reduce1)
    back1 = net.swap(outbox.at[1], in_sum.at[1])
    work[1].head_weights()
    drain(outs[1])
    dwqkv_low[...] = dwqkv[...].astype(BF).reshape(16, 64, 512)
    dwo_low[...] = dwo[...].astype(BF).reshape(2, 8, 16, 1024)
    back0.wait()
    back1.wait()


def token_places(block_table, first, seq):
    blocks = block_table.shape[1]
    block = seq // blocks
    logical = (
        jnp.repeat(block_table, block, axis=1) * block + jnp.arange(seq, dtype=jnp.int32) % block
    )
    prompt = seq // 2
    segment = jnp.where(logical < prompt, 0, jnp.where(logical < prompt + first, 1, 2))
    end = jnp.where(segment == 1, prompt - 1 + first, seq - 1)
    position = jnp.where(segment == 0, logical, 895 - (end - logical))
    return logical, segment, position


def per_device(
    tokens,
    cotangent,
    block_table,
    segment_ids,
    positions,
    gain_attn,
    w_query,
    key_projection,
    value_projection,
    query_norm_gain,
    key_norm_gain,
    w_out,
    gain_ffn,
    w_gate,
    w_up,
    w_down,
):
    ctx = lax.axis_index("ctx")
    mbs, width = tokens.shape[0], tokens.shape[-1]
    tok = tokens[:, 0]
    cot = cotangent[:, 0].reshape(256, width)

    f = lax.axis_index("fsdp")
    here = (jnp.arange(16) == f)[:, None]

    def placed(gain):
        return jnp.where(here, gain[None], jnp.zeros((), BF)).reshape(-1)

    small = jnp.concatenate(
        [
            placed(gain_attn),
            placed(gain_ffn),
            placed(query_norm_gain),
            placed(key_norm_gain),
            jnp.zeros((256 + 11 * 512,), BF),
        ]
    ).reshape(16, 512)
    count = jnp.sum((segment_ids[:, 0] == 1).astype(jnp.int32), axis=1, keepdims=True)
    other = lax.ppermute(count, "fsdp", [(i, i ^ 1) for i in range(16)])
    first = jnp.where(ctx % 2 == f % 2, count, other)
    logical, seg, where_at = token_places(block_table, first, 1024)
    later = jnp.where(seg == 0, 4096, logical)
    start = jnp.where(seg == 2, 512 + first, 0)
    lk = jnp.broadcast_to(logical[:, :, None], (mbs, 1024, HEAD))
    lk2 = jnp.broadcast_to(later[:, :, None], (mbs, 1024, HEAD))
    lq, sq = logical[:, None, :], start[:, None, :]
    cos, sin = rope_tables(where_at)

    vm = pltpu.VMEM
    saves = [
        ((2, 1024, width), BF),
        ((2, 1024, 384), F32),
        ((2, 2, 1024, HEAD), BF),
        ((2, 1024, HEAD), BF),
        ((2, 1024, HEAD), BF),
        ((2, 256, 1024), BF),
        ((2, 2, 1, 1024), F32),
    ]
    sequence = vm((2, 8, 128, width), BF)
    (
        attended, normed_mid, gain_rows, wqkv, wo, cot_all, wg, wu, wd, _, *saved
    ) = comm_call(
        front_body,
        RING_Z + RING_X + WEIGHT_PLANE,
        [
            ((2, 128, width), F32),
            ((2, 128, width), BF),
            ((8, width), F32),
            ((16, 80, 512), BF),
            ((2, 8, 16, width), BF),
            ((2, 8, 128, width), BF),
            ((16, 64, 384), BF),
            ((16, 64, 384), BF),
            ((2, 192, width), BF),
            ((8, 16, width), BF),
        ]
        + saves,
        [vm(shape, kind) for shape, kind in saves]
        + [sequence, sequence, vm((1024, 256), BF), vm((HEAD, 1024), BF)]
        + [vm((2, 80, 512), BF), vm((8, 64, 384), BF), vm((8, 64, 384), BF)]
        + [vm((2, 128, width), BF), vm((2, 128, width), BF)]
        + reduce_ring_scratch(width) * 2,
        0,
        [True] + [False] * 9 + [True] * 6,
        [True] * 5 + [False] * 12,
        160,
        64,
    )(
        tok, cotangent[:, 0], small, w_query, key_projection, value_projection,
        w_out.reshape(8, 16, width), w_gate, w_up, w_down, cos, sin, lk, lk2, lq, sq,
    )
    g_attn_gain, g_ffn_gain = gain_rows[0], gain_rows[1]
    attended = attended.reshape(256, width)
    r2 = lax.rsqrt(jnp.mean(attended * attended, axis=-1, keepdims=True) + 1e-06)
    wg, wu, wd = wg.reshape(width, 384), wu.reshape(width, 384), wd.reshape(384, width)

    def gather_tp_body(net, src, out):
        def block(place, lo, n):
            return out.at[:, tp_of(place), pl.ds(lo, n)]

        net.local(src, out.at[:, tp_of(net.me)])
        return [gather_ring(net, "x", src, block, 128)]

    (mid_all,) = comm_call(
        gather_tp_body, RING_X, [((2, 8, 128, width), BF)], [], 2, [False], [False], 16
    )(normed_mid)
    nm = mid_all.reshape(2048, width)
    ct = cot_all.reshape(2048, width)
    gate, up = forward_dot(nm, wg), forward_dot(nm, wu)
    sig = jax.nn.sigmoid(gate)
    silu = gate * sig
    hidden = (silu * up).astype(BF)
    out_part = forward_dot(hidden, wd).astype(BF).reshape(2, 8, 128, width)
    g_hidden = against_cols(ct, wd)
    g_gate = (g_hidden * up * sig * (1.0 + gate * (1.0 - sig))).astype(BF)
    g_up = (g_hidden * silu).astype(BF)
    grad_down_part = across_rows(hidden, ct).astype(BF)
    grad_gate_part = across_rows(nm, g_gate).astype(BF)
    grad_up_part = across_rows(nm, g_up).astype(BF)
    mid_part = (against_cols(g_gate, wg) + against_cols(g_up, wu)).astype(BF)
    mid_part = mid_part.reshape(2, 8, 128, width)

    def reduce_tp_body(net, part, total, *bufs):
        return [
            reduce_ring(net, "x", part.at[m], tp_of, total.at[m], *bufs[4 * m : 4 * m + 4])
            for m in range(2)
        ]

    (g_mid,) = comm_call(
        reduce_tp_body,
        RING_X,
        [((2, 128, width), F32)],
        reduce_ring_scratch(width) * 2,
        3,
        [True],
        [True],
        48,
    )(mid_part)
    g_mid = g_mid.reshape(256, width)
    n2 = g_mid * g_ffn_gain
    grad_ffn_gain = jnp.sum(g_mid * attended * r2, axis=0)
    g_attended = (
        cot.astype(F32)
        + r2 * n2
        - attended * (r2 * r2 * r2) * jnp.mean(n2 * attended, axis=-1, keepdims=True)
    )
    g_attn = g_attended.astype(BF)

    in_sum, out_sum, dwqkv, dwo, head_gains = comm_call(
        back_body,
        RING_Z + RING_X,
        [
            ((2, 128, width), BF),
            ((2, 128, width), F32),
            ((16, 64, 512), BF),
            ((2, 8, 16, width), BF),
            ((8, HEAD), F32),
        ],
        [vm(shape, kind) for shape, kind in saves]
        + [sequence, sequence, sequence, vm((2, 1024, 512), BF)]
        + [vm((1024, 512), F32), vm((256, 1024), F32), vm((HEAD, 1024), BF)]
        + [vm((1024, HEAD), F32), vm((1024, HEAD), F32), vm((2, 1024, HEAD), F32)]
        + [vm((2, 128, width), BF)]
        + reduce_ring_scratch(width) * 4,
        4,
        [True] + [False] * 8 + [True] * 9,
        [True] * 5,
        96,
        24,
    )(g_attn.reshape(2, 128, width), out_part, *saved, wqkv, wo, gain_rows, cos, sin, lk, lk2, lq, sq)
    output = (attended + out_sum.reshape(256, width)).astype(BF)
    grad_query_gain, grad_key_gain = head_gains[0], head_gains[1]
    g_in = in_sum.reshape(256, width).astype(F32)
    x_own = tok.reshape(256, width).astype(F32)
    r1 = lax.rsqrt(jnp.mean(x_own * x_own, axis=-1, keepdims=True) + 1e-06)
    n1 = g_in * g_attn_gain
    grad_attn_gain = jnp.sum(g_in * x_own * r1, axis=0)
    grad_tokens = (
        g_attended
        + r1 * n1
        - x_own * (r1 * r1 * r1) * jnp.mean(n1 * x_own, axis=-1, keepdims=True)
    )

    small_terms = jnp.concatenate(
        [
            grad_attn_gain.reshape(16, 64),
            grad_ffn_gain.reshape(16, 64),
            grad_query_gain.reshape(16, 8),
            grad_key_gain.reshape(16, 8),
            jnp.zeros((16, 512 - 144), F32),
        ],
        axis=1,
    ).astype(BF)
    small_terms = jnp.broadcast_to(small_terms[:, None], (16, 16, 512))

    def terms_body(net, a, n, b, g, u, d, oa, on, ob, og, ou, od):
        return [
            scatter_samples(net, lambda place: a.at[chunk_of(place)], oa),
            scatter_samples(net, lambda place: n.at[chunk_of(place)], on),
            scatter_samples(net, lambda place: b.at[place["yl"], chip_of(place)], ob),
            scatter_copies(net, g, u, d, og, ou, od),
        ]

    ta, tn, tb, tg, tu, td = comm_call(
        terms_body,
        SAMPLE_SHIFTS + COPY_SHIFTS,
        [
            ((16, 64, 512), BF),
            ((16, 16, 512), BF),
            ((16, 16, width), BF),
            ((16, 64, 384), BF),
            ((16, 64, 384), BF),
            ((16, 192, 128), BF),
        ],
        [],
        6,
        [False] * 6,
        [False] * 6,
        96,
        8,
    )(
        dwqkv,
        small_terms,
        dwo,
        grad_gate_part.reshape(16, 64, 384),
        grad_up_part.reshape(16, 64, 384),
        grad_down_part.reshape(2, 192, width),
    )

    def summed(t):
        return jnp.sum(t.astype(F32), axis=0).astype(BF)

    def spread_body(net, a, n, b, g, u, d, oa, on, ob, og, ou, od, ma, mn, mb_, mo, mg, mu, md):
        def heads(src, mid, out):
            return spread(net, src, mid, HEAD_SHIFTS, head_of, lambda: swap_task(net, mid, out))

        def swap_out():
            return swap_task(net, mo, ob)

        return [
            spread(
                net, b, mb_, HEAD_SHIFTS, head_of, lambda: exchange_chips(net, mb_, mo, swap_out)
            ),
            spread(net, g, mg, CTX_SHIFTS, ctx_of, lambda: exchange_tp(net, mg, og)),
            spread(net, u, mu, CTX_SHIFTS, ctx_of, lambda: exchange_tp(net, mu, ou)),
            spread_down(net, d, md, od),
            heads(a, ma, oa),
            heads(n, mn, on),
        ]

    sa_, sn_, sb_, sg_, su_, sd_, *_ = comm_call(
        spread_body,
        CTX_SHIFTS + CHIP_SHIFTS + TP_SHIFTS + HEAD_SHIFTS + PLANE_SHIFTS + RING_Z,
        [
            ((8, 64, 512), BF),
            ((8, 16, 512), BF),
            ((8, 16, width), BF),
            ((64, 3072), BF),
            ((64, 3072), BF),
            ((192, width), BF),
            ((8, 64, 512), BF),
            ((8, 16, 512), BF),
            ((8, 16, width), BF),
            ((8, 16, width), BF),
            ((8, 64, 384), BF),
            ((8, 64, 384), BF),
            ((192, 128), BF),
        ],
        [],
        7,
        [False] * 6,
        [False] * 13,
        80,
        20,
    )(summed(ta), summed(tn), summed(tb), summed(tg), summed(tu), summed(td))

    qkv_grad = sa_.astype(F32)
    grad_w_query = qkv_grad[:, :, :256].transpose(1, 0, 2).reshape(64, 2048)
    grad_w_key = qkv_grad[:, :, 256:384].transpose(1, 0, 2).reshape(64, 1024)
    grad_w_value = qkv_grad[:, :, 384:].transpose(1, 0, 2).reshape(64, 1024)
    gains = jnp.sum(sn_[:, 0].astype(F32), axis=0)
    grad_w_out = sb_.astype(F32).reshape(128, width)
    grad_w_gate, grad_w_up, grad_w_down = (t.astype(F32) for t in (sg_, su_, sd_))
    return (
        output.reshape(2, 1, 128, width),
        grad_tokens.reshape(2, 1, 128, width),
        gains[:64],
        grad_w_query,
        grad_w_key,
        grad_w_value,
        gains[128:136],
        gains[136:144],
        grad_w_out,
        gains[64:128],
        grad_w_gate,
        grad_w_up,
        grad_w_down,
    )


def solution(mesh):
    placed = (
        P(None, "fsdp", "ctx", None),
        P(None, "fsdp", "ctx", None),
        P(),
        P(None, "fsdp", None),
        P(None, "fsdp", "ctx"),
        P("fsdp"),
        P("fsdp", None),
        P("fsdp", None),
        P("fsdp", None),
        P("fsdp"),
        P("fsdp"),
        P("fsdp", None),
        P("fsdp"),
        P("fsdp", None),
        P("fsdp", None),
        P("fsdp", None),
    )
    return jax.shard_map(
        per_device,
        mesh=mesh,
        in_specs=placed,
        out_specs=(
            P(None, "fsdp", "ctx", None),
            P(None, "fsdp", "ctx", None),
            P("fsdp"),
            P("fsdp", None),
            P("fsdp", None),
            P("fsdp", None),
            P("fsdp"),
            P("fsdp"),
            P("fsdp", None),
            P("fsdp"),
            P("fsdp", None),
            P("fsdp", None),
            P("fsdp", None),
        ),
        check_vma=False,
    )
```

time: 554 us -> 451 us (0.81)
  the two profiles are of different devices: /device:TPU:1 before, /device:TPU:9 now
where the time goes in v2:
time: 451 us; the launch traced here: 445 us
  Pallas kernels  367 us (81%)
  other arithmetic  34.1 us (8%)
  matrix products  31.7 us (7%)
  local copies, waits for them, and re-layouts  10.3 us (2%)
    pallas_call x1, Pallas kernels, per_device(): comm_call(front_body, RING_Z + RING_X + WEIGHT_PLANE, [((2, 128, width),...  98.6 us
    pallas_call x1, Pallas kernels, per_device(): comm_call(back_body, RING_Z + RING_X, [((2, 128, width), BF), ((2, 128, w...  79 us
    pallas_call x1, Pallas kernels, per_device(): comm_call(spread_body, CTX_SHIFTS + CHIP_SHIFTS + TP_SHIFTS + HEAD_SHIFTS...  63.5 us
    pallas_call x1, Pallas kernels, per_device(): comm_call(terms_body, SAMPLE_SHIFTS + COPY_SHIFTS, [((16, 64, 512), BF),...  62.7 us
    pallas_call x1, Pallas kernels, per_device(): comm_call(gather_tp_body, RING_X, [((2, 8, 128, width), BF)], [], 2, [Fal...  36.9 us
    pallas_call x1, Pallas kernels, per_device(): comm_call(reduce_tp_body, RING_X, [((2, 128, width), F32)], reduce_ring_s...  26.4 us
    dot_general x3, matrix products, against_cols(): lax.dot_general(a, b, (((1,), (1,)), ((), ())), preferred_element_type=F32)  11.7 us
    dot_general x3, matrix products, forward_dot(): return jnp.dot(a, b, preferred_element_type=F32)  10.8 us
  transfers between devices with their start and end apart: 1, of which 0 were waited for; matrix products, arithmetic and copies ran while one was open for 1% of the time, Pallas kernels for 0%

profile of v2, /device:TPU:9, one launch (start us, length us, event | category | flops | bytes accessed | tf_op | source)
XLA Modules:
  0.0 445.3 jit_solution(2480310673017806303)
XLA Ops:
  0.6 0.8 fusion.16
  1.5 0.8 collective-permute-start
  2.2 0.7 broadcast_multiply_fusion.2
  3.2 0.7 broadcast_select_fusion.3
  4.1 0.7 broadcast_select_fusion.1
  6.4 1.2 fusion.6
  7.8 0.7 compare_select_fusion
  8.6 3.7 fusion.12
  12.3 1.9 pad_maximum_fusion
  14.2 1.3 broadcast_in_dim.151.refs_12_.refs_14_
  15.5 1.3 broadcast_in_dim.153.refs_13_.refs_15_
  16.9 98.6 %shard_map.246 = (f32[2,128,1024]{2,1,0:T(8,128)}, bf16[2,128,1024]{2,1,0:T(8,128)(2,1)}, f32[8,1024]{1,0:T(8,128)}, bf16[16,80,512]{2,1,0:T(8,128)(2,1)}, bf16[...) custom-call(bf16[2,128,1024]{2,1,0:T(8,128)(2,1)} %bitcast.93, ...), custom_call_target="tpu_custom_call" | custom-call | tf_op jit(solution)/shard_map/pallas_call | solution.py:1028
  115.4 36.9 %shard_map.247 = bf16[2,8,128,1024]{3,2,1,0:T(8,128)(2,1)} custom-call(bf16[2,128,1024]{2,1,0:T(8,128)(2,1)} %get-tuple-element.49.refs_0_), custom_call_target="tpu_custom_call" | custom-call | tf_op jit(solution)/shard_map/pallas_call | solution.py:1070
  152.4 4.8 %fusion.24 = f32[2048,384]{1,0:T(8,128)S(1)} fusion(bf16[2048,1024]{1,0:T(8,128)(2,1)} %bitcast.117, bf16[384,1024]{1,0:T(8,128)(2,1)S(1)} %bitcast.119), kind=kOutput, calls=%fused_computation.90 | convolution fusion | flops 1610612736 | bytes 8126464 | tf_op jit(solution)/shard_map/dot_general | solution.py:608
  157.2 2.4 fusion.25
  159.6 3.9 multiply_convert_fusion
  163.6 2.7 convolution_convert_fusion.1
  166.3 4.5 %convolution_convert_fusion = bf16[2048,1024]{1,0:T(8,128)(2,1)} fusion(bf16[2048,384]{1,0:T(8,128)(2,1)S(1)} %get-tuple-element.115, bf16[384,1024]{1,0:T(8,128)(2,1)S(1)} %bitcast.120), kind=kOutput, calls=%fused_computation.1 | convolution fusion | flops 1612709888 | bytes 6553600 | tf_op jit(solution)/shard_map/dot_general | solution.py:612
  170.8 3.2 convolution_convert_fusion.3
  174.0 2.4 fusion.26
  176.4 3.2 convolution_convert_fusion.2
  179.6 4.5 %add_convert_fusion = bf16[2048,1024]{1,0:T(8,128)(2,1)} fusion(f32[2048,1024]{1,0:T(8,128)S(1)} %fusion.26, bf16[2048,384]{1,0:T(8,128)(2,1)S(1)} %get-tuple-element.117, bf16[1024,384]{1,0:T(8,128)(2,1)S(1)} %bitcast.101), kind=kOutput, calls=%fused_computation | convolution fusion | flops 1614807040 | bytes 14942208 | tf_op jit(solution)/shard_map/dot_general | solution.py:608
  184.2 26.4 %shard_map.248 = f32[2,128,1024]{2,1,0:T(8,128)} custom-call(bf16[2,8,128,1024]{3,2,1,0:T(8,128)(2,1)} %bitcast.92), custom_call_target="tpu_custom_call" | custom-call | tf_op jit(solution)/shard_map/pallas_call | solution.py:1095
  210.6 0.9 fusion.21
  211.6 1.5 multiply_reduce_fusion
  213.2 1.1 subtract_convert_fusion.refs_0_
  214.3 79.0 %shard_map.249 = (bf16[2,128,1024]{2,1,0:T(8,128)(2,1)}, f32[2,128,1024]{2,1,0:T(8,128)}, bf16[16,64,512]{2,1,0:T(8,128)(2,1)}, bf16[2,8,16,1024]{3,2,1,0:T(8,128)(2,1)}, f32[8,128]{1,0:T(8,128)}) custom-call(bf16[2,128,1024]{2,1,0:T(8,128)(2,1)} %subtract_convert_fusion.refs_0_, bf16[2,8,128,1024]{3,2,1,0:T(8,128)(2,1)} %bitcast.99, ...), custom_call_target="tpu_custom_call" | custom-call | tf_op jit(solution)/shard_map/pallas_call | solution.py:1115
  293.2 1.4 fusion.10
  294.7 0.7 convert.27
  295.8 0.7 broadcast_in_dim.157.refs_1_
  296.5 62.7 %shard_map.250 = (bf16[16,64,512]{2,1,0:T(8,128)(2,1)}, bf16[16,16,512]{2,1,0:T(8,128)(2,1)}, bf16[16,16,1024]{2,1,0:T(8,128)(2,1)}, bf16[16,64,384]{2,1,0:T(8,1...) custom-call(bf16[16,64,512]{2,1,0:T(8,128)(2,1)} %get-tuple-element.64.refs_0_, ...), custom_call_target="tpu_custom_call" | custom-call | tf_op jit(solution)/shard_map/pallas_call | solution.py:1170
  359.3 2.1 reduce_sum.151.refs_0_
  361.3 1.9 reduce_sum.154.refs_3_
  363.2 1.9 reduce_sum.155.refs_4_
  365.1 1.9 reduce_sum.156.refs_5_
  367.0 1.7 reduce_sum.153.refs_2_
  369.4 63.5 %shard_map.251 = (bf16[8,64,512]{2,1,0:T(8,128)(2,1)}, bf16[8,16,512]{2,1,0:T(8,128)(2,1)}, bf16[8,16,1024]{2,1,0:T(8,128)(2,1)}, bf16[64,3072]{1,0:T(8,128)(2,1...) custom-call(bf16[64,512]{1,0:T(8,128)(2,1)} %reduce_sum.151.refs_0_,, ...), custom_call_target="tpu_custom_call" | custom-call | tf_op jit(solution)/shard_map/pallas_call | solution.py:1217
  432.9 1.2 convert_element_type.122
  434.3 0.9 convert_reduce_fusion
  436.4 0.8 copy.39
  437.2 0.7 copy.44
  437.9 0.7 copy.45
  438.7 0.9 convert_element_type.123
  439.6 0.9 convert_element_type.124
  440.5 1.0 convert_element_type.125
  441.5 0.9 bitcast_convert_fusion
  442.4 0.9 fusion.11
  443.3 1.6 fusion.5
  (70 shorter events, 4.8 us)
Async XLA Ops:
  1.5 6.2 %collective-permute-start = (s32[2,1]{0,1:T(1,128)S(1)}, s32[2,1]{0,1:T(1,128)S(1)}, u32[]{:S(2)}, u32[]{:S(2)}) collective-permute-start(s32[2,1]{0,1:T(1,128)S(1)} %bitcast.116), channel_id=1, source_target_pairs={{0,1},{1,0},{2,3},{3,2},{4,5},{5,4},{6,7},{7,6},{8,9},{9,8},{10,11... | collective-permute-start | bytes 32 | tf_op jit(solution)/shard_map/ppermute | solution.py:1005
  115.4 36.9 %copy-start.15 = (bf16[2,192,1024]{2,1,0:T(8,128)(2,1)S(1)}, bf16[2,192,1024]{2,1,0:T(8,128)(2,1)}, u32[]{:S(2)}) copy-start(bf16[2,192,1024]{2,1,0:T(8,128)(2,1)} %get-tuple-element.48) | copy-start | bytes 2359300
  152.4 4.8 %copy-start.4 = (bf16[2,8,128,1024]{3,2,1,0:T(8,128)(2,1)S(1)}, bf16[2,8,128,1024]{3,2,1,0:T(8,128)(2,1)}, u32[]{:S(2)}) copy-start(bf16[2,8,128,1024]{3,2,1,0:T(8,128)(2,1)} %shard_map.247) | copy-start | bytes 12582916
  152.4 4.8 %copy-start.8 = (bf16[16,64,384]{2,1,0:T(8,128)(2,1)S(1)}, bf16[16,64,384]{2,1,0:T(8,128)(2,1)}, u32[]{:S(2)}) copy-start(bf16[16,64,384]{2,1,0:T(8,128)(2,1)} %get-tuple-element.51) | copy-start | bytes 2359300
  157.2 2.4 copy-start.7
  159.6 3.9 copy-start.14
  184.2 27.3 %copy-start = (f32[2,128,1024]{2,1,0:T(8,128)S(1)}, f32[2,128,1024]{2,1,0:T(8,128)}, u32[]{:S(2)}) copy-start(f32[2,128,1024]{2,1,0:T(8,128)} %get-tuple-element.46) | copy-start | bytes 3145732
  184.2 29.0 %copy-start.3 = (bf16[2,1,128,1024]{3,2,1,0:T(8,128)(2,1)S(1)}, bf16[2,1,128,1024]{3,2,1,0:T(8,128)(2,1)}, u32[]{:S(2)}) copy-start(bf16[2,1,128,1024]{3,2,1,0:T(8,128)(2,1)} %param.17) | copy-start | bytes 1572868
  210.6 2.6 copy-start.1
  214.3 79.0 %copy-start.2 = (bf16[2,1,128,1024]{3,2,1,0:T(8,128)(2,1)S(1)}, bf16[2,1,128,1024]{3,2,1,0:T(8,128)(2,1)}, u32[]{:S(2)}) copy-start(bf16[2,1,128,1024]{3,2,1,0:T(8,128)(2,1)} %param.16) | copy-start | bytes 1572868
  359.3 9.4 %copy-start.13 = (bf16[16,16,512]{2,1,0:T(8,128)(2,1)S(1)}, bf16[16,16,512]{2,1,0:T(8,128)(2,1)}, u32[]{:S(2)}) copy-start(bf16[16,16,512]{2,1,0:T(8,128)(2,1)} %get-tuple-element.68) | copy-start | bytes 786436
  432.9 5.8 %copy-start.11 = (bf16[64,3072]{1,0:T(8,128)(2,1)S(1)}, bf16[64,3072]{1,0:T(8,128)(2,1)}, u32[]{:S(2)}) copy-start(bf16[64,3072]{1,0:T(8,128)(2,1)} %get-tuple-element.76) | copy-start | bytes 1179652
  432.9 6.7 %copy-start.10 = (bf16[64,3072]{1,0:T(8,128)(2,1)S(1)}, bf16[64,3072]{1,0:T(8,128)(2,1)}, u32[]{:S(2)}) copy-start(bf16[64,3072]{1,0:T(8,128)(2,1)} %get-tuple-element.77) | copy-start | bytes 1179652
  434.2 6.4 %copy-start.9 = (bf16[192,1024]{1,0:T(8,128)(2,1)S(1)}, bf16[192,1024]{1,0:T(8,128)(2,1)}, u32[]{:S(2)}) copy-start(bf16[192,1024]{1,0:T(8,128)(2,1)} %get-tuple-element.78) | copy-start | bytes 1179652
  434.2 7.3 %copy-start.12 = (bf16[8,16,1024]{2,1,0:T(8,128)(2,1)S(1)}, bf16[8,16,1024]{2,1,0:T(8,128)(2,1)}, u32[]{:S(2)}) copy-start(bf16[8,16,1024]{2,1,0:T(8,128)(2,1)} %get-tuple-element.75) | copy-start | bytes 786436
  436.4 6.0 %copy-start.6 = (f32[2,128,1024]{2,1,0:T(8,128)S(1)}, f32[2,128,1024]{2,1,0:T(8,128)}, u32[]{:S(2)}) copy-start(f32[2,128,1024]{2,1,0:T(8,128)} %get-tuple-element.62) | copy-start | bytes 3145732
  439.6 3.7 copy-start.5

commit v3 on v2

--- a/solution.py
+++ b/solution.py
@@ -85,6 +85,7 @@
     if a or b or d
 ]
 HEAD_SHIFTS = [{"z": a, "core": b} for a in range(4) for b in range(2) if a or b]
+Y_SHIFTS = [{"yl": 1}, {"yh": 1}, {"yl": 1, "yh": 1}]
 RING_Z = [{"z": 1}, {"z": 3}, {"core": 1}, {"yl": 1, "core": 1}]
 RING_X = [{"x": 1}, {"x": 3}, {"core": 1}]
 
@@ -94,10 +95,9 @@
 
 
 class Net:
-    def __init__(self, send_sems, recv_sems, local_sems, pair_sems):
+    def __init__(self, send_sems, recv_sems, local_sems):
         self.me = my_place()
         self.send_sems, self.recv_sems, self.local_sems = send_sems, recv_sems, local_sems
-        self.pair_sems = pair_sems
         self.count = 0
         self.locals = 0
         self.pending = []
@@ -124,18 +124,6 @@
         copy.start()
         self.pending.append(copy.wait_send)
         return copy
-
-    def pair(self, src, dst, place, recv, new=True):
-        if new:
-            self.count += 1
-        return pltpu.make_async_remote_copy(
-            src_ref=src,
-            dst_ref=dst,
-            send_sem=self.send_sems.at[self.count - 1],
-            recv_sem=self.pair_sems.at[recv],
-            device_id=device_of(place),
-            device_id_type=MESH,
-        )
 
     def spare(self):
         self.locals += 1
@@ -210,7 +198,7 @@
     shifts = unique(shifts)
 
     def kernel(*refs):
-        refs, sems = refs[:-4], refs[-4:]
+        refs, sems = refs[:-3], refs[-3:]
         net = Net(*sems)
         net.enter(shifts)
         drain(*(body(net, *refs) or ()))
@@ -228,10 +216,9 @@
             pltpu.SemaphoreType.DMA((n_remote,)),
             pltpu.SemaphoreType.DMA((n_remote,)),
             pltpu.SemaphoreType.DMA((n_local,)),
-            pltpu.SemaphoreType.DMA((2,)),
         ],
         compiler_params=pltpu.CompilerParams(
-            collective_id=cid, has_side_effects=True, vmem_limit_bytes=60 << 20
+            collective_id=cid, has_side_effects=True, vmem_limit_bytes=62 << 20
         ),
     )
 
@@ -244,39 +231,7 @@
     next(task, None)
 
 
-class Weave:
-    def __init__(self):
-        self.tasks = []
-
-    def add(self, task):
-        next(task)
-        self.tasks.append(task)
-        return task
-
-    def tick(self, count=1):
-        for _ in range(count):
-            if self.tasks:
-                self.step(self.tasks.pop(0))
-
-    def step(self, task):
-        try:
-            next(task)
-            self.tasks.append(task)
-        except StopIteration:
-            pass
-
-    def finish(self, task):
-        if task in self.tasks:
-            self.tasks.remove(task)
-            for _ in task:
-                pass
-
-    def finish_all(self):
-        drain(*self.tasks)
-        self.tasks = []
-
-
-def gather_ring(net, axis, src, block, rows):
+def gather_ring(net, axis, src, block, rows, pair="core"):
     me = net.me
     half = rows // 2
     low, high = (0, half), (half, half)
@@ -291,7 +246,7 @@
         here = cut(part) if step == 0 else at(step, part)
         return net.send(here, at(step, part), **shift)
 
-    right, left, other = {axis: 1}, {axis: -1}, {"core": 1}
+    right, left, other = {axis: 1}, {axis: -1}, {pair: 1}
     r0 = send(0, low, right)
     l1 = send(0, high, left)
     r1 = send(0, high, right)
@@ -373,7 +328,7 @@
     ]
 
 
-def gather_heads_weights(net, wq, wk, wv, small, stage, out):
+def gather_heads_weights(net, wq, wk, wv, small, stage, out, small_out):
     me = net.me
     mine = fsdp_of(me)
     staged = []
@@ -381,24 +336,31 @@
         h = me["z"] * 2 + core
         place = stage.at[core]
         for src, dst in (
-            (wq.at[:, pl.ds(pl.multiple_of(h * 256, 256), 256)], place.at[pl.ds(0, 64), pl.ds(0, 256)]),
-            (wk.at[:, pl.ds(pl.multiple_of(h * 128, 128), 128)], place.at[pl.ds(0, 64), pl.ds(256, 128)]),
-            (wv.at[:, pl.ds(pl.multiple_of(h * 128, 128), 128)], place.at[pl.ds(0, 64), pl.ds(384, 128)]),
-            (small, place.at[pl.ds(64, 16)]),
+            (wq.at[:, pl.ds(pl.multiple_of(h * 256, 256), 256)], place.at[:, pl.ds(0, 256)]),
+            (wk.at[:, pl.ds(pl.multiple_of(h * 128, 128), 128)], place.at[:, pl.ds(256, 128)]),
+            (wv.at[:, pl.ds(pl.multiple_of(h * 128, 128), 128)], place.at[:, pl.ds(384, 128)]),
         ):
             staged.append(net.local(src, dst))
     yield
     for copy in staged:
         net.settle(copy)
-    kept = net.local(stage.at[me["core"]], out.at[mine])
+    kept = [
+        net.local(stage.at[me["core"]], out.at[mine]),
+        net.local(small, small_out.at[mine]),
+    ]
     copies = [
-        net.send(stage.at[moved(me, shift)["core"]], out.at[mine], **shift)
+        net.send(src, dst, **shift)
         for shift in WEIGHT_PLANE
+        for src, dst in (
+            (stage.at[moved(me, shift)["core"]], out.at[mine]),
+            (small, small_out.at[mine]),
+        )
     ]
     yield
     for copy in copies:
         copy.wait_recv()
-    net.settle(kept)
+    for copy in kept:
+        net.settle(copy)
 
 
 def gather_out_weights(net, src, mid, out):
@@ -423,51 +385,37 @@
     net.settle(kept)
 
 
-def gather_ff_weights(net, gate, up, down, gate_stage, up_stage, gate_out, up_out, down_out):
+def pack_columns(src, stage, lane):
+    first = lax.broadcasted_iota(jnp.int32, (64, 256), 1) < 64
+    for j in range(8):
+        low = 192 * j - 64 * (j % 2)
+        a = src[:, low : low + 256].astype(F32)
+        b = src[:, 1536 + low : 1536 + low + 256].astype(F32)
+        if j % 2:
+            a = pltpu.roll(a, 192, 1)
+        else:
+            b = pltpu.roll(b, 64, 1)
+        rest = jnp.where(first, jnp.concatenate([a[:, 128:], a[:, 128:]], axis=1), b)
+        stage[j, :, lane : lane + 128] = a[:, :128].astype(BF)
+        stage[j, :, lane + 128 : lane + 384] = rest.astype(BF)
+
+
+def gather_ff_weights(net, down, stage, out, down_out):
     me = net.me
     mine = fsdp_of(me)
-    staged = []
-    for j in range(8):
-        at = pl.ds(j * 384, 384)
-        staged.append(net.local(gate.at[:, at], gate_stage.at[j]))
-        staged.append(net.local(up.at[:, at], up_stage.at[j]))
-    chip = chip_of(me)
-    near = dict(me, x=chip // 2, core=chip % 2)
-    far = dict(near, yh=(me["yh"] + 1) % 2, yl=(me["yl"] + 1) % 2)
-    half = me["core"]
-    here = tp_of(me) == chip
-    away = jnp.logical_not(here)
-    one = net.pair(down, down_out.at[half], near, half)
-    two = net.pair(down, down_out.at[half], far, half)
-    stay = pltpu.make_async_copy(down, down_out.at[half], net.spare())
-    yield
-    for copy in staged:
-        net.settle(copy)
-
-    def pieces(place):
-        j = tp_of(place)
-        return [(gate_stage.at[j], gate_out.at[mine]), (up_stage.at[j], up_out.at[mine])]
-
-    kept = [net.local(src, dst) for src, dst in pieces(me)]
-    copies = [
-        net.send(src, dst, **shift)
-        for shift in WEIGHT_PLANE
-        for src, dst in pieces(moved(me, shift))
-    ]
-    two.start()
-    pl.when(here)(stay.start)
-    pl.when(away)(one.start)
+    kept = [
+        net.local(stage.at[tp_of(me)], out.at[mine]),
+        net.local(down, down_out.at[me["yh"]]),
+    ]
+    copies = [net.send(down, down_out.at[me["yh"]], yh=1, yl=1)]
+    copies += [
+        net.send(stage.at[tp_of(moved(me, shift))], out.at[mine], **shift) for shift in WEIGHT_PLANE
+    ]
     yield
     for copy in copies:
         copy.wait_recv()
     for copy in kept:
         net.settle(copy)
-    for h in (0, 1):
-        arrived = net.pair(down, down_out.at[h], near, h, new=False)
-        pl.when(jnp.logical_not(here & (half == h)))(arrived.wait_recv)
-    two.wait_send()
-    pl.when(here)(stay.wait)
-    pl.when(away)(one.wait_send)
 
 
 def chunk_of(place):
@@ -485,110 +433,84 @@
     net.settle(kept)
 
 
-def copy_index(place):
-    return place["yh"] * 8 + ctx_of(place)
-
-
-def scatter_copies(net, gate, up, down, gate_out, up_out, down_out):
+def reduce_ff(net, g, d, rhg, rhd, sg, sd, rg, rd, tg, td, yg, yd, gsum, dsum):
     me = net.me
-
-    def piece(place):
-        return down.at[place["yh"], :, pl.ds(pl.multiple_of(ctx_of(place) * 128, 128), 128)]
-
-    mine = copy_index(me)
-
-    def pieces(place):
-        at = copy_index(place)
-        return [
-            (gate.at[at], gate_out.at[mine]),
-            (up.at[at], up_out.at[mine]),
-            (piece(place), down_out.at[mine]),
+    z = [(me["z"] + k) % 4 for k in range(4)]
+    ring = ({"z": 1}, {"z": -1})
+    half = [
+        [
+            net.send(g.at[h, z[2]], rhg.at[h], **ring[h]),
+            net.send(d.at[z[2], h], rhd.at[h], **ring[h]),
         ]
-
-    for src, dst in pieces(me):
-        net.local(src, dst)
-    copies = [
-        net.send(src, dst, **shift) for shift in COPY_SHIFTS for src, dst in pieces(moved(me, shift))
-    ]
+        for h in range(2)
+    ]
+    near = [
+        net.send(g.at[1, z[1]], rg.at[0, 1], **ring[0]),
+        net.send(d.at[z[1], 1], rd.at[0, 1], **ring[0]),
+        net.send(g.at[0, z[3]], rg.at[1, 0], **ring[1]),
+        net.send(d.at[z[3], 0], rd.at[1, 0], **ring[1]),
+    ]
+    yield
+    for h, to in ((0, z[1]), (1, z[3])):
+        for copy in half[h]:
+            copy.wait_recv()
+        add_rows(sg.at[h], [g.at[h, to], rhg.at[h]], 128)
+        add_rows(sd.at[h], [d.at[to, h], rhd.at[h]], 192)
+        near.append(net.send(sg.at[h], rg.at[h, h], **ring[h]))
+        near.append(net.send(sd.at[h], rd.at[h, h], **ring[h]))
+    yield
+    for copy in near:
+        copy.wait_recv()
+    for h in range(2):
+        add_rows(tg.at[h], [g.at[h, z[0]], rg.at[0, h], rg.at[1, h]], 128)
+        for l in range(2):
+            at = pl.ds(128 * l, 128)
+            terms = [d.at[z[0], h, :, at], rd.at[0, h, :, at], rd.at[1, h, :, at]]
+            add_rows(td.at[h, l], terms, 192)
+    copies = []
+    for k, shift in enumerate(Y_SHIFTS):
+        to = moved(me, shift)
+        rows = pl.ds(pl.multiple_of(to["yl"] * 64, 64), 64)
+        copies.append(net.send(tg.at[to["yh"], rows], yg.at[k], **shift))
+        copies.append(net.send(td.at[to["yh"], to["yl"]], yd.at[k], **shift))
     yield
     for copy in copies:
         copy.wait_recv()
-
-
-def spread(net, src, out, shifts, index, after=None):
+    rows = pl.ds(pl.multiple_of(me["yl"] * 64, 64), 64)
+    add_rows(gsum, [tg.at[me["yh"], rows]] + [yg.at[k] for k in range(3)], 64)
+    add_rows(dsum, [td.at[me["yh"], me["yl"]]] + [yd.at[k] for k in range(3)], 192)
+
+
+def reduce_ff_scratch():
+    shapes = [(128, 768), (192, 256)]
+    out = [pltpu.VMEM((2,) + s, BF) for s in shapes]
+    out += [pltpu.VMEM((2,) + s, BF) for s in shapes]
+    out += [pltpu.VMEM((2, 2) + s, BF) for s in shapes]
+    out += [pltpu.VMEM((2, 128, 768), BF), pltpu.VMEM((2, 2, 192, 128), BF)]
+    out += [pltpu.VMEM((3, 64, 768), BF), pltpu.VMEM((3, 192, 128), BF)]
+    out += [pltpu.VMEM((64, 768), BF), pltpu.VMEM((192, 128), BF)]
+    return out
+
+
+def exchange(net, src, out, shifts, index):
     me = net.me
-    mine = out.at[index(me)]
-    kept = net.local(src, mine)
-    copies = [net.send(src, mine, **shift) for shift in shifts]
+    mine = index(me)
+    kept = net.local(src.at[mine], out.at[mine])
+    copies = [net.send(src.at[index(moved(me, shift))], out.at[mine], **shift) for shift in shifts]
     yield
     for copy in copies:
         copy.wait_recv()
     net.settle(kept)
-    if after is not None:
+
+
+def sum_everywhere(net, own, first, middle, second, total):
+    stages = ((own, first, TP_SHIFTS, middle), (middle, second, COPY_SHIFTS, total))
+    for src, slots, shifts, dst in stages:
+        copies = [net.send(src, slots.at[k], **shift) for k, shift in enumerate(shifts)]
         yield
-        yield from after()
-
-
-def swap_task(net, src, out):
-    swapped = net.swap(src, out)
-    yield
-    swapped.wait()
-
-
-def exchange_chips(net, src, out, after):
-    me = net.me
-    mine = chip_of(me)
-    kept = net.local(src.at[mine], out.at[mine])
-    copies = [
-        net.send(src.at[chip_of(moved(me, shift))], out.at[mine], **shift) for shift in CHIP_SHIFTS
-    ]
-    yield
-    for copy in copies:
-        copy.wait_recv()
-    net.settle(kept)
-    yield from after()
-
-
-def exchange_tp(net, src, out):
-    me = net.me
-    mine = tp_of(me)
-    place = out.at[:, pl.ds(pl.multiple_of(mine * 384, 128), 384)]
-    net.local(src.at[mine], place)
-    copies = [net.send(src.at[tp_of(moved(me, shift))], place, **shift) for shift in TP_SHIFTS]
-    yield
-    for copy in copies:
-        copy.wait_recv()
-
-
-def spread_down(net, src, mid, out):
-    me = net.me
-    j = tp_of(me)
-    goal = dict(me, yh=j // 4, x=j % 4, core=me["yh"])
-    stays = (j == chip_of(me)) & (me["yh"] == me["core"])
-    sent = net.pair(src, mid, goal, 0)
-    kept = pltpu.make_async_copy(src, mid, net.spare())
-
-    @pl.when(stays)
-    def _():
-        kept.start()
-        kept.wait()
-
-    @pl.when(jnp.logical_not(stays))
-    def _():
-        sent.start()
-
-    yield
-
-    @pl.when(jnp.logical_not(stays))
-    def _():
-        sent.wait()
-
-    place = out.at[:, pl.ds(pl.multiple_of(ctx_of(me) * 128, 128), 128)]
-    net.local(mid, place)
-    copies = [net.send(mid, place, **shift) for shift in CTX_SHIFTS]
-    yield
-    for copy in copies:
-        copy.wait_recv()
+        for copy in copies:
+            copy.wait_recv()
+        dst[...] = src[...] + jnp.sum(slots[...], axis=0)
 
 
 def rope_tables(where_at):
@@ -619,9 +541,10 @@
     return lax.rsqrt(jnp.mean(v * v, axis=-1, keepdims=True) + 1e-06)
 
 
-def visible_tile(lk, lk2, lq, sq):
-    lk, lk2 = jnp.concatenate([lk, lk], axis=1), jnp.concatenate([lk2, lk2], axis=1)
-    return (lk <= lq) & (lk2 >= sq)
+def visible_tile(lk, lq, sq):
+    later = jnp.where(lk < 512, 4096, lk)
+    later, lk = jnp.concatenate([later, later], axis=1), jnp.concatenate([lk, lk], axis=1)
+    return (lk <= lq) & (later >= sq)
 
 
 def half_loop(body, part, parts, count):
@@ -631,7 +554,7 @@
 class Front:
     def __init__(self, m, gains, wqkv, wo, xs, tables, saved, part, mixed, vt):
         self.gains, self.wqkv, self.wo, self.xs = gains, wqkv, wo, xs.at[m]
-        self.cos, self.sin, self.lk, self.lk2, self.lq, self.sq = (t.at[m] for t in tables)
+        self.cos, self.sin, self.lk, self.lq, self.sq = (t.at[m] for t in tables)
         self.xn, self.raw, self.q, self.k, self.v, self.mixt, self.rl = (t.at[m] for t in saved)
         self.part, self.mixed, self.vt = part.at[m], mixed, vt
 
@@ -660,7 +583,7 @@
     def attend(self, head, i, carry):
         rows = pl.ds(pl.multiple_of(i * 256, 256), 256)
         s = against_cols(self.k[...], self.q[head, rows, :])
-        seen = visible_tile(self.lk[...], self.lk2[...], self.lq[:, rows], self.sq[:, rows])
+        seen = visible_tile(self.lk[...], self.lq[:, rows], self.sq[:, rows])
         e = jnp.where(seen, jnp.exp2(s * EXP2_SCALE), 0.0)
         inv = 1.0 / jnp.sum(e, axis=0, keepdims=True)
         self.rl[head, :, rows] = inv
@@ -696,14 +619,14 @@
 
 def front_body(
     net,
-    tok, cot, small, wq, wk, wv, wo_in, wg, wu, wd, cos, sin, lk, lk2, lq, sq,
-    attended, normed, gains, wqkv, wo, cots, wgs, wus, wds, mid,
+    tok, cot, small, wq, wk, wv, wo_in, wg, wu, wd, cos, sin, lk, lq, sq,
+    attended, normed, gains, wqkv, wo, cots, wgu, wds, mid,
     xn_out, raw_out, q_out, k_out, v_out, mixt_out, rl_out,
     xn, raw, q, k, v, mixt, rl,
-    xs, part, mixed, vt, stage, gate_stage, up_stage, outbox, inbox, *bufs,
+    xs, part, mixed, vt, stage, smalls, gu_stage, outbox, inbox, *bufs,
 ):
     me = net.me
-    heads = gather_heads_weights(net, wq, wk, wv, small, stage, wqkv)
+    heads = gather_heads_weights(net, wq, wk, wv, small, stage, wqkv, smalls)
     next(heads)
     swaps = [net.swap(tok.at[m], xs.at[m, ctx_of(me)]) for m in range(2)]
     gather = [
@@ -711,7 +634,7 @@
         for m in range(2)
     ]
     outs = gather_out_weights(net, wo_in, mid, wo)
-    feed = gather_ff_weights(net, wg, wu, wd, gate_stage, up_stage, wgs, wus, wds)
+    feed = gather_ff_weights(net, wd, gu_stage, wgu, wds)
 
     def cot_block(place, lo, n):
         return cots.at[:, tp_of(place), pl.ds(lo, n)]
@@ -722,21 +645,23 @@
     swaps[0].wait()
     next(gather[0])
     next(outs)
-    next(feed)
+    pack_columns(wg, gu_stage, 0)
+    pack_columns(wu, gu_stage, 384)
     next(gather[0])
     swaps[1].wait()
     next(gather[1])
     next(gather[0])
     drain(gather[0])
-    next(outs)
     drain(heads)
     next(cots_in)
-    sums = jnp.sum(wqkv[:, pl.ds(64, 16), :].astype(F32), axis=0)
+    next(outs)
+    pairs = [smalls[2 * i].astype(F32) + smalls[2 * i + 1].astype(F32) for i in range(8)]
+    both = sum(pairs[1:], pairs[0])
     gains[...] = jnp.zeros_like(gains)
-    gains[0:1, :] = jnp.concatenate([sums[0:1], sums[1:2]], axis=1)
-    gains[1:2, :] = jnp.concatenate([sums[2:3], sums[3:4]], axis=1)
-    gains[2:3, :512] = sums[4:5]
-    tables = (cos, sin, lk, lk2, lq, sq)
+    gains[0:1, :] = jnp.concatenate([p[0:1] for p in pairs], axis=1)
+    gains[1:2, :] = jnp.concatenate([p[1:2] for p in pairs], axis=1)
+    gains[2:3, : 2 * HEAD] = jnp.concatenate([both[2:3], both[3:4]], axis=1)
+    tables = (cos, sin, lk, lq, sq)
     saved = (xn, raw, q, k, v, mixt, rl)
     work = [
         Front(m, gains, wqkv, wo, xs, tables, saved, part, mixed, vt).pieces() for m in range(2)
@@ -754,10 +679,8 @@
     for at, piece in enumerate(work[0][:-1]):
         piece()
         step(gather[1])
-        if at == 1:
+        if at == 3:
             drain(outs)
-        if at == 4:
-            step(cots_in)
     drain(gather[1])
     work[0][-1]()
     reduce0 = reduce_ring(net, "z", part.at[0], head_of, outbox.at[0], *bufs[:4])
@@ -777,21 +700,134 @@
     next(reduce1)
     save(1)
     next(reduce1)
-    drain(cots_in)
+    step(cots_in)
     next(reduce1)
     back0.wait()
     settle(0)
     drain(reduce1)
     back1 = net.swap(outbox.at[1], inbox.at[1])
+    drain(cots_in)
     drain(feed)
     back1.wait()
     settle(1)
 
 
+class Feed:
+    def __init__(self, m, wgu, wd, nm, ct, hid, ggu, out, mid, dg, dd):
+        self.m, self.wgu, self.wd = m, wgu, wd
+        self.nm, self.ct, self.hid, self.ggu = nm.at[m], ct.at[m], hid.at[m], ggu.at[m]
+        self.out, self.mid, self.dg, self.dd = out.at[m], mid.at[m], dg, dd
+
+    def tile(self, i, carry):
+        rows = pl.ds(pl.multiple_of(i * 256, 256), 256)
+        blocks = pl.ds(i * 2, 2)
+        wgu = self.wgu[...].reshape(1024, 768)
+        wd = self.wd[...].reshape(384, 1024)
+        y = forward_dot(self.nm[blocks].reshape(256, 1024), wgu)
+        gate, up = y[:, :384], y[:, 384:]
+        gh = against_cols(self.ct[blocks].reshape(256, 1024), wd)
+        sig = 1.0 / (1.0 + jnp.exp(-gate))
+        silu = gate * sig
+        hidden = (silu * up).astype(BF)
+        self.hid[rows, :] = hidden
+        gg = (gh * up * sig * (1.0 + gate * (1.0 - sig))).astype(BF)
+        gu = (gh * silu).astype(BF)
+        self.ggu[rows, :384] = gg
+        self.ggu[rows, 384:] = gu
+        self.mid[blocks] = (
+            against_cols(self.ggu[rows, :], wgu).astype(BF).reshape(2, 128, 1024)
+        )
+        self.out[blocks] = forward_dot(hidden, wd).astype(BF).reshape(2, 128, 1024)
+        return carry
+
+    def pieces(self):
+        return [functools.partial(half_loop, self.tile, p, 4, 4) for p in range(4)]
+
+    def in_weights(self):
+        def some(i, carry):
+            at = pl.ds(pl.multiple_of(i * 128, 128), 128)
+            y = across_rows(self.nm[:, :, at].reshape(1024, 128), self.ggu[...])
+            self.dg[at, :] = y if self.m == 0 else self.dg[at, :] + y
+            return carry
+
+        lax.fori_loop(0, 8, some, 0)
+
+    def down_weights(self):
+        def some(i, carry):
+            at = pl.ds(pl.multiple_of(i * 128, 128), 128)
+            y = across_rows(self.hid[:, at], self.ct[...].reshape(1024, 1024))
+            self.dd[at, :] = y if self.m == 0 else self.dd[at, :] + y
+            return carry
+
+        lax.fori_loop(0, 3, some, 0)
+
+
+def feed_body(
+    net,
+    normed, attended, cot, cots, wgu, wds, gains,
+    g_attended, g_attn, gain_sum, dg_low, dd_low, out_part_out,
+    nm, hid, ggu, out_part, mid_part, dg, dd, total, *bufs,
+):
+    me = net.me
+
+    def block(m):
+        def at(place, lo, n):
+            return nm.at[m, tp_of(place), pl.ds(lo, n)]
+
+        return at
+
+    own = [net.local(normed.at[m], nm.at[m, tp_of(me)]) for m in range(2)]
+    gather = [gather_ring(net, "x", normed.at[m], block(m), 128) for m in range(2)]
+    next(gather[0])
+    next(gather[0])
+    next(gather[1])
+    for copy in own:
+        net.settle(copy)
+    drain(gather[0])
+    work = [Feed(m, wgu, wds, nm, cots, hid, ggu, out_part, mid_part, dg, dd) for m in range(2)]
+    gain_sum[...] = jnp.zeros_like(gain_sum)
+
+    def settle(m):
+        x, g_mid = attended[m], total[m]
+        r = norm_scale(x)
+        n = g_mid * gains[1:2, :]
+        gain_sum[0:1, :] += jnp.sum(g_mid * x * r, axis=0, keepdims=True)
+        y = cot[m].astype(F32) + r * n - x * (r * r * r) * jnp.mean(n * x, axis=-1, keepdims=True)
+        g_attended[m] = y
+        g_attn[m] = y.astype(BF)
+
+    for piece in work[0].pieces():
+        piece()
+        step(gather[1])
+    drain(gather[1])
+    net.local(out_part.at[0], out_part_out.at[0])
+    reduce0 = reduce_ring(net, "x", mid_part.at[0], tp_of, total.at[0], *bufs[:4])
+    next(reduce0)
+    for at, piece in enumerate(work[1].pieces()):
+        piece()
+        step(reduce0)
+    drain(reduce0)
+    net.local(out_part.at[1], out_part_out.at[1])
+    reduce1 = reduce_ring(net, "x", mid_part.at[1], tp_of, total.at[1], *bufs[4:])
+    next(reduce1)
+    settle(0)
+    work[0].in_weights()
+    next(reduce1)
+    work[0].down_weights()
+    next(reduce1)
+    work[1].in_weights()
+    drain(reduce1)
+    settle(1)
+    work[1].down_weights()
+    dg_low[...] = dg[...].astype(BF).reshape(2, 4, 128, 768)
+    for j in range(4):
+        dd_low[j] = dd[:, 256 * j : 256 * j + 256].astype(BF).reshape(2, 192, 256)
+
+
 class Back:
     def __init__(self, m, gains, wqkv, wo, g, tables, saved, part, graw, dwqkv, dwo, sums, work):
         self.m, self.gains, self.wqkv, self.wo, self.g = m, gains, wqkv, wo, g.at[m]
-        self.cos, self.sin, self.lk, self.lk2, self.lq, self.sq = (t.at[m] for t in tables)
+        self.cos, self.sin, self.lk, self.lq, self.sq = (t.at[m] for t in tables)
         self.xn, self.raw, self.q, self.k, self.v, self.mixt, self.rl = (t.at[m] for t in saved)
         self.part, self.graw = part.at[m], graw.at[m]
         self.dwqkv, self.dwo, self.sums = dwqkv, dwo, sums
@@ -814,7 +850,7 @@
         )
         qt = self.q[head, rows, :]
         s = against_cols(self.k[...], qt)
-        seen = visible_tile(self.lk[...], self.lk2[...], self.lq[:, rows], self.sq[:, rows])
+        seen = visible_tile(self.lk[...], self.lq[:, rows], self.sq[:, rows])
         p = jnp.where(seen, jnp.exp2(s * EXP2_SCALE), 0.0) * self.rl[head, :, rows]
         dp = forward_dot(self.v[...], gmt)
         ds = (p * (dp - delta)).astype(BF)
@@ -874,13 +910,16 @@
 
 def back_body(
     net,
-    g_own, out_part_in, xn_in, raw_in, q_in, k_in, v_in, mixt_in, rl_in,
-    wqkv, wo, gains, cos, sin, lk, lk2, lq, sq,
-    in_sum, out_sum, dwqkv_low, dwo_low, sums,
+    g_own, tok, gain_sum, dg, dd, out_part_in, xn_in, raw_in, q_in, k_in, v_in, mixt_in, rl_in,
+    wqkv, wo, gains, cos, sin, lk, lq, sq,
+    in_sum, out_sum, heads_out, outs_out, gu_out, down_out, gain_total,
     xn, raw, q, k, v, mixt, rl,
-    g, out_part, part, graw, dwqkv, dwo, kt, dk, dv, dq, outbox, *bufs,
+    g, out_part, part, graw, dwqkv, dwo, kt, dk, dv, dq, outbox, sums,
+    qkv_low, wo_low, qkv_in, wo_in, qkv_sum, wo_sum, qkv_all, wo_all, wo_mid, gu_all,
+    gain_own, gain_first, gain_middle, gain_second, *bufs,
 ):
     me = net.me
+    ff, bufs = bufs[:12], bufs[12:]
     swaps = [net.swap(g_own.at[m], g.at[m, ctx_of(me)]) for m in range(2)]
     fetched = [net.local(out_part_in.at[0], out_part.at[0])]
     saved = (xn, raw, q, k, v, mixt, rl)
@@ -898,6 +937,31 @@
         reduce_ring(net, "x", out_part.at[m], tp_of, out_sum.at[m], *bufs[4 * m + 8 : 4 * m + 12])
         for m in range(2)
     ]
+    gsum, dsum = ff[-2:]
+
+    def feed_gradients():
+        yield from reduce_ff(net, dg, dd, *ff)
+        kept = [
+            net.local(gsum, gu_all.at[ctx_of(me)]),
+            net.local(dsum, down_out.at[ctx_of(me)]),
+        ]
+        spreads = [
+            gather_ring(
+                net, "z", src, lambda place, lo, n, out=out: out.at[ctx_of(place), pl.ds(lo, n)],
+                rows, "yl",
+            )
+            for src, out, rows in ((gsum, gu_all, 64), (dsum, down_out, 192))
+        ]
+        for _ in range(4):
+            for spread in spreads:
+                next(spread)
+            yield
+        drain(*spreads)
+        for copy in kept:
+            net.settle(copy)
+        yield from exchange(net, gu_all, gu_out, TP_SHIFTS, tp_of)
+
+    feed = feed_gradients()
     swaps[0].wait()
     next(gather[0])
     net.settle(fetched[0])
@@ -907,10 +971,11 @@
     next(gather[1])
     next(gather[0])
     drain(gather[0])
+    next(feed)
     for copy in needed:
         net.settle(copy)
     net.settle(fetched[1])
-    tables = (cos, sin, lk, lk2, lq, sq)
+    tables = (cos, sin, lk, lq, sq)
     work = [
         Back(m, gains, wqkv, wo, g, tables, saved, part, graw, dwqkv, dwo, sums, (kt, dk, dv, dq))
         for m in range(2)
@@ -925,29 +990,80 @@
     next(reduce0)
     drain(outs[0])
     next(outs[1])
+    step(feed)
     for at, piece in enumerate(work[1].pieces()):
         piece()
         if at in (1, 2, 3):
             step(reduce0)
         if at in (2, 4, 6):
             step(outs[1])
+        if at in (3, 4, 6):
+            step(feed)
     drain(reduce0)
     back0 = net.swap(outbox.at[0], in_sum.at[0])
     reduce1 = reduce_ring(net, "z", part.at[1], head_of, outbox.at[1], *bufs[4:8])
     next(reduce1)
     work[0].out_weights()
     next(reduce1)
+    work[1].out_weights()
     work[0].head_weights()
     next(reduce1)
-    work[1].out_weights()
+    work[1].head_weights()
+    qkv_low[...] = dwqkv[...].astype(BF).reshape(16, 64, 512)
+    low = dwo[...].astype(BF)
+    for half in range(2):
+        wo_low[:, :, half * 16 : half * 16 + 16, :] = low[:, half * 512 : half * 512 + 512].reshape(
+            2, 8, 16, 512
+        )
+    scattered = [
+        scatter_samples(net, lambda place: qkv_low.at[chunk_of(place)], qkv_in),
+        scatter_samples(net, lambda place: wo_low.at[place["yl"], chip_of(place)], wo_in),
+    ]
+    for task in scattered:
+        next(task)
+    step(feed)
     drain(reduce1)
     back1 = net.swap(outbox.at[1], in_sum.at[1])
-    work[1].head_weights()
     drain(outs[1])
-    dwqkv_low[...] = dwqkv[...].astype(BF).reshape(16, 64, 512)
-    dwo_low[...] = dwo[...].astype(BF).reshape(2, 8, 16, 1024)
+    step(feed)
     back0.wait()
     back1.wait()
+    row = jnp.zeros((1, 1024), F32)
+    for m in range(2):
+        x = tok[m].astype(F32)
+        row = row + jnp.sum(in_sum[m].astype(F32) * x * norm_scale(x), axis=0, keepdims=True)
+    for k in range(8):
+        at = slice(k * 128, k * 128 + 128)
+        gain_own[k : k + 1, :] = row[:, at]
+        gain_own[8 + k : 9 + k, :] = gain_sum[0:1, at]
+    gain_own[16:24, :] = sums[...]
+    gain = sum_everywhere(net, gain_own, gain_first, gain_middle, gain_second, gain_total)
+    next(gain)
+    drain(*scattered)
+    qkv_sum[...] = jnp.sum(qkv_in[...].astype(F32), axis=0).astype(BF)
+    wo_sum[...] = jnp.sum(wo_in[...].astype(F32), axis=0).astype(BF)
+    kept = [
+        net.local(qkv_sum, qkv_all.at[head_of(me)]),
+        net.local(wo_sum, wo_all.at[head_of(me)]),
+    ]
+    spreads = [
+        gather_ring(net, "z", src, sequence_block(out), rows)
+        for src, out, rows in ((qkv_sum, qkv_all, 64), (wo_sum, wo_all, 32))
+    ]
+    for task in spreads:
+        next(task)
+    step(feed)
+    next(gain)
+    drain(*spreads)
+    for copy in kept:
+        net.settle(copy)
+    heads_back = net.swap(qkv_all, heads_out)
+    drain(exchange(net, wo_all, wo_mid, CHIP_SHIFTS, chip_of))
+    outs_back = net.swap(wo_mid, outs_out)
+    drain(gain)
+    drain(feed)
+    heads_back.wait()
+    outs_back.wait()
 
 
 def token_places(block_table, first, seq):
@@ -984,7 +1100,6 @@
     ctx = lax.axis_index("ctx")
     mbs, width = tokens.shape[0], tokens.shape[-1]
     tok = tokens[:, 0]
-    cot = cotangent[:, 0].reshape(256, width)
 
     f = lax.axis_index("fsdp")
     here = (jnp.arange(16) == f)[:, None]
@@ -992,23 +1107,27 @@
     def placed(gain):
         return jnp.where(here, gain[None], jnp.zeros((), BF)).reshape(-1)
 
+    zero = jnp.zeros((64,), BF)
+    odd = f % 2 == 1
+
+    def halved(gain):
+        return jnp.concatenate([jnp.where(odd, zero, gain), jnp.where(odd, gain, zero)])
+
     small = jnp.concatenate(
         [
-            placed(gain_attn),
-            placed(gain_ffn),
+            halved(gain_attn),
+            halved(gain_ffn),
             placed(query_norm_gain),
             placed(key_norm_gain),
-            jnp.zeros((256 + 11 * 512,), BF),
+            jnp.zeros((12 * HEAD,), BF),
         ]
-    ).reshape(16, 512)
+    ).reshape(16, HEAD)
     count = jnp.sum((segment_ids[:, 0] == 1).astype(jnp.int32), axis=1, keepdims=True)
     other = lax.ppermute(count, "fsdp", [(i, i ^ 1) for i in range(16)])
     first = jnp.where(ctx % 2 == f % 2, count, other)
     logical, seg, where_at = token_places(block_table, first, 1024)
-    later = jnp.where(seg == 0, 4096, logical)
     start = jnp.where(seg == 2, 512 + first, 0)
     lk = jnp.broadcast_to(logical[:, :, None], (mbs, 1024, HEAD))
-    lk2 = jnp.broadcast_to(later[:, :, None], (mbs, 1024, HEAD))
     lq, sq = logical[:, None, :], start[:, None, :]
     cos, sin = rope_tables(where_at)
 
@@ -1023,241 +1142,127 @@
         ((2, 2, 1, 1024), F32),
     ]
     sequence = vm((2, 8, 128, width), BF)
-    (
-        attended, normed_mid, gain_rows, wqkv, wo, cot_all, wg, wu, wd, _, *saved
-    ) = comm_call(
+    attended, normed, gain_rows, wqkv, wo, cots, wgu, wds, _, *saved = comm_call(
         front_body,
         RING_Z + RING_X + WEIGHT_PLANE,
         [
             ((2, 128, width), F32),
             ((2, 128, width), BF),
             ((8, width), F32),
-            ((16, 80, 512), BF),
+            ((16, 64, 512), BF),
             ((2, 8, 16, width), BF),
             ((2, 8, 128, width), BF),
-            ((16, 64, 384), BF),
-            ((16, 64, 384), BF),
+            ((16, 64, 768), BF),
             ((2, 192, width), BF),
             ((8, 16, width), BF),
         ]
         + saves,
         [vm(shape, kind) for shape, kind in saves]
         + [sequence, sequence, vm((1024, 256), BF), vm((HEAD, 1024), BF)]
-        + [vm((2, 80, 512), BF), vm((8, 64, 384), BF), vm((8, 64, 384), BF)]
+        + [vm((2, 64, 512), BF), vm((16, 16, HEAD), BF), vm((8, 64, 768), BF)]
         + [vm((2, 128, width), BF), vm((2, 128, width), BF)]
         + reduce_ring_scratch(width) * 2,
         0,
-        [True] + [False] * 9 + [True] * 6,
-        [True] * 5 + [False] * 12,
+        [True] + [False] * 6 + [True] * 2 + [False] + [True] * 5,
+        [True] * 5 + [False] * 11,
         160,
         64,
     )(
         tok, cotangent[:, 0], small, w_query, key_projection, value_projection,
-        w_out.reshape(8, 16, width), w_gate, w_up, w_down, cos, sin, lk, lk2, lq, sq,
+        w_out.reshape(8, 16, width), w_gate, w_up, w_down, cos, sin, lk, lq, sq,
     )
-    g_attn_gain, g_ffn_gain = gain_rows[0], gain_rows[1]
-    attended = attended.reshape(256, width)
-    r2 = lax.rsqrt(jnp.mean(attended * attended, axis=-1, keepdims=True) + 1e-06)
-    wg, wu, wd = wg.reshape(width, 384), wu.reshape(width, 384), wd.reshape(384, width)
-
-    def gather_tp_body(net, src, out):
-        def block(place, lo, n):
-            return out.at[:, tp_of(place), pl.ds(lo, n)]
-
-        net.local(src, out.at[:, tp_of(net.me)])
-        return [gather_ring(net, "x", src, block, 128)]
-
-    (mid_all,) = comm_call(
-        gather_tp_body, RING_X, [((2, 8, 128, width), BF)], [], 2, [False], [False], 16
-    )(normed_mid)
-    nm = mid_all.reshape(2048, width)
-    ct = cot_all.reshape(2048, width)
-    gate, up = forward_dot(nm, wg), forward_dot(nm, wu)
-    sig = jax.nn.sigmoid(gate)
-    silu = gate * sig
-    hidden = (silu * up).astype(BF)
-    out_part = forward_dot(hidden, wd).astype(BF).reshape(2, 8, 128, width)
-    g_hidden = against_cols(ct, wd)
-    g_gate = (g_hidden * up * sig * (1.0 + gate * (1.0 - sig))).astype(BF)
-    g_up = (g_hidden * silu).astype(BF)
-    grad_down_part = across_rows(hidden, ct).astype(BF)
-    grad_gate_part = across_rows(nm, g_gate).astype(BF)
-    grad_up_part = across_rows(nm, g_up).astype(BF)
-    mid_part = (against_cols(g_gate, wg) + against_cols(g_up, wu)).astype(BF)
-    mid_part = mid_part.reshape(2, 8, 128, width)
-
-    def reduce_tp_body(net, part, total, *bufs):
-        return [
-            reduce_ring(net, "x", part.at[m], tp_of, total.at[m], *bufs[4 * m : 4 * m + 4])
-            for m in range(2)
-        ]
-
-    (g_mid,) = comm_call(
-        reduce_tp_body,
+    g_attended, g_attn, gain_sum, dg, dd, out_part = comm_call(
+        feed_body,
         RING_X,
-        [((2, 128, width), F32)],
-        reduce_ring_scratch(width) * 2,
-        3,
-        [True],
-        [True],
-        48,
-    )(mid_part)
-    g_mid = g_mid.reshape(256, width)
-    n2 = g_mid * g_ffn_gain
-    grad_ffn_gain = jnp.sum(g_mid * attended * r2, axis=0)
-    g_attended = (
-        cot.astype(F32)
-        + r2 * n2
-        - attended * (r2 * r2 * r2) * jnp.mean(n2 * attended, axis=-1, keepdims=True)
-    )
-    g_attn = g_attended.astype(BF)
-
-    in_sum, out_sum, dwqkv, dwo, head_gains = comm_call(
+        [
+            ((2, 128, width), F32),
+            ((2, 128, width), BF),
+            ((8, width), F32),
+            ((2, 4, 128, 768), BF),
+            ((4, 2, 192, 256), BF),
+            ((2, 8, 128, width), BF),
+        ],
+        [sequence, vm((2, 1024, 384), BF), vm((2, 1024, 768), BF), sequence, sequence]
+        + [vm((1024, 768), F32), vm((384, width), F32), vm((2, 128, width), F32)]
+        + reduce_ring_scratch(width) * 2,
+        1,
+        [True] * 7,
+        [True] * 5 + [False],
+        64,
+        8,
+    )(normed, attended, cotangent[:, 0], cots, wgu, wds, gain_rows)
+    in_sum, out_sum, heads, outs, gu, down, gain_total = comm_call(
         back_body,
-        RING_Z + RING_X,
+        RING_Z + RING_X + [{"yl": 1}] + SAMPLE_SHIFTS + CHIP_SHIFTS + TP_SHIFTS + COPY_SHIFTS,
         [
             ((2, 128, width), BF),
             ((2, 128, width), F32),
-            ((16, 64, 512), BF),
-            ((2, 8, 16, width), BF),
-            ((8, HEAD), F32),
+            ((8, 64, 512), BF),
+            ((8, 32, 512), BF),
+            ((8, 64, 768), BF),
+            ((8, 192, 128), BF),
+            ((24, HEAD), F32),
         ],
         [vm(shape, kind) for shape, kind in saves]
         + [sequence, sequence, sequence, vm((2, 1024, 512), BF)]
         + [vm((1024, 512), F32), vm((256, 1024), F32), vm((HEAD, 1024), BF)]
         + [vm((1024, HEAD), F32), vm((1024, HEAD), F32), vm((2, 1024, HEAD), F32)]
-        + [vm((2, 128, width), BF)]
+        + [vm((2, 128, width), BF), vm((8, HEAD), F32)]
+        + [vm((16, 64, 512), BF), vm((2, 8, 32, 512), BF)]
+        + [vm((16, 64, 512), BF), vm((16, 32, 512), BF)]
+        + [vm((64, 512), BF), vm((32, 512), BF)]
+        + [vm((8, 64, 512), BF), vm((8, 32, 512), BF), vm((8, 32, 512), BF), vm((8, 64, 768), BF)]
+        + [vm((24, HEAD), F32), vm((7, 24, HEAD), F32), vm((24, HEAD), F32), vm((15, 24, HEAD), F32)]
+        + reduce_ff_scratch()
         + reduce_ring_scratch(width) * 4,
-        4,
-        [True] + [False] * 8 + [True] * 9,
-        [True] * 5,
-        96,
-        24,
-    )(g_attn.reshape(2, 128, width), out_part, *saved, wqkv, wo, gain_rows, cos, sin, lk, lk2, lq, sq)
-    output = (attended + out_sum.reshape(256, width)).astype(BF)
-    grad_query_gain, grad_key_gain = head_gains[0], head_gains[1]
-    g_in = in_sum.reshape(256, width).astype(F32)
-    x_own = tok.reshape(256, width).astype(F32)
-    r1 = lax.rsqrt(jnp.mean(x_own * x_own, axis=-1, keepdims=True) + 1e-06)
-    n1 = g_in * g_attn_gain
-    grad_attn_gain = jnp.sum(g_in * x_own * r1, axis=0)
+        2,
+        [True] * 5 + [False] * 8 + [True] * 8,
+        [True] * 2 + [False] * 4 + [True],
+        224,
+        40,
+    )(g_attn, tok, gain_sum, dg, dd, out_part, *saved, wqkv, wo, gain_rows, cos, sin, lk, lq, sq)
+    output = (attended + out_sum).astype(BF)
+    g_in = in_sum.astype(F32)
+    x_own = tok.astype(F32)
+    r1 = norm_scale(x_own)
+    n1 = g_in * gain_rows[0]
     grad_tokens = (
         g_attended
         + r1 * n1
         - x_own * (r1 * r1 * r1) * jnp.mean(n1 * x_own, axis=-1, keepdims=True)
     )
-
-    small_terms = jnp.concatenate(
-        [
-            grad_attn_gain.reshape(16, 64),
-            grad_ffn_gain.reshape(16, 64),
-            grad_query_gain.reshape(16, 8),
-            grad_key_gain.reshape(16, 8),
-            jnp.zeros((16, 512 - 144), F32),
-        ],
-        axis=1,
-    ).astype(BF)
-    small_terms = jnp.broadcast_to(small_terms[:, None], (16, 16, 512))
-
-    def terms_body(net, a, n, b, g, u, d, oa, on, ob, og, ou, od):
-        return [
-            scatter_samples(net, lambda place: a.at[chunk_of(place)], oa),
-            scatter_samples(net, lambda place: n.at[chunk_of(place)], on),
-            scatter_samples(net, lambda place: b.at[place["yl"], chip_of(place)], ob),
-            scatter_copies(net, g, u, d, og, ou, od),
-        ]
-
-    ta, tn, tb, tg, tu, td = comm_call(
-        terms_body,
-        SAMPLE_SHIFTS + COPY_SHIFTS,
-        [
-            ((16, 64, 512), BF),
-            ((16, 16, 512), BF),
-            ((16, 16, width), BF),
-            ((16, 64, 384), BF),
-            ((16, 64, 384), BF),
-            ((16, 192, 128), BF),
-        ],
-        [],
-        6,
-        [False] * 6,
-        [False] * 6,
-        96,
-        8,
-    )(
-        dwqkv,
-        small_terms,
-        dwo,
-        grad_gate_part.reshape(16, 64, 384),
-        grad_up_part.reshape(16, 64, 384),
-        grad_down_part.reshape(2, 192, width),
-    )
-
-    def summed(t):
-        return jnp.sum(t.astype(F32), axis=0).astype(BF)
-
-    def spread_body(net, a, n, b, g, u, d, oa, on, ob, og, ou, od, ma, mn, mb_, mo, mg, mu, md):
-        def heads(src, mid, out):
-            return spread(net, src, mid, HEAD_SHIFTS, head_of, lambda: swap_task(net, mid, out))
-
-        def swap_out():
-            return swap_task(net, mo, ob)
-
-        return [
-            spread(
-                net, b, mb_, HEAD_SHIFTS, head_of, lambda: exchange_chips(net, mb_, mo, swap_out)
-            ),
-            spread(net, g, mg, CTX_SHIFTS, ctx_of, lambda: exchange_tp(net, mg, og)),
-            spread(net, u, mu, CTX_SHIFTS, ctx_of, lambda: exchange_tp(net, mu, ou)),
-            spread_down(net, d, md, od),
-            heads(a, ma, oa),
-            heads(n, mn, on),
-        ]
-
-    sa_, sn_, sb_, sg_, su_, sd_, *_ = comm_call(
-        spread_body,
-        CTX_SHIFTS + CHIP_SHIFTS + TP_SHIFTS + HEAD_SHIFTS + PLANE_SHIFTS + RING_Z,
-        [
-            ((8, 64, 512), BF),
-            ((8, 16, 512), BF),
-            ((8, 16, width), BF),
-            ((64, 3072), BF),
-            ((64, 3072), BF),
-            ((192, width), BF),
-            ((8, 64, 512), BF),
-            ((8, 16, 512), BF),
-            ((8, 16, width), BF),
-            ((8, 16, width), BF),
-            ((8, 64, 384), BF),
-            ((8, 64, 384), BF),
-            ((192, 128), BF),
-        ],
-        [],
-        7,
-        [False] * 6,
-        [False] * 13,
-        80,
-        20,
-    )(summed(ta), summed(tn), summed(tb), summed(tg), summed(tu), summed(td))
-
-    qkv_grad = sa_.astype(F32)
+    qkv_grad = heads.astype(F32)
     grad_w_query = qkv_grad[:, :, :256].transpose(1, 0, 2).reshape(64, 2048)
     grad_w_key = qkv_grad[:, :, 256:384].transpose(1, 0, 2).reshape(64, 1024)
     grad_w_value = qkv_grad[:, :, 384:].transpose(1, 0, 2).reshape(64, 1024)
-    gains = jnp.sum(sn_[:, 0].astype(F32), axis=0)
-    grad_w_out = sb_.astype(F32).reshape(128, width)
-    grad_w_gate, grad_w_up, grad_w_down = (t.astype(F32) for t in (sg_, su_, sd_))
+    grad_w_out = outs.astype(F32).reshape(8, 2, 16, 512).transpose(0, 2, 1, 3).reshape(128, width)
+
+    def columns(part):
+        return part.reshape(8, 64, 2, 192).transpose(1, 2, 0, 3).reshape(64, 3072).astype(F32)
+
+    grad_w_gate, grad_w_up = columns(gu[:, :, :384]), columns(gu[:, :, 384:])
+    grad_w_down = down.astype(F32).transpose(1, 0, 2).reshape(192, width)
+
+    def mine(rows, n):
+        return lax.dynamic_slice_in_dim(rows.reshape(-1), f * n, n)
+
+    gains = [
+        mine(gain_total[0:8], 64),
+        mine(gain_total[8:16], 64),
+        mine(gain_total[16], 8),
+        mine(gain_total[17], 8),
+    ]
     return (
         output.reshape(2, 1, 128, width),
         grad_tokens.reshape(2, 1, 128, width),
-        gains[:64],
+        gains[0],
         grad_w_query,
         grad_w_key,
         grad_w_value,
-        gains[128:136],
-        gains[136:144],
+        gains[2],
+        gains[3],
         grad_w_out,
-        gains[64:128],
+        gains[1],
         grad_w_gate,
         grad_w_up,
         grad_w_down,

time: 451 us -> 352 us (0.78)
  the two profiles are of different devices: /device:TPU:9 before, /device:TPU:1 now
where the time goes in v3:
time: 352 us; the launch traced here: 345 us
  Pallas kernels  308 us (88%)
  local copies, waits for them, and re-layouts  20.7 us (6%)
  other arithmetic  14.4 us (4%)
    pallas_call x1, Pallas kernels, per_device(): comm_call(back_body, RING_Z + RING_X + [{'yl': 1}] + SAMPLE_SHIFTS + CHIP...  158 us
    pallas_call x1, Pallas kernels, per_device(): comm_call(front_body, RING_Z + RING_X + WEIGHT_PLANE, [((2, 128, width),...  91 us
    pallas_call x1, Pallas kernels, per_device(): comm_call(feed_body, RING_X, [((2, 128, width), F32), ((2, 128, width), B...  58.2 us
  transfers between devices with their start and end apart: 1, of which 0 were waited for; matrix products, arithmetic and copies ran while one was open for 1% of the time, Pallas kernels for 0%

profile of v3, /device:TPU:1, one launch (start us, length us, event | category | flops | bytes accessed | tf_op | source)
XLA Modules:
  0.0 345.3 jit_solution(10591651363256136882)
XLA Ops:
  0.6 0.8 fusion.10
  1.5 1.5 collective-permute-start
  3.0 0.7 broadcast_multiply_fusion.1
  3.7 0.1 broadcast_in_dim.93
  3.7 0.1 mul.121
  3.8 0.1 mul.127
  3.9 0.7 broadcast_select_fusion
  4.7 0.1 select_n.143
  4.8 0.1 select_n.145
  4.9 0.7 broadcast_select_fusion.3
  5.6 0.7 concatenate.9
  6.2 0.0 collective-permute-done
  6.3 0.7 compare_select_fusion
  6.9 0.1 fusion.7
  7.0 3.7 %fusion.6 = (f32[2,1024,64]{2,1,0:T(8,128)S(1)}, f32[2,1024,64]{2,1,0:T(8,128)S(1)}, f32[2,1024,64]{2,1,0:T(8,128)S(1)}) fusion(f32[64]{0:T(128)S(1)} %multiply_exponential_fusion, f32[2,1024]{1,0:T(2,128)S(1)} %get-tuple-element.99), kind=kLoop, calls=%fused_computation.21 | loop fusion | flops 262144 | bytes 1581312 | tf_op jit(solution)/shard_map/neg | solution.py:522
  10.7 1.9 pad_maximum_fusion
  12.7 1.3 broadcast_in_dim.99.refs_12_.refs_18_
  14.0 91.0 %shard_map.246 = (f32[2,128,1024]{2,1,0:T(8,128)}, bf16[2,128,1024]{2,1,0:T(8,128)(2,1)}, f32[8,1024]{1,0:T(8,128)}, bf16[16,64,512]{2,1,0:T(8,128)(2,1)}, bf16[...) custom-call(bf16[2,128,1024]{2,1,0:T(8,128)(2,1)} %bitcast.69, ...), custom_call_target="tpu_custom_call" | custom-call | tf_op jit(solution)/shard_map/pallas_call | solution.py:1145
  105.1 58.2 %shard_map.247 = (f32[2,128,1024]{2,1,0:T(8,128)}, bf16[2,128,1024]{2,1,0:T(8,128)(2,1)}, f32[8,1024]{1,0:T(8,128)}, bf16[2,4,128,768]{3,2,1,0:T(8,128)(2,1)}, b...) custom-call(bf16[2,128,1024]{2,1,0:T(8,128)(2,1)} %get-tuple-element.42.refs_0_, ...), custom_call_target="tpu_custom_call" | custom-call | tf_op jit(solution)/shard_map/pallas_call | solution.py:1174
  163.3 158.4 %shard_map.248 = (bf16[2,128,1024]{2,1,0:T(8,128)(2,1)}, f32[2,128,1024]{2,1,0:T(8,128)}, bf16[8,64,512]{2,1,0:T(8,128)(2,1)}, bf16[8,32,512]{2,1,0:T(8,128)(2,1...) custom-call(bf16[2,128,1024]{2,1,0:T(8,128)(2,1)} %get-tuple-element.47.refs_0_, ...), custom_call_target="tpu_custom_call" | custom-call | tf_op jit(solution)/shard_map/pallas_call | solution.py:1194
  321.8 1.2 convert_element_type.54
  323.0 0.8 slice_bitcast_fusion
  323.8 0.8 slice_bitcast_fusion.1
  324.7 0.8 slice.30
  325.5 0.7 slice_bitcast_fusion.3
  326.1 0.8 fusion.14
  326.9 0.0 copy-done.5
  326.9 0.2 slice_convert_fusion
  327.1 0.8 reshape.359
  327.8 0.6 copy.37
  328.5 1.3 reshape.351
  329.7 0.7 reshape.360
  330.5 0.6 copy.38
  331.1 1.3 reshape.352
  332.4 2.0 copy.42
  334.4 1.7 copy.50
  336.1 1.8 copy.51
  337.8 0.3 fusion
  338.3 0.4 copy.36
  338.7 0.9 copy.46
  339.6 1.0 copy_bitcast_fusion
  340.5 0.0 copy-done.1
  340.5 0.9 fusion.5
  341.5 0.6 dynamic_slice.16
  342.1 0.6 dynamic_slice.21
  342.6 0.6 dynamic-slice_bitcast_fusion
  343.2 0.6 dynamic-slice_bitcast_fusion.1
  343.8 1.3 fusion.3
  (22 shorter events, 0.1 us)
Async XLA Ops:
  1.5 4.8 %collective-permute-start = (s32[2,1]{0,1:T(1,128)S(1)}, s32[2,1]{0,1:T(1,128)S(1)}, u32[]{:S(2)}, u32[]{:S(2)}) collective-permute-start(s32[2,1]{0,1:T(1,128)S(1)} %bitcast.85), channel_id=1, source_target_pairs={{0,1},{1,0},{2,3},{3,2},{4,5},{5,4},{6,7},{7,6},{8,9},{9,8},{10,11... | collective-permute-start | bytes 32 | tf_op jit(solution)/shard_map/ppermute | solution.py:1126
  321.8 5.1 %copy-start.5 = (bf16[8,64,768]{2,1,0:T(8,128)(2,1)S(1)}, bf16[8,64,768]{2,1,0:T(8,128)(2,1)}, u32[]{:S(2)}) copy-start(bf16[8,64,768]{2,1,0:T(8,128)(2,1)} %get-tuple-element.67) | copy-start | bytes 2359300
  329.7 8.1 %copy-start = (bf16[2,1,128,1024]{3,2,1,0:T(8,128)(2,1)S(1)}, bf16[2,1,128,1024]{3,2,1,0:T(8,128)(2,1)}, u32[]{:S(2)}) copy-start(bf16[2,1,128,1024]{3,2,1,0:T(8,128)(2,1)} %param.16) | copy-start | bytes 1572868
  329.7 8.1 %copy-start.2 = (bf16[2,128,1024]{2,1,0:T(8,128)(2,1)S(1)}, bf16[2,128,1024]{2,1,0:T(8,128)(2,1)}, u32[]{:S(2)}) copy-start(bf16[2,128,1024]{2,1,0:T(8,128)(2,1)} %get-tuple-element.63) | copy-start | bytes 1572868
  330.5 7.7 %copy-start.7 = (bf16[8,32,512]{2,1,0:T(8,128)(2,1)S(1)}, bf16[8,32,512]{2,1,0:T(8,128)(2,1)}, u32[]{:S(2)}) copy-start(bf16[8,32,512]{2,1,0:T(8,128)(2,1)} %get-tuple-element.66) | copy-start | bytes 786436
  331.1 9.4 %copy-start.1 = (f32[2,128,1024]{2,1,0:T(8,128)S(1)}, f32[2,128,1024]{2,1,0:T(8,128)}, u32[]{:S(2)}) copy-start(f32[2,128,1024]{2,1,0:T(8,128)} %get-tuple-element.41.refs_1_) | copy-start | bytes 3145732
  332.4 7.1 %copy-start.6 = (bf16[8,192,128]{2,1,0:T(8,128)(2,1)S(1)}, bf16[8,192,128]{2,1,0:T(8,128)(2,1)}, u32[]{:S(2)}) copy-start(bf16[8,192,128]{2,1,0:T(8,128)(2,1)} %get-tuple-element.68) | copy-start | bytes 1179652
  332.4 8.1 %copy-start.4 = (f32[2,128,1024]{2,1,0:T(8,128)S(1)}, f32[2,128,1024]{2,1,0:T(8,128)}, u32[]{:S(2)}) copy-start(f32[2,128,1024]{2,1,0:T(8,128)} %get-tuple-element.61) | copy-start | bytes 3145732
  336.1 7.7 %copy-start.3 = (f32[2,128,1024]{2,1,0:T(8,128)S(1)}, f32[2,128,1024]{2,1,0:T(8,128)}, u32[]{:S(2)}) copy-start(f32[2,128,1024]{2,1,0:T(8,128)} %get-tuple-element.62) | copy-start | bytes 3145732

commit v4 on v3

--- a/solution.py
+++ b/solution.py
@@ -24,7 +24,11 @@
 def moved(me, shift):
     to = dict(me)
     for axis, step in shift.items():
-        to[axis] = (me[axis] + (step % SIZES[axis])) % SIZES[axis]
+        if axis == "y":
+            y = (me["yh"] * 2 + me["yl"] + step % 4) % 4
+            to["yh"], to["yl"] = y // 2, y % 2
+        else:
+            to[axis] = (me[axis] + (step % SIZES[axis])) % SIZES[axis]
     return to
 
 
@@ -85,7 +89,7 @@
     if a or b or d
 ]
 HEAD_SHIFTS = [{"z": a, "core": b} for a in range(4) for b in range(2) if a or b]
-Y_SHIFTS = [{"yl": 1}, {"yh": 1}, {"yl": 1, "yh": 1}]
+RING_Y = [{"y": 1}, {"y": 3}]
 RING_Z = [{"z": 1}, {"z": 3}, {"core": 1}, {"yl": 1, "core": 1}]
 RING_X = [{"x": 1}, {"x": 3}, {"core": 1}]
 
@@ -240,7 +244,7 @@
         return block(moved(me, {axis: step}), *part)
 
     def cut(part):
-        return src.at[..., pl.ds(*part), :]
+        return at(0, part) if src is None else src.at[..., pl.ds(*part), :]
 
     def send(step, part, shift):
         here = cut(part) if step == 0 else at(step, part)
@@ -251,13 +255,17 @@
     l1 = send(0, high, left)
     r1 = send(0, high, right)
     l0 = send(0, low, left)
-    own = send(0, (0, rows), other)
+    own = pair and send(0, (0, rows), other)
     yield
     r0.wait_recv()
     fr = send(-1, low, right)
     l1.wait_recv()
     fl = send(1, high, left)
     yield
+    if not pair:
+        for copy in (r1, l0, fr, fl):
+            copy.wait_recv()
+        return
     r1.wait_recv()
     cr = send(-1, (0, rows), other)
     l0.wait_recv()
@@ -284,7 +292,7 @@
     lax.fori_loop(0, rows // step, one, 0)
 
 
-def reduce_ring(net, axis, part, index, total, rc, s, rh, r):
+def reduce_ring(net, axis, part, index, total, rc, rh, r, extra=()):
     me = net.me
     low, high = pl.ds(0, 64), pl.ds(64, 64)
     right, left, other = {axis: 1}, {axis: -1}, {"core": 1}
@@ -292,75 +300,131 @@
     def at(step, core, rows=pl.ds(0, 128)):
         return part.at[index(moved(me, {axis: step, "core": core})), rows]
 
+    def add(step, rows, n, *more):
+        add_rows(rc.at[step, rows], [at(step, 0, rows), rc.at[step, rows], *more], n)
+
     cc = {}
     for step in (2, 1, 3, 0):
         cc[step] = net.send(at(step, 1), rc.at[step], **other)
     yield
     cc[2].wait_recv()
-    add_rows(s.at[2], [at(2, 0), rc.at[2]], 128)
-    h_r = net.send(s.at[2, low], rh.at[0], **right)
-    h_l = net.send(s.at[2, high], rh.at[1], **left)
+    add(2, low, 64)
+    h_r = net.send(rc.at[2, low], rh.at[0], **right)
+    add(2, high, 64)
+    h_l = net.send(rc.at[2, high], rh.at[1], **left)
     cc[1].wait_recv()
-    add_rows(s.at[1, high], [at(1, 0, high), rc.at[1, high]], 64)
-    r_high = net.send(s.at[1, high], r.at[0, high], **right)
+    add(1, high, 64)
+    r_high = net.send(rc.at[1, high], r.at[0, high], **right)
     cc[3].wait_recv()
-    add_rows(s.at[3, low], [at(3, 0, low), rc.at[3, low]], 64)
-    l_low = net.send(s.at[3, low], r.at[1, low], **left)
+    add(3, low, 64)
+    l_low = net.send(rc.at[3, low], r.at[1, low], **left)
     yield
     h_r.wait_recv()
-    add_rows(s.at[1, low], [at(1, 0, low), rc.at[1, low], rh.at[0]], 64)
-    r_low = net.send(s.at[1, low], r.at[0, low], **right)
+    add(1, low, 64, rh.at[0])
+    r_low = net.send(rc.at[1, low], r.at[0, low], **right)
     h_l.wait_recv()
-    add_rows(s.at[3, high], [at(3, 0, high), rc.at[3, high], rh.at[1]], 64)
-    l_high = net.send(s.at[3, high], r.at[1, high], **left)
+    add(3, high, 64, rh.at[1])
+    l_high = net.send(rc.at[3, high], r.at[1, high], **left)
     yield
     for copy in (cc[0], r_high, l_low, r_low, l_high):
         copy.wait_recv()
+    add_rows(total, [at(0, 0), rc.at[0], r.at[0], r.at[1], *extra], 128)
+
+
+def reduce_ring_tiles(net, axis, part, index, total, rc, rh, r):
+    me = net.me
+    low, high = pl.ds(0, 64), pl.ds(64, 64)
+    right, left, other = {axis: 1}, {axis: -1}, {"core": 1}
+
+    def at(step, core, rows=pl.ds(0, 128)):
+        return part.at[index(moved(me, {axis: step, "core": core})), rows]
+
+    def add(step, rows, n, *more):
+        add_rows(rc.at[step, rows], [at(step, 0, rows), rc.at[step, rows], *more], n)
+
+    def over(step):
+        return net.send(at(step, 1), rc.at[step], **other)
+
+    c2 = over(2)
+    yield
+    c1 = over(1)
+    c2.wait_recv()
+    add(2, low, 64)
+    h_r = net.send(rc.at[2, low], rh.at[0], **right)
+    add(2, high, 64)
+    h_l = net.send(rc.at[2, high], rh.at[1], **left)
+    yield
+    c3 = over(3)
+    c1.wait_recv()
+    add(1, high, 64)
+    r_high = net.send(rc.at[1, high], r.at[0, high], **right)
+    yield
+    c0 = over(0)
+    c3.wait_recv()
+    add(3, low, 64)
+    l_low = net.send(rc.at[3, low], r.at[1, low], **left)
+    h_r.wait_recv()
+    add(1, low, 64, rh.at[0])
+    r_low = net.send(rc.at[1, low], r.at[0, low], **right)
+    h_l.wait_recv()
+    add(3, high, 64, rh.at[1])
+    l_high = net.send(rc.at[3, high], r.at[1, high], **left)
+    yield
+    for copy in (c0, r_high, l_low, r_low, l_high):
+        copy.wait_recv()
     add_rows(total, [at(0, 0), rc.at[0], r.at[0], r.at[1]], 128)
+
+
+TILES = (2, 1, 3, 0)
 
 
 def reduce_ring_scratch(width):
     return [
-        pltpu.VMEM((4, 128, width), BF),
         pltpu.VMEM((4, 128, width), BF),
         pltpu.VMEM((2, 64, width), BF),
         pltpu.VMEM((2, 128, width), BF),
     ]
 
 
+def by_x_then_y(net, pick, out):
+    me = net.me
+    mine = out.at[me["yh"], tp_of(me), me["yl"]]
+    kept = net.local(pick(me), mine)
+    copies = [net.send(pick(moved(me, shift)), mine, **shift) for shift in TP_SHIFTS]
+    yield
+    for copy in copies:
+        copy.wait_recv()
+    net.settle(kept)
+
+    def block(place, lo, n):
+        return out.at[place["yh"], pl.ds(lo, n), place["yl"]]
+
+    yield from gather_ring(net, "y", None, block, 8, None)
+
+
 def gather_heads_weights(net, wq, wk, wv, small, stage, out, small_out):
     me = net.me
     mine = fsdp_of(me)
     staged = []
+    rows = pl.ds(pl.multiple_of(me["yl"] * 32, 32), 32)
     for core in range(2):
         h = me["z"] * 2 + core
         place = stage.at[core]
-        for src, dst in (
-            (wq.at[:, pl.ds(pl.multiple_of(h * 256, 256), 256)], place.at[:, pl.ds(0, 256)]),
-            (wk.at[:, pl.ds(pl.multiple_of(h * 128, 128), 128)], place.at[:, pl.ds(256, 128)]),
-            (wv.at[:, pl.ds(pl.multiple_of(h * 128, 128), 128)], place.at[:, pl.ds(384, 128)]),
-        ):
-            staged.append(net.local(src, dst))
+        for src, n, lane in ((wq, 256, 0), (wk, 128, 256), (wv, 128, 384)):
+            columns = src.at[rows, pl.ds(pl.multiple_of(h * n, n), n)]
+            staged.append(net.local(columns, place.at[:, pl.ds(lane, n)]))
     yield
     for copy in staged:
         net.settle(copy)
-    kept = [
-        net.local(stage.at[me["core"]], out.at[mine]),
-        net.local(small, small_out.at[mine]),
-    ]
-    copies = [
-        net.send(src, dst, **shift)
-        for shift in WEIGHT_PLANE
-        for src, dst in (
-            (stage.at[moved(me, shift)["core"]], out.at[mine]),
-            (small, small_out.at[mine]),
-        )
-    ]
-    yield
+    task = by_x_then_y(net, lambda place: stage.at[place["core"]], out)
+    next(task)
+    kept = net.local(small, small_out.at[mine])
+    copies = [net.send(small, small_out.at[mine], **shift) for shift in WEIGHT_PLANE]
+    yield
+    yield from task
     for copy in copies:
         copy.wait_recv()
-    for copy in kept:
-        net.settle(copy)
+    net.settle(kept)
 
 
 def gather_out_weights(net, src, mid, out):
@@ -402,20 +466,15 @@
 
 def gather_ff_weights(net, down, stage, out, down_out):
     me = net.me
-    mine = fsdp_of(me)
-    kept = [
-        net.local(stage.at[tp_of(me)], out.at[mine]),
-        net.local(down, down_out.at[me["yh"]]),
-    ]
-    copies = [net.send(down, down_out.at[me["yh"]], yh=1, yl=1)]
-    copies += [
-        net.send(stage.at[tp_of(moved(me, shift))], out.at[mine], **shift) for shift in WEIGHT_PLANE
-    ]
-    yield
-    for copy in copies:
-        copy.wait_recv()
-    for copy in kept:
-        net.settle(copy)
+    rows = pl.ds(pl.multiple_of(me["yl"] * 32, 32), 32)
+    task = by_x_then_y(net, lambda place: stage.at[tp_of(place), rows], out)
+    next(task)
+    kept = net.local(down, down_out.at[me["yh"]])
+    copy = net.send(down, down_out.at[me["yh"]], yh=1, yl=1)
+    yield
+    yield from task
+    copy.wait_recv()
+    net.settle(kept)
 
 
 def chunk_of(place):
@@ -433,62 +492,57 @@
     net.settle(kept)
 
 
-def reduce_ff(net, g, d, rhg, rhd, sg, sd, rg, rd, tg, td, yg, yd, gsum, dsum):
+def reduce_ff(net, g, d, rhg, rhd, rg, rd, tg, td, zg, zd, gsum, dsum):
     me = net.me
-    z = [(me["z"] + k) % 4 for k in range(4)]
-    ring = ({"z": 1}, {"z": -1})
-    half = [
-        [
-            net.send(g.at[h, z[2]], rhg.at[h], **ring[h]),
-            net.send(d.at[z[2], h], rhd.at[h], **ring[h]),
-        ]
-        for h in range(2)
-    ]
-    near = [
-        net.send(g.at[1, z[1]], rg.at[0, 1], **ring[0]),
-        net.send(d.at[z[1], 1], rd.at[0, 1], **ring[0]),
-        net.send(g.at[0, z[3]], rg.at[1, 0], **ring[1]),
-        net.send(d.at[z[3], 0], rd.at[1, 0], **ring[1]),
-    ]
-    yield
-    for h, to in ((0, z[1]), (1, z[3])):
+    ring = ({"y": 1}, {"y": -1})
+    some = [pl.ds(0, 2), pl.ds(2, 2)]
+
+    def terms(step, h):
+        to = moved(me, {"y": step})
+        return g.at[to["yh"], some[h], to["yl"]], d.at[to["yh"], to["yl"], some[h]]
+
+    def send(step, h, dst_g, dst_d, to):
+        src_g, src_d = terms(step, h)
+        return [net.send(src_g, dst_g, **to), net.send(src_d, dst_d, **to)]
+
+    half = [send(2, h, rhg.at[h], rhd.at[h], ring[h]) for h in range(2)]
+    near = send(1, 1, rg.at[0, 1], rd.at[0, 1], ring[0])
+    near += send(-1, 0, rg.at[1, 0], rd.at[1, 0], ring[1])
+    yield
+    for h, step in ((0, 1), (1, -1)):
         for copy in half[h]:
             copy.wait_recv()
-        add_rows(sg.at[h], [g.at[h, to], rhg.at[h]], 128)
-        add_rows(sd.at[h], [d.at[to, h], rhd.at[h]], 192)
-        near.append(net.send(sg.at[h], rg.at[h, h], **ring[h]))
-        near.append(net.send(sd.at[h], rd.at[h, h], **ring[h]))
+        own_g, own_d = terms(step, h)
+        for k in range(2):
+            add_rows(rhg.at[h, k], [own_g.at[k], rhg.at[h, k]], 64)
+            add_rows(rhd.at[h, k], [own_d.at[k], rhd.at[h, k]], 192)
+        near.append(net.send(rhg.at[h], rg.at[h, h], **ring[h]))
+        near.append(net.send(rhd.at[h], rd.at[h, h], **ring[h]))
     yield
     for copy in near:
         copy.wait_recv()
     for h in range(2):
-        add_rows(tg.at[h], [g.at[h, z[0]], rg.at[0, h], rg.at[1, h]], 128)
-        for l in range(2):
-            at = pl.ds(128 * l, 128)
-            terms = [d.at[z[0], h, :, at], rd.at[0, h, :, at], rd.at[1, h, :, at]]
-            add_rows(td.at[h, l], terms, 192)
+        own_g, own_d = terms(0, h)
+        for k in range(2):
+            add_rows(tg.at[2 * h + k], [own_g.at[k], rg.at[0, h, k], rg.at[1, h, k]], 64)
+            add_rows(td.at[2 * h + k], [own_d.at[k], rd.at[0, h, k], rd.at[1, h, k]], 192)
     copies = []
-    for k, shift in enumerate(Y_SHIFTS):
-        to = moved(me, shift)
-        rows = pl.ds(pl.multiple_of(to["yl"] * 64, 64), 64)
-        copies.append(net.send(tg.at[to["yh"], rows], yg.at[k], **shift))
-        copies.append(net.send(td.at[to["yh"], to["yl"]], yd.at[k], **shift))
+    for k in range(3):
+        to = moved(me, {"z": k + 1})
+        copies.append(net.send(tg.at[to["z"]], zg.at[k], z=k + 1))
+        copies.append(net.send(td.at[to["z"]], zd.at[k], z=k + 1))
     yield
     for copy in copies:
         copy.wait_recv()
-    rows = pl.ds(pl.multiple_of(me["yl"] * 64, 64), 64)
-    add_rows(gsum, [tg.at[me["yh"], rows]] + [yg.at[k] for k in range(3)], 64)
-    add_rows(dsum, [td.at[me["yh"], me["yl"]]] + [yd.at[k] for k in range(3)], 192)
+    add_rows(gsum, [tg.at[me["z"]]] + [zg.at[k] for k in range(3)], 64)
+    add_rows(dsum, [td.at[me["z"]]] + [zd.at[k] for k in range(3)], 192)
 
 
 def reduce_ff_scratch():
-    shapes = [(128, 768), (192, 256)]
-    out = [pltpu.VMEM((2,) + s, BF) for s in shapes]
-    out += [pltpu.VMEM((2,) + s, BF) for s in shapes]
-    out += [pltpu.VMEM((2, 2) + s, BF) for s in shapes]
-    out += [pltpu.VMEM((2, 128, 768), BF), pltpu.VMEM((2, 2, 192, 128), BF)]
-    out += [pltpu.VMEM((3, 64, 768), BF), pltpu.VMEM((3, 192, 128), BF)]
-    out += [pltpu.VMEM((64, 768), BF), pltpu.VMEM((192, 128), BF)]
+    shapes = [(64, 768), (192, 128)]
+    out = []
+    for lead in ((2, 2), (2, 2, 2), (4,), (3,), ()):
+        out += [pltpu.VMEM(lead + s, BF) for s in shapes]
     return out
 
 
@@ -563,7 +617,7 @@
         x = self.xs[pl.ds(i * 2, 2)].reshape(256, 1024).astype(F32)
         low = (x * norm_scale(x) * self.gains[0:1, :]).astype(BF)
         self.xn[rows, :] = low
-        y = forward_dot(low, self.wqkv[:, pl.ds(0, 64), :].reshape(1024, 512))
+        y = forward_dot(low, self.wqkv[...].reshape(1024, 512))
         self.raw[rows, :] = y[:, :384]
         c, s = self.cos[rows, :], self.sin[rows, :]
         for head in range(3):
@@ -598,16 +652,13 @@
         self.part[pl.ds(i * 2, 2)] = y.reshape(2, 128, 1024)
         return carry
 
-    def pieces(self):
-        return (
-            [functools.partial(half_loop, self.project, p, 2, 4) for p in range(2)]
-            + [
-                functools.partial(half_loop, functools.partial(self.attend, head), p, 2, 4)
-                for head in range(2)
-                for p in range(2)
-            ]
-            + [functools.partial(half_loop, self.project_out, 0, 1, 4)]
-        )
+    def projection(self):
+        half_loop(self.project, 0, 1, 4)
+
+    def tile(self, i):
+        self.attend(0, i, 0)
+        self.attend(1, i, 0)
+        self.project_out(i, 0)
 
 
 def sequence_block(out):
@@ -642,19 +693,24 @@
     cots_in = gather_ring(net, "x", cot, cot_block, 128)
     own_cot = net.local(cot, cots.at[:, tp_of(me)])
     next(heads)
+    pack_columns(wg, gu_stage, 0)
+    pack_columns(wu, gu_stage, 384)
+    next(feed)
     swaps[0].wait()
     next(gather[0])
+    next(heads)
     next(outs)
-    pack_columns(wg, gu_stage, 0)
-    pack_columns(wu, gu_stage, 384)
+    next(cots_in)
     next(gather[0])
     swaps[1].wait()
     next(gather[1])
+    next(heads)
     next(gather[0])
     drain(gather[0])
     drain(heads)
+    next(outs)
+    next(feed)
     next(cots_in)
-    next(outs)
     pairs = [smalls[2 * i].astype(F32) + smalls[2 * i + 1].astype(F32) for i in range(8)]
     both = sum(pairs[1:], pairs[0])
     gains[...] = jnp.zeros_like(gains)
@@ -663,9 +719,7 @@
     gains[2:3, : 2 * HEAD] = jnp.concatenate([both[2:3], both[3:4]], axis=1)
     tables = (cos, sin, lk, lq, sq)
     saved = (xn, raw, q, k, v, mixt, rl)
-    work = [
-        Front(m, gains, wqkv, wo, xs, tables, saved, part, mixed, vt).pieces() for m in range(2)
-    ]
+    work = [Front(m, gains, wqkv, wo, xs, tables, saved, part, mixed, vt) for m in range(2)]
 
     def save(m):
         for src, dst in zip(saved, (xn_out, raw_out, q_out, k_out, v_out, mixt_out, rl_out)):
@@ -676,40 +730,39 @@
         attended[m] = x
         normed[m] = (x * norm_scale(x) * gains[1:2, :]).astype(BF)
 
-    for at, piece in enumerate(work[0][:-1]):
-        piece()
+    def reduce(m):
+        buf = bufs[3 * m : 3 * m + 3]
+        yield from reduce_ring_tiles(net, "z", part.at[m], head_of, outbox.at[m], *buf)
+        swap = net.swap(outbox.at[m], inbox.at[m])
+        yield
+        swap.wait()
+        settle(m)
+
+    reduces = [reduce(m) for m in range(2)]
+    work[0].projection()
+    step(gather[1])
+    drain(outs)
+    for k in TILES:
+        work[0].tile((me["z"] + k) % 4)
+        next(reduces[0])
         step(gather[1])
-        if at == 3:
-            drain(outs)
+        if k == 3:
+            step(feed)
+    step(cots_in)
     drain(gather[1])
-    work[0][-1]()
-    reduce0 = reduce_ring(net, "z", part.at[0], head_of, outbox.at[0], *bufs[:4])
-    next(reduce0)
-    step(cots_in)
-    next(feed)
     save(0)
-    for at, piece in enumerate(work[1]):
-        piece()
-        if at in (0, 2, 4):
-            step(reduce0)
-        if at == 5:
+    work[1].projection()
+    step(reduces[0])
+    for at, k in enumerate(TILES):
+        work[1].tile((me["z"] + k) % 4)
+        next(reduces[1])
+        if at == 1:
+            drain(reduces[0])
             step(cots_in)
-    drain(reduce0)
-    back0 = net.swap(outbox.at[0], inbox.at[0])
-    reduce1 = reduce_ring(net, "z", part.at[1], head_of, outbox.at[1], *bufs[4:])
-    next(reduce1)
     save(1)
-    next(reduce1)
-    step(cots_in)
-    next(reduce1)
-    back0.wait()
-    settle(0)
-    drain(reduce1)
-    back1 = net.swap(outbox.at[1], inbox.at[1])
+    drain(reduces[1])
     drain(cots_in)
     drain(feed)
-    back1.wait()
-    settle(1)
 
 
 class Feed:
@@ -718,7 +771,7 @@
         self.nm, self.ct, self.hid, self.ggu = nm.at[m], ct.at[m], hid.at[m], ggu.at[m]
         self.out, self.mid, self.dg, self.dd = out.at[m], mid.at[m], dg, dd
 
-    def tile(self, i, carry):
+    def tile(self, i):
         rows = pl.ds(pl.multiple_of(i * 256, 256), 256)
         blocks = pl.ds(i * 2, 2)
         wgu = self.wgu[...].reshape(1024, 768)
@@ -738,10 +791,6 @@
             against_cols(self.ggu[rows, :], wgu).astype(BF).reshape(2, 128, 1024)
         )
         self.out[blocks] = forward_dot(hidden, wd).astype(BF).reshape(2, 128, 1024)
-        return carry
-
-    def pieces(self):
-        return [functools.partial(half_loop, self.tile, p, 4, 4) for p in range(4)]
 
     def in_weights(self):
         def some(i, carry):
@@ -796,32 +845,31 @@
         g_attended[m] = y
         g_attn[m] = y.astype(BF)
 
-    for piece in work[0].pieces():
-        piece()
+    def reduce(m):
+        buf = bufs[3 * m : 3 * m + 3]
+        yield from reduce_ring_tiles(net, "x", mid_part.at[m], tp_of, total.at[m], *buf)
+        settle(m)
+
+    reduces = [reduce(m) for m in range(2)]
+    for k in TILES:
+        work[0].tile((me["x"] + k) % 4)
+        next(reduces[0])
         step(gather[1])
+    net.local(out_part.at[0], out_part_out.at[0])
     drain(gather[1])
-    net.local(out_part.at[0], out_part_out.at[0])
-    reduce0 = reduce_ring(net, "x", mid_part.at[0], tp_of, total.at[0], *bufs[:4])
-    next(reduce0)
-    for at, piece in enumerate(work[1].pieces()):
-        piece()
-        step(reduce0)
-    drain(reduce0)
+    for at, k in enumerate(TILES):
+        work[1].tile((me["x"] + k) % 4)
+        next(reduces[1])
+        if at == 1:
+            drain(reduces[0])
     net.local(out_part.at[1], out_part_out.at[1])
-    reduce1 = reduce_ring(net, "x", mid_part.at[1], tp_of, total.at[1], *bufs[4:])
-    next(reduce1)
-    settle(0)
-    work[0].in_weights()
-    next(reduce1)
-    work[0].down_weights()
-    next(reduce1)
-    work[1].in_weights()
-    drain(reduce1)
-    settle(1)
-    work[1].down_weights()
-    dg_low[...] = dg[...].astype(BF).reshape(2, 4, 128, 768)
-    for j in range(4):
-        dd_low[j] = dd[:, 256 * j : 256 * j + 256].astype(BF).reshape(2, 192, 256)
+    for one in work:
+        one.in_weights()
+        one.down_weights()
+    drain(reduces[1])
+    dg_low[...] = dg[...].astype(BF).reshape(2, 4, 2, 64, 768)
+    for c in range(8):
+        dd_low[:, c % 2, c // 2] = dd[:, 128 * c : 128 * c + 128].astype(BF).reshape(2, 192, 128)
 
 
 class Back:
@@ -874,7 +922,7 @@
             d = r * n - u * (r * r * r) * jnp.mean(n * u, axis=-1, keepdims=True)
             self.graw[rows, at] = d.astype(BF)
         self.graw[rows, 384:] = self.dv[rows, :].astype(BF)
-        y = against_cols(self.graw[rows, :], self.wqkv[:, pl.ds(0, 64), :].reshape(1024, 512))
+        y = against_cols(self.graw[rows, :], self.wqkv[...].reshape(1024, 512))
         self.part[pl.ds(i * 2, 2)] = y.astype(BF).reshape(2, 128, 1024)
         return carry
 
@@ -919,7 +967,7 @@
     gain_own, gain_first, gain_middle, gain_second, *bufs,
 ):
     me = net.me
-    ff, bufs = bufs[:12], bufs[12:]
+    ff, bufs = bufs[:10], bufs[10:]
     swaps = [net.swap(g_own.at[m], g.at[m, ctx_of(me)]) for m in range(2)]
     fetched = [net.local(out_part_in.at[0], out_part.at[0])]
     saved = (xn, raw, q, k, v, mixt, rl)
@@ -934,7 +982,7 @@
         gather_ring(net, "z", g.at[m, head_of(me)], sequence_block(g.at[m]), 128) for m in range(2)
     ]
     outs = [
-        reduce_ring(net, "x", out_part.at[m], tp_of, out_sum.at[m], *bufs[4 * m + 8 : 4 * m + 12])
+        reduce_ring(net, "x", out_part.at[m], tp_of, out_sum.at[m], *bufs[3 * m + 6 : 3 * m + 9])
         for m in range(2)
     ]
     gsum, dsum = ff[-2:]
@@ -986,48 +1034,49 @@
         if at in (1, 3, 5):
             step(outs[0])
     drain(gather[1])
-    reduce0 = reduce_ring(net, "z", part.at[0], head_of, outbox.at[0], *bufs[:4])
-    next(reduce0)
+    def reduce(m):
+        yield from reduce_ring(net, "z", part.at[m], head_of, outbox.at[m], *bufs[3 * m : 3 * m + 3])
+        swap = net.swap(outbox.at[m], in_sum.at[m])
+        yield
+        swap.wait()
+
+    reduces = [reduce(m) for m in range(2)]
+    next(reduces[0])
     drain(outs[0])
     next(outs[1])
-    step(feed)
     for at, piece in enumerate(work[1].pieces()):
         piece()
-        if at in (1, 2, 3):
-            step(reduce0)
+        if at in (1, 3, 5):
+            step(reduces[0])
         if at in (2, 4, 6):
             step(outs[1])
-        if at in (3, 4, 6):
+        if at in (2, 4, 6):
             step(feed)
-    drain(reduce0)
-    back0 = net.swap(outbox.at[0], in_sum.at[0])
-    reduce1 = reduce_ring(net, "z", part.at[1], head_of, outbox.at[1], *bufs[4:8])
-    next(reduce1)
-    work[0].out_weights()
-    next(reduce1)
-    work[1].out_weights()
+    next(reduces[1])
     work[0].head_weights()
-    next(reduce1)
+    step(reduces[1])
+    step(reduces[0])
     work[1].head_weights()
     qkv_low[...] = dwqkv[...].astype(BF).reshape(16, 64, 512)
+    scattered = [
+        scatter_samples(net, lambda place: qkv_low.at[chunk_of(place)], qkv_in),
+        scatter_samples(net, lambda place: wo_low.at[place["yl"], chip_of(place)], wo_in),
+    ]
+    next(scattered[0])
+    step(reduces[1])
+    step(feed)
+    work[0].out_weights()
+    step(reduces[1])
+    work[1].out_weights()
     low = dwo[...].astype(BF)
     for half in range(2):
         wo_low[:, :, half * 16 : half * 16 + 16, :] = low[:, half * 512 : half * 512 + 512].reshape(
             2, 8, 16, 512
         )
-    scattered = [
-        scatter_samples(net, lambda place: qkv_low.at[chunk_of(place)], qkv_in),
-        scatter_samples(net, lambda place: wo_low.at[place["yl"], chip_of(place)], wo_in),
-    ]
-    for task in scattered:
-        next(task)
-    step(feed)
-    drain(reduce1)
-    back1 = net.swap(outbox.at[1], in_sum.at[1])
+    next(scattered[1])
+    drain(*reduces)
     drain(outs[1])
     step(feed)
-    back0.wait()
-    back1.wait()
     row = jnp.zeros((1, 1024), F32)
     for m in range(2):
         x = tok[m].astype(F32)
@@ -1144,22 +1193,22 @@
     sequence = vm((2, 8, 128, width), BF)
     attended, normed, gain_rows, wqkv, wo, cots, wgu, wds, _, *saved = comm_call(
         front_body,
-        RING_Z + RING_X + WEIGHT_PLANE,
+        RING_Z + RING_X + RING_Y + WEIGHT_PLANE,
         [
             ((2, 128, width), F32),
             ((2, 128, width), BF),
             ((8, width), F32),
-            ((16, 64, 512), BF),
+            ((2, 8, 2, 32, 512), BF),
             ((2, 8, 16, width), BF),
             ((2, 8, 128, width), BF),
-            ((16, 64, 768), BF),
+            ((2, 8, 2, 32, 768), BF),
             ((2, 192, width), BF),
             ((8, 16, width), BF),
         ]
         + saves,
         [vm(shape, kind) for shape, kind in saves]
         + [sequence, sequence, vm((1024, 256), BF), vm((HEAD, 1024), BF)]
-        + [vm((2, 64, 512), BF), vm((16, 16, HEAD), BF), vm((8, 64, 768), BF)]
+        + [vm((2, 32, 512), BF), vm((16, 16, HEAD), BF), vm((8, 64, 768), BF)]
         + [vm((2, 128, width), BF), vm((2, 128, width), BF)]
         + reduce_ring_scratch(width) * 2,
         0,
@@ -1178,8 +1227,8 @@
             ((2, 128, width), F32),
             ((2, 128, width), BF),
             ((8, width), F32),
-            ((2, 4, 128, 768), BF),
-            ((4, 2, 192, 256), BF),
+            ((2, 4, 2, 64, 768), BF),
+            ((2, 2, 4, 192, 128), BF),
             ((2, 8, 128, width), BF),
         ],
         [sequence, vm((2, 1024, 384), BF), vm((2, 1024, 768), BF), sequence, sequence]
@@ -1193,7 +1242,7 @@
     )(normed, attended, cotangent[:, 0], cots, wgu, wds, gain_rows)
     in_sum, out_sum, heads, outs, gu, down, gain_total = comm_call(
         back_body,
-        RING_Z + RING_X + [{"yl": 1}] + SAMPLE_SHIFTS + CHIP_SHIFTS + TP_SHIFTS + COPY_SHIFTS,
+        RING_Z + RING_X + RING_Y + [{"yl": 1}] + SAMPLE_SHIFTS + CHIP_SHIFTS + TP_SHIFTS + COPY_SHIFTS,
         [
             ((2, 128, width), BF),
             ((2, 128, width), F32),

time: 352 us -> 313 us (0.89)
  Pallas kernels: 308 us -> 270 us
    pallas_call x2, Pallas kernels: 249 us -> 220 us  [the longest x1 132 us: per_device(): comm_call(back_body, RING_Z + RING_X + RING_Y + [{'yl': 1}] + SAMPLE_SHIF...]
    pallas_call x1, Pallas kernels: 58.2 us -> 50.6 us  [per_device(): comm_call(feed_body, RING_X, [((2, 128, width), F32), ((2, 128, width), B...]
where the time goes in v4:
time: 313 us; the launch traced here: 308 us
  Pallas kernels  270 us (86%)
  local copies, waits for them, and re-layouts  20.7 us (7%)
  other arithmetic  14.4 us (5%)
    pallas_call x1, Pallas kernels, per_device(): comm_call(back_body, RING_Z + RING_X + RING_Y + [{'yl': 1}] + SAMPLE_SHIF...  132 us
    pallas_call x1, Pallas kernels, per_device(): comm_call(front_body, RING_Z + RING_X + RING_Y + WEIGHT_PLANE, [((2, 128,...  88 us
    pallas_call x1, Pallas kernels, per_device(): comm_call(feed_body, RING_X, [((2, 128, width), F32), ((2, 128, width), B...  50.6 us
  transfers between devices with their start and end apart: 1, of which 0 were waited for; matrix products, arithmetic and copies ran while one was open for 1% of the time, Pallas kernels for 0%

profile of v4, /device:TPU:1, one launch (start us, length us, event | category | flops | bytes accessed | tf_op | source)
XLA Modules:
  0.0 308.0 jit_solution(15241216005779477254)
XLA Ops:
  0.6 0.8 fusion.10
  1.5 1.5 collective-permute-start
  3.0 0.7 broadcast_multiply_fusion.1
  3.7 0.1 broadcast_in_dim.93
  3.7 0.1 mul.121
  3.8 0.1 mul.127
  3.9 0.7 broadcast_select_fusion
  4.7 0.1 select_n.143
  4.8 0.1 select_n.145
  4.9 0.7 broadcast_select_fusion.3
  5.6 0.7 concatenate.9
  6.2 0.0 collective-permute-done
  6.3 0.7 compare_select_fusion
  6.9 0.1 fusion.7
  7.0 3.7 %fusion.6 = (f32[2,1024,64]{2,1,0:T(8,128)S(1)}, f32[2,1024,64]{2,1,0:T(8,128)S(1)}, f32[2,1024,64]{2,1,0:T(8,128)S(1)}) fusion(f32[64]{0:T(128)S(1)} %multiply_exponential_fusion, f32[2,1024]{1,0:T(2,128)S(1)} %get-tuple-element.99), kind=kLoop, calls=%fused_computation.21 | loop fusion | flops 262144 | bytes 1581312 | tf_op jit(solution)/shard_map/neg | solution.py:576
  10.7 1.9 pad_maximum_fusion
  12.7 1.3 broadcast_in_dim.99.refs_12_.refs_18_
  14.0 88.0 %shard_map.246 = (f32[2,128,1024]{2,1,0:T(8,128)}, bf16[2,128,1024]{2,1,0:T(8,128)(2,1)}, f32[8,1024]{1,0:T(8,128)}, bf16[2,8,2,32,512]{4,3,2,1,0:T(8,128)(2,1)}...) custom-call(bf16[2,128,1024]{2,1,0:T(8,128)(2,1)} %bitcast.69, ...), custom_call_target="tpu_custom_call" | custom-call | tf_op jit(solution)/shard_map/pallas_call | solution.py:1194
  102.0 50.6 %shard_map.247 = (f32[2,128,1024]{2,1,0:T(8,128)}, bf16[2,128,1024]{2,1,0:T(8,128)(2,1)}, f32[8,1024]{1,0:T(8,128)}, bf16[2,4,2,64,768]{4,3,2,1,0:T(8,128)(2,1)}...) custom-call(bf16[2,128,1024]{2,1,0:T(8,128)(2,1)} %get-tuple-element.42.refs_0_, ...), custom_call_target="tpu_custom_call" | custom-call | tf_op jit(solution)/shard_map/pallas_call | solution.py:1223
  152.6 131.8 %shard_map.248 = (bf16[2,128,1024]{2,1,0:T(8,128)(2,1)}, f32[2,128,1024]{2,1,0:T(8,128)}, bf16[8,64,512]{2,1,0:T(8,128)(2,1)}, bf16[8,32,512]{2,1,0:T(8,128)(2,1...) custom-call(bf16[2,128,1024]{2,1,0:T(8,128)(2,1)} %get-tuple-element.47.refs_0_, ...), custom_call_target="tpu_custom_call" | custom-call | tf_op jit(solution)/shard_map/pallas_call | solution.py:1243
  284.4 1.2 convert_element_type.54
  285.7 0.8 slice_bitcast_fusion
  286.5 0.8 slice_bitcast_fusion.1
  287.4 0.8 slice.30
  288.1 0.7 slice_bitcast_fusion.3
  288.8 0.8 fusion.14
  289.6 0.2 slice_convert_fusion
  289.8 0.8 reshape.359
  290.5 0.6 copy.37
  291.1 1.3 reshape.351
  292.4 0.7 reshape.360
  293.2 0.0 copy-start.7
  293.2 0.6 copy.38
  293.8 1.3 reshape.352
  295.1 2.0 copy.42
  297.1 1.7 copy.50
  298.8 1.8 copy.51
  300.5 0.0 copy-done
  300.5 0.3 fusion
  300.9 0.4 copy.36
  301.3 0.9 copy.46
  302.2 1.0 copy_bitcast_fusion
  303.2 0.9 fusion.5
  304.1 0.6 dynamic_slice.16
  304.7 0.6 dynamic_slice.21
  305.3 0.6 dynamic-slice_bitcast_fusion
  305.9 0.6 dynamic-slice_bitcast_fusion.1
  306.5 1.3 fusion.3
  (22 shorter events, 0.1 us)
Async XLA Ops:
  1.5 4.8 %collective-permute-start = (s32[2,1]{0,1:T(1,128)S(1)}, s32[2,1]{0,1:T(1,128)S(1)}, u32[]{:S(2)}, u32[]{:S(2)}) collective-permute-start(s32[2,1]{0,1:T(1,128)S(1)} %bitcast.85), channel_id=1, source_target_pairs={{0,1},{1,0},{2,3},{3,2},{4,5},{5,4},{6,7},{7,6},{8,9},{9,8},{10,11... | collective-permute-start | bytes 32 | tf_op jit(solution)/shard_map/ppermute | solution.py:1175
  284.4 5.1 %copy-start.5 = (bf16[8,64,768]{2,1,0:T(8,128)(2,1)S(1)}, bf16[8,64,768]{2,1,0:T(8,128)(2,1)}, u32[]{:S(2)}) copy-start(bf16[8,64,768]{2,1,0:T(8,128)(2,1)} %get-tuple-element.67) | copy-start | bytes 2359300
  292.4 8.1 %copy-start = (bf16[2,1,128,1024]{3,2,1,0:T(8,128)(2,1)S(1)}, bf16[2,1,128,1024]{3,2,1,0:T(8,128)(2,1)}, u32[]{:S(2)}) copy-start(bf16[2,1,128,1024]{3,2,1,0:T(8,128)(2,1)} %param.16) | copy-start | bytes 1572868
  292.4 8.1 %copy-start.2 = (bf16[2,128,1024]{2,1,0:T(8,128)(2,1)S(1)}, bf16[2,128,1024]{2,1,0:T(8,128)(2,1)}, u32[]{:S(2)}) copy-start(bf16[2,128,1024]{2,1,0:T(8,128)(2,1)} %get-tuple-element.63) | copy-start | bytes 1572868
  293.2 7.7 %copy-start.7 = (bf16[8,32,512]{2,1,0:T(8,128)(2,1)S(1)}, bf16[8,32,512]{2,1,0:T(8,128)(2,1)}, u32[]{:S(2)}) copy-start(bf16[8,32,512]{2,1,0:T(8,128)(2,1)} %get-tuple-element.66) | copy-start | bytes 786436
  293.8 9.4 %copy-start.1 = (f32[2,128,1024]{2,1,0:T(8,128)S(1)}, f32[2,128,1024]{2,1,0:T(8,128)}, u32[]{:S(2)}) copy-start(f32[2,128,1024]{2,1,0:T(8,128)} %get-tuple-element.41.refs_1_) | copy-start | bytes 3145732
  295.1 7.1 %copy-start.6 = (bf16[8,192,128]{2,1,0:T(8,128)(2,1)S(1)}, bf16[8,192,128]{2,1,0:T(8,128)(2,1)}, u32[]{:S(2)}) copy-start(bf16[8,192,128]{2,1,0:T(8,128)(2,1)} %get-tuple-element.68) | copy-start | bytes 1179652
  295.1 8.1 %copy-start.4 = (f32[2,128,1024]{2,1,0:T(8,128)S(1)}, f32[2,128,1024]{2,1,0:T(8,128)}, u32[]{:S(2)}) copy-start(f32[2,128,1024]{2,1,0:T(8,128)} %get-tuple-element.61) | copy-start | bytes 3145732
  298.8 7.7 %copy-start.3 = (f32[2,128,1024]{2,1,0:T(8,128)S(1)}, f32[2,128,1024]{2,1,0:T(8,128)}, u32[]{:S(2)}) copy-start(f32[2,128,1024]{2,1,0:T(8,128)} %get-tuple-element.62) | copy-start | bytes 3145732

commit v5 on v4

--- a/solution.py
+++ b/solution.py
@@ -106,12 +106,13 @@
         self.locals = 0
         self.pending = []
 
-    def enter(self, shifts):
+    def enter(self, shifts, between):
         barrier = pltpu.get_barrier_semaphore()
         for shift in shifts:
             pl.semaphore_signal(
                 barrier, inc=1, device_id=device_of(moved(self.me, shift)), device_id_type=MESH
             )
+        between()
         pl.semaphore_wait(barrier, len(shifts))
 
     def send(self, src, dst, **shift):
@@ -198,22 +199,25 @@
     return out
 
 
-def comm_call(body, shifts, outs, scratch, cid, in_vmem, out_vmem, n_remote, n_local=1):
+def comm_call(
+    body, shifts, outs, scratch, cid, in_vmem, out_vmem, n_remote, n_local=1, first=None
+):
     shifts = unique(shifts)
 
     def kernel(*refs):
         refs, sems = refs[:-3], refs[-3:]
         net = Net(*sems)
-        net.enter(shifts)
+        net.enter(shifts, functools.partial(first, *refs) if first else lambda: None)
         drain(*(body(net, *refs) or ()))
         net.finish()
 
     vm = pl.BlockSpec(memory_space=pltpu.VMEM)
     hb = pl.BlockSpec(memory_space=pl.ANY)
+    sm = pl.BlockSpec(memory_space=pltpu.SMEM)
     return pl.pallas_call(
         kernel,
         out_shape=[jax.ShapeDtypeStruct(s, d) for s, d in outs],
-        in_specs=[vm if v else hb for v in in_vmem],
+        in_specs=[sm if v is None else vm if v else hb for v in in_vmem],
         out_specs=[vm if v else hb for v in out_vmem],
         scratch_shapes=list(scratch)
         + [
@@ -222,7 +226,7 @@
             pltpu.SemaphoreType.DMA((n_local,)),
         ],
         compiler_params=pltpu.CompilerParams(
-            collective_id=cid, has_side_effects=True, vmem_limit_bytes=62 << 20
+            collective_id=cid, has_side_effects=True, vmem_limit_bytes=63 << 20
         ),
     )
 
@@ -557,6 +561,34 @@
     net.settle(kept)
 
 
+def unpack_columns(src, lane, out):
+    first = lax.broadcasted_iota(jnp.int32, (64, 128), 1) < 64
+
+    def tile(j, k):
+        return src[j, :, lane + 128 * k : lane + 128 * k + 128].astype(F32)
+
+    def half(t):
+        return pltpu.roll(t, 64, 1)
+
+    for pair in range(4):
+        j, n = 2 * pair, 2 * pair + 1
+        a = [tile(j, k) for k in range(3)]
+        b = [tile(n, k) for k in range(3)]
+        low = (
+            a[0],
+            jnp.where(first, a[1], half(b[0])),
+            jnp.where(first, half(b[0]), half(b[1])),
+        )
+        high = (
+            jnp.where(first, half(a[1]), half(a[2])),
+            jnp.where(first, half(a[2]), b[1]),
+            b[2],
+        )
+        for base, tiles in ((3 * pair, low), (12 + 3 * pair, high)):
+            for k, t in enumerate(tiles):
+                out[:, 128 * (base + k) : 128 * (base + k) + 128] = t.astype(BF)
+
+
 def sum_everywhere(net, own, first, middle, second, total):
     stages = ((own, first, TP_SHIFTS, middle), (middle, second, COPY_SHIFTS, total))
     for src, slots, shifts, dst in stages:
@@ -567,13 +599,9 @@
         dst[...] = src[...] + jnp.sum(slots[...], axis=0)
 
 
-def rope_tables(where_at):
-    frequency = jnp.exp(
-        jnp.arange(0, HEAD // 2, dtype=F32) * (-2.0 * math.log(1000000.0) / HEAD)
-    )
-    angles = where_at.astype(F32)[..., None] * frequency
-    cos, sin = jnp.cos(angles), jnp.sin(angles)
-    return jnp.concatenate([cos, cos], axis=-1), jnp.concatenate([-sin, sin], axis=-1)
+def rope_frequency():
+    half = jnp.exp(jnp.arange(0, HEAD // 2, dtype=F32) * (-2.0 * math.log(1000000.0) / HEAD))
+    return jnp.concatenate([half, half])[None]
 
 
 def across_rows(a, b):
@@ -661,6 +689,20 @@
         self.project_out(i, 0)
 
 
+def make_tables(m, table, first, frequency, cos, sin, lk):
+    row = lax.broadcasted_iota(jnp.int32, (64, HEAD), 0)
+    lane = lax.broadcasted_iota(jnp.int32, (64, HEAD), 1)
+    for b in range(16):
+        rows = slice(64 * b, 64 * b + 64)
+        at = table[m, b] * 64 + row
+        lk[m, rows, :] = at
+        later = jnp.where(at < 512 + first[m, 0], at + (384 - first[m, 0]), at - 128)
+        angle = jnp.where(at < 512, at, later).astype(F32) * frequency[...]
+        cos[m, rows, :] = jnp.cos(angle)
+        turn = jnp.sin(angle)
+        sin[m, rows, :] = jnp.where(lane < HEAD // 2, -turn, turn)
+
+
 def sequence_block(out):
     def block(place, lo, n):
         return out.at[head_of(place), pl.ds(lo, n)]
@@ -668,10 +710,16 @@
     return block
 
 
+def front_first(
+    tok, cot, small, wq, wk, wv, wo_in, wg, wu, wd, table, first, frequency, lq, sq, cos, sin, lk, *_
+):
+    make_tables(0, table, first, frequency, cos, sin, lk)
+
+
 def front_body(
     net,
-    tok, cot, small, wq, wk, wv, wo_in, wg, wu, wd, cos, sin, lk, lq, sq,
-    attended, normed, gains, wqkv, wo, cots, wgu, wds, mid,
+    tok, cot, small, wq, wk, wv, wo_in, wg, wu, wd, table, first, frequency, lq, sq,
+    cos, sin, lk, attended, normed, gains, wqkv, wo, cots, wgu, wds, mid,
     xn_out, raw_out, q_out, k_out, v_out, mixt_out, rl_out,
     xn, raw, q, k, v, mixt, rl,
     xs, part, mixed, vt, stage, smalls, gu_stage, outbox, inbox, *bufs,
@@ -693,14 +741,15 @@
     cots_in = gather_ring(net, "x", cot, cot_block, 128)
     own_cot = net.local(cot, cots.at[:, tp_of(me)])
     next(heads)
-    pack_columns(wg, gu_stage, 0)
-    pack_columns(wu, gu_stage, 384)
-    next(feed)
+    make_tables(1, table, first, frequency, cos, sin, lk)
     swaps[0].wait()
     next(gather[0])
     next(heads)
     next(outs)
     next(cots_in)
+    pack_columns(wg, gu_stage, 0)
+    pack_columns(wu, gu_stage, 384)
+    next(feed)
     next(gather[0])
     swaps[1].wait()
     next(gather[1])
@@ -960,10 +1009,12 @@
     net,
     g_own, tok, gain_sum, dg, dd, out_part_in, xn_in, raw_in, q_in, k_in, v_in, mixt_in, rl_in,
     wqkv, wo, gains, cos, sin, lk, lq, sq,
-    in_sum, out_sum, heads_out, outs_out, gu_out, down_out, gain_total,
+    in_sum, out_sum, gain_total,
+    gq, gk, gv, gwo, gate, up, gwd,
     xn, raw, q, k, v, mixt, rl,
     g, out_part, part, graw, dwqkv, dwo, kt, dk, dv, dq, outbox, sums,
-    qkv_low, wo_low, qkv_in, wo_in, qkv_sum, wo_sum, qkv_all, wo_all, wo_mid, gu_all,
+    qkv_low, wo_low, qkv_in, wo_in, qkv_sum, wo_sum, qkv_all, wo_all, wo_mid, gu_all, gu_out,
+    heads_out, outs_out, down_out,
     gain_own, gain_first, gain_middle, gain_second, *bufs,
 ):
     me = net.me
@@ -1110,9 +1161,21 @@
     drain(exchange(net, wo_all, wo_mid, CHIP_SHIFTS, chip_of))
     outs_back = net.swap(wo_mid, outs_out)
     drain(gain)
+    heads_back.wait()
+    for h in range(8):
+        gq[:, 256 * h : 256 * h + 256] = heads_out[h, :, :256]
+        gk[:, 128 * h : 128 * h + 128] = heads_out[h, :, 256:384]
+        gv[:, 128 * h : 128 * h + 128] = heads_out[h, :, 384:]
     drain(feed)
-    heads_back.wait()
+    for c in range(8):
+        gwd[:, 128 * c : 128 * c + 128] = down_out[c]
+    for k, dst in enumerate((gate, up)):
+        unpack_columns(gu_out, 384 * k, dst)
     outs_back.wait()
+    for i in range(8):
+        for half in range(2):
+            rows = slice(16 * half, 16 * half + 16)
+            gwo[16 * i : 16 * i + 16, 512 * half : 512 * half + 512] = outs_out[i, rows, :]
 
 
 def token_places(block_table, first, seq):
@@ -1123,9 +1186,7 @@
     )
     prompt = seq // 2
     segment = jnp.where(logical < prompt, 0, jnp.where(logical < prompt + first, 1, 2))
-    end = jnp.where(segment == 1, prompt - 1 + first, seq - 1)
-    position = jnp.where(segment == 0, logical, 895 - (end - logical))
-    return logical, segment, position
+    return logical, segment
 
 
 def per_device(
@@ -1174,11 +1235,10 @@
     count = jnp.sum((segment_ids[:, 0] == 1).astype(jnp.int32), axis=1, keepdims=True)
     other = lax.ppermute(count, "fsdp", [(i, i ^ 1) for i in range(16)])
     first = jnp.where(ctx % 2 == f % 2, count, other)
-    logical, seg, where_at = token_places(block_table, first, 1024)
+    logical, seg = token_places(block_table, first, 1024)
     start = jnp.where(seg == 2, 512 + first, 0)
-    lk = jnp.broadcast_to(logical[:, :, None], (mbs, 1024, HEAD))
     lq, sq = logical[:, None, :], start[:, None, :]
-    cos, sin = rope_tables(where_at)
+    frequency = rope_frequency()
 
     vm = pltpu.VMEM
     saves = [
@@ -1191,10 +1251,13 @@
         ((2, 2, 1, 1024), F32),
     ]
     sequence = vm((2, 8, 128, width), BF)
-    attended, normed, gain_rows, wqkv, wo, cots, wgu, wds, _, *saved = comm_call(
+    cos, sin, lk, attended, normed, gain_rows, wqkv, wo, cots, wgu, wds, _, *saved = comm_call(
         front_body,
         RING_Z + RING_X + RING_Y + WEIGHT_PLANE,
         [
+            ((2, 1024, HEAD), F32),
+            ((2, 1024, HEAD), F32),
+            ((2, 1024, HEAD), jnp.int32),
             ((2, 128, width), F32),
             ((2, 128, width), BF),
             ((8, width), F32),
@@ -1212,13 +1275,14 @@
         + [vm((2, 128, width), BF), vm((2, 128, width), BF)]
         + reduce_ring_scratch(width) * 2,
         0,
-        [True] + [False] * 6 + [True] * 2 + [False] + [True] * 5,
-        [True] * 5 + [False] * 11,
+        [True] + [False] * 6 + [True] * 2 + [False] + [None] * 2 + [True] * 3,
+        [True] * 8 + [False] * 11,
         160,
         64,
+        front_first,
     )(
         tok, cotangent[:, 0], small, w_query, key_projection, value_projection,
-        w_out.reshape(8, 16, width), w_gate, w_up, w_down, cos, sin, lk, lq, sq,
+        w_out.reshape(8, 16, width), w_gate, w_up, w_down, block_table, first, frequency, lq, sq,
     )
     g_attended, g_attn, gain_sum, dg, dd, out_part = comm_call(
         feed_body,
@@ -1240,17 +1304,20 @@
         64,
         8,
     )(normed, attended, cotangent[:, 0], cots, wgu, wds, gain_rows)
-    in_sum, out_sum, heads, outs, gu, down, gain_total = comm_call(
+    in_sum, out_sum, gain_total, *weights = comm_call(
         back_body,
         RING_Z + RING_X + RING_Y + [{"yl": 1}] + SAMPLE_SHIFTS + CHIP_SHIFTS + TP_SHIFTS + COPY_SHIFTS,
         [
             ((2, 128, width), BF),
             ((2, 128, width), F32),
-            ((8, 64, 512), BF),
-            ((8, 32, 512), BF),
-            ((8, 64, 768), BF),
-            ((8, 192, 128), BF),
             ((24, HEAD), F32),
+            ((64, 2048), BF),
+            ((64, 1024), BF),
+            ((64, 1024), BF),
+            ((128, width), BF),
+            ((64, 3072), BF),
+            ((64, 3072), BF),
+            ((192, width), BF),
         ],
         [vm(shape, kind) for shape, kind in saves]
         + [sequence, sequence, sequence, vm((2, 1024, 512), BF)]
@@ -1261,12 +1328,13 @@
         + [vm((16, 64, 512), BF), vm((16, 32, 512), BF)]
         + [vm((64, 512), BF), vm((32, 512), BF)]
         + [vm((8, 64, 512), BF), vm((8, 32, 512), BF), vm((8, 32, 512), BF), vm((8, 64, 768), BF)]
+        + [vm((8, 64, 768), BF), vm((8, 64, 512), BF), vm((8, 32, 512), BF), vm((8, 192, 128), BF)]
         + [vm((24, HEAD), F32), vm((7, 24, HEAD), F32), vm((24, HEAD), F32), vm((15, 24, HEAD), F32)]
         + reduce_ff_scratch()
         + reduce_ring_scratch(width) * 4,
         2,
         [True] * 5 + [False] * 8 + [True] * 8,
-        [True] * 2 + [False] * 4 + [True],
+        [True] * 10,
         224,
         40,
     )(g_attn, tok, gain_sum, dg, dd, out_part, *saved, wqkv, wo, gain_rows, cos, sin, lk, lq, sq)
@@ -1280,17 +1348,9 @@
         + r1 * n1
         - x_own * (r1 * r1 * r1) * jnp.mean(n1 * x_own, axis=-1, keepdims=True)
     )
-    qkv_grad = heads.astype(F32)
-    grad_w_query = qkv_grad[:, :, :256].transpose(1, 0, 2).reshape(64, 2048)
-    grad_w_key = qkv_grad[:, :, 256:384].transpose(1, 0, 2).reshape(64, 1024)
-    grad_w_value = qkv_grad[:, :, 384:].transpose(1, 0, 2).reshape(64, 1024)
-    grad_w_out = outs.astype(F32).reshape(8, 2, 16, 512).transpose(0, 2, 1, 3).reshape(128, width)
-
-    def columns(part):
-        return part.reshape(8, 64, 2, 192).transpose(1, 2, 0, 3).reshape(64, 3072).astype(F32)
-
-    grad_w_gate, grad_w_up = columns(gu[:, :, :384]), columns(gu[:, :, 384:])
-    grad_w_down = down.astype(F32).transpose(1, 0, 2).reshape(192, width)
+    grad_w_query, grad_w_key, grad_w_value, grad_w_out, grad_w_gate, grad_w_up, grad_w_down = (
+        w.astype(F32) for w in weights
+    )
 
     def mine(rows, n):
         return lax.dynamic_slice_in_dim(rows.reshape(-1), f * n, n)

time: 313 us -> 309 us (0.987)
  local copies, waits for them, and re-layouts: 20.7 us -> 5.84 us
  Pallas kernels: 270 us -> 278 us
  other arithmetic: 14.4 us -> 17.6 us
    pallas_call x1, Pallas kernels: 88 us -> 97.3 us  [per_device(): comm_call(front_body, RING_Z + RING_X + RING_Y + WEIGHT_PLANE, [((2, 1024...]
    convert_element_type x3 -> x7, other arithmetic: 1.5 us -> 9.05 us  [per_device(): w.astype(F32)]
    reshape x4 -> x0, local copies, waits for them, and re-layouts: 5.83 us -> none  [the longest x1 1.99 us: per_device(): grad_w_query = qkv_grad[:, :, :256].transpose(1, 0, 2).reshape(64, 2048)]
    convert_element_type x6 -> x0, local copies, waits for them, and re-layouts: 5.28 us -> none  [columns(): part.reshape(8, 64, 2, 192).transpose(1, 2, 0, 3).reshape(64, 3072)]
    neg x1 -> x0, other arithmetic: 3.72 us -> none  [rope_tables(): -sin]
where the time goes in v5:
time: 309 us; the launch traced here: 304 us
  Pallas kernels  278 us (90%)
  other arithmetic  17.6 us (6%)
  local copies, waits for them, and re-layouts  5.84 us (2%)
    pallas_call x1, Pallas kernels, per_device(): comm_call(back_body, RING_Z + RING_X + RING_Y + [{'yl': 1}] + SAMPLE_SHIF...  129 us
    pallas_call x1, Pallas kernels, per_device(): comm_call(front_body, RING_Z + RING_X + RING_Y + WEIGHT_PLANE, [((2, 1024...  97.3 us
    pallas_call x1, Pallas kernels, per_device(): comm_call(feed_body, RING_X, [((2, 128, width), F32), ((2, 128, width), B...  51.1 us
    convert_element_type x7, other arithmetic, per_device(): w.astype(F32)  9.05 us
  transfers between devices with their start and end apart: 1, of which 0 were waited for; matrix products, arithmetic and copies ran while one was open for 1% of the time, Pallas kernels for 0%

profile of v5, /device:TPU:1, one launch (start us, length us, event | category | flops | bytes accessed | tf_op | source)
XLA Modules:
  0.0 303.6 jit_solution(3086167777537530585)
XLA Ops:
  0.6 0.8 fusion.6
  1.5 0.1 copy.33
  1.6 1.4 collective-permute-start
  3.0 0.7 broadcast_multiply_fusion.1
  3.7 0.1 broadcast_in_dim.78
  3.8 0.1 mul.97
  3.9 0.7 broadcast_select_fusion
  4.6 0.1 select_n.114
  4.7 0.1 select_n.116
  4.8 0.6 maximum_bitcast_fusion.refs_12_
  5.4 0.7 broadcast_select_fusion.3
  6.1 0.7 concatenate.6
  6.8 0.0 collective-permute-done
  6.8 0.7 add_reduce_fusion
  7.5 0.7 compare_select_fusion
  8.1 97.3 %shard_map.246 = (f32[2,1024,128]{2,1,0:T(8,128)}, f32[2,1024,128]{2,1,0:T(8,128)}, s32[2,1024,128]{2,1,0:T(8,128)}, f32[2,128,1024]{2,1,0:T(8,128)}, bf16[2,128...) custom-call(bf16[2,128,1024]{2,1,0:T(8,128)(2,1)} %bitcast.27, ...), custom_call_target="tpu_custom_call" | custom-call | tf_op jit(solution)/shard_map/pallas_call | solution.py:1254
  105.4 0.8 slice.15
  106.2 51.1 %shard_map.247 = (f32[2,128,1024]{2,1,0:T(8,128)}, bf16[2,128,1024]{2,1,0:T(8,128)(2,1)}, f32[8,1024]{1,0:T(8,128)}, bf16[2,4,2,64,768]{4,3,2,1,0:T(8,128)(2,1)}...) custom-call(bf16[2,128,1024]{2,1,0:T(8,128)(2,1)} %get-tuple-element.48.refs_0_, ...), custom_call_target="tpu_custom_call" | custom-call | tf_op jit(solution)/shard_map/pallas_call | solution.py:1287
  157.3 0.0 copy-start
  157.3 129.4 %shard_map.248 = (bf16[2,128,1024]{2,1,0:T(8,128)(2,1)}, f32[2,128,1024]{2,1,0:T(8,128)}, f32[24,128]{1,0:T(8,128)}, bf16[64,2048]{1,0:T(8,128)(2,1)}, bf16[64,1...) custom-call(bf16[2,128,1024]{2,1,0:T(8,128)(2,1)} %get-tuple-element, ...), custom_call_target="tpu_custom_call" | custom-call | tf_op jit(solution)/shard_map/pallas_call | solution.py:1307
  286.7 0.0 copy-start.6
  286.7 0.0 copy-start.5
  286.7 0.0 copy-start.1
  286.7 0.0 copy-start.4
  286.7 0.8 slice_bitcast_fusion
  287.6 0.8 fusion.10
  288.3 0.0 copy-done
  288.3 1.4 fusion
  289.7 0.0 copy-start.2
  289.8 0.0 copy-start.3
  289.8 2.0 convert_element_type.42
  291.8 1.9 convert_element_type.43
  293.7 2.0 convert_element_type.44
  295.7 0.0 copy-done.6
  295.7 0.8 convert_element_type.38
  296.5 0.0 copy-done.5
  296.5 0.8 convert_element_type.41
  297.4 0.0 copy-done.1
  297.4 0.9 fusion.5
  298.3 0.7 convert_element_type.39
  299.1 0.0 copy-done.7
  299.1 0.7 convert_element_type.40
  299.8 0.6 dynamic_slice.16
  300.4 0.6 dynamic_slice.21
  300.9 0.6 dynamic-slice_bitcast_fusion
  301.5 0.6 dynamic-slice_bitcast_fusion.1
  302.1 0.0 copy-done.2
  302.1 1.3 fusion.3
  (11 shorter events, 0.0 us)
Async XLA Ops:
  1.6 5.2 %collective-permute-start = (s32[2,1]{1,0:T(2,128)S(1)}, s32[2,1]{1,0:T(2,128)S(1)}, u32[]{:S(2)}, u32[]{:S(2)}) collective-permute-start(s32[2,1]{1,0:T(2,128)S(1)} %copy.33), channel_id=1, source_target_pairs={{0,1},{1,0},{2,3},{3,2},{4,5},{5,4},{6,7},{7,6},{8,9},{9,8},{10,11... | collective-permute-start | bytes 32 | tf_op jit(solution)/shard_map/ppermute | solution.py:1236
  157.3 131.1 %copy-start = (bf16[2,1,128,1024]{3,2,1,0:T(8,128)(2,1)S(1)}, bf16[2,1,128,1024]{3,2,1,0:T(8,128)(2,1)}, u32[]{:S(2)}) copy-start(bf16[2,1,128,1024]{3,2,1,0:T(8,128)(2,1)} %param.16) | copy-start | bytes 1572868
  286.7 9.0 %copy-start.6 = (bf16[64,2048]{1,0:T(8,128)(2,1)S(1)}, bf16[64,2048]{1,0:T(8,128)(2,1)}, u32[]{:S(2)}) copy-start(bf16[64,2048]{1,0:T(8,128)(2,1)} %get-tuple-element.74) | copy-start | bytes 786436
  286.7 9.8 %copy-start.5 = (bf16[128,1024]{1,0:T(8,128)(2,1)S(1)}, bf16[128,1024]{1,0:T(8,128)(2,1)}, u32[]{:S(2)}) copy-start(bf16[128,1024]{1,0:T(8,128)(2,1)} %get-tuple-element.77) | copy-start | bytes 786436
  286.7 10.7 %copy-start.1 = (f32[2,128,1024]{2,1,0:T(8,128)S(1)}, f32[2,128,1024]{2,1,0:T(8,128)}, u32[]{:S(2)}) copy-start(f32[2,128,1024]{2,1,0:T(8,128)} %get-tuple-element.47.refs_1_) | copy-start | bytes 3145732
  286.7 10.7 %copy-start.4 = (f32[2,128,1024]{2,1,0:T(8,128)S(1)}, f32[2,128,1024]{2,1,0:T(8,128)}, u32[]{:S(2)}) copy-start(f32[2,128,1024]{2,1,0:T(8,128)} %get-tuple-element.70) | copy-start | bytes 3145732
  288.3 10.0 %copy-start.8 = (bf16[64,1024]{1,0:T(8,128)(2,1)S(1)}, bf16[64,1024]{1,0:T(8,128)(2,1)}, u32[]{:S(2)}) copy-start(bf16[64,1024]{1,0:T(8,128)(2,1)} %get-tuple-element.75) | copy-start | bytes 393220
  289.7 9.3 %copy-start.7 = (bf16[64,1024]{1,0:T(8,128)(2,1)S(1)}, bf16[64,1024]{1,0:T(8,128)(2,1)}, u32[]{:S(2)}) copy-start(bf16[64,1024]{1,0:T(8,128)(2,1)} %get-tuple-element.76) | copy-start | bytes 393220
  289.7 12.4 %copy-start.2 = (bf16[2,128,1024]{2,1,0:T(8,128)(2,1)S(1)}, bf16[2,128,1024]{2,1,0:T(8,128)(2,1)}, u32[]{:S(2)}) copy-start(bf16[2,128,1024]{2,1,0:T(8,128)(2,1)} %get-tuple-element.72) | copy-start | bytes 1572868
  289.8 12.4 %copy-start.3 = (f32[2,128,1024]{2,1,0:T(8,128)S(1)}, f32[2,128,1024]{2,1,0:T(8,128)}, u32[]{:S(2)}) copy-start(f32[2,128,1024]{2,1,0:T(8,128)} %get-tuple-element.71) | copy-start | bytes 3145732

commit v6 on v5

--- a/solution.py
+++ b/solution.py
@@ -710,21 +710,21 @@
     return block
 
 
-def front_first(
-    tok, cot, small, wq, wk, wv, wo_in, wg, wu, wd, table, first, frequency, lq, sq, cos, sin, lk, *_
-):
-    make_tables(0, table, first, frequency, cos, sin, lk)
+def front_first(*refs):
+    table, first, frequency = refs[10:13]
+    make_tables(0, table, first, frequency, *refs[-3:])
 
 
 def front_body(
     net,
     tok, cot, small, wq, wk, wv, wo_in, wg, wu, wd, table, first, frequency, lq, sq,
-    cos, sin, lk, attended, normed, gains, wqkv, wo, cots, wgu, wds, mid,
+    cos_out, sin_out, lk_out, attended, normed, gains, wqkv_out, wo_out, cots, wgu, wds, mid,
     xn_out, raw_out, q_out, k_out, v_out, mixt_out, rl_out,
     xn, raw, q, k, v, mixt, rl,
     xs, part, mixed, vt, stage, smalls, gu_stage, outbox, inbox, *bufs,
 ):
     me = net.me
+    wqkv, wo, cos, sin, lk = bufs[-5:]
     heads = gather_heads_weights(net, wq, wk, wv, small, stage, wqkv, smalls)
     next(heads)
     swaps = [net.swap(tok.at[m], xs.at[m, ctx_of(me)]) for m in range(2)]
@@ -742,6 +742,8 @@
     own_cot = net.local(cot, cots.at[:, tp_of(me)])
     next(heads)
     make_tables(1, table, first, frequency, cos, sin, lk)
+    for src, dst in ((cos, cos_out), (sin, sin_out), (lk, lk_out)):
+        net.local(src, dst)
     swaps[0].wait()
     next(gather[0])
     next(heads)
@@ -800,6 +802,8 @@
     step(cots_in)
     drain(gather[1])
     save(0)
+    net.local(wqkv, wqkv_out)
+    net.local(wo, wo_out)
     work[1].projection()
     step(reduces[0])
     for at, k in enumerate(TILES):
@@ -862,11 +866,12 @@
 
 def feed_body(
     net,
-    normed, attended, cot, cots, wgu, wds, gains,
+    normed, attended, cot, cots_in, wgu_in, wds_in, gains,
     g_attended, g_attn, gain_sum, dg_low, dd_low, out_part_out,
-    nm, hid, ggu, out_part, mid_part, dg, dd, total, *bufs,
+    nm, hid, ggu, out_part, mid_part, dg, dd, total, cots, wgu, wds, *bufs,
 ):
     me = net.me
+    loads = [net.local(*pair) for pair in ((wgu_in, wgu), (wds_in, wds), (cots_in, cots))]
 
     def block(m):
         def at(place, lo, n):
@@ -879,7 +884,7 @@
     next(gather[0])
     next(gather[0])
     next(gather[1])
-    for copy in own:
+    for copy in own + loads:
         net.settle(copy)
     drain(gather[0])
     work = [Feed(m, wgu, wds, nm, cots, hid, ggu, out_part, mid_part, dg, dd) for m in range(2)]
@@ -1007,8 +1012,9 @@
 
 def back_body(
     net,
-    g_own, tok, gain_sum, dg, dd, out_part_in, xn_in, raw_in, q_in, k_in, v_in, mixt_in, rl_in,
-    wqkv, wo, gains, cos, sin, lk, lq, sq,
+    g_own, tok, gain_sum, dg_in, dd_in, out_part_in,
+    xn_in, raw_in, q_in, k_in, v_in, mixt_in, rl_in,
+    wqkv_in, wo_in_, gains, cos_in, sin_in, lk_in, lq, sq,
     in_sum, out_sum, gain_total,
     gq, gk, gv, gwo, gate, up, gwd,
     xn, raw, q, k, v, mixt, rl,
@@ -1019,6 +1025,7 @@
 ):
     me = net.me
     ff, bufs = bufs[:10], bufs[10:]
+    dg, dd, wqkv, wo, cos, sin, lk = bufs[-7:]
     swaps = [net.swap(g_own.at[m], g.at[m, ctx_of(me)]) for m in range(2)]
     fetched = [net.local(out_part_in.at[0], out_part.at[0])]
     saved = (xn, raw, q, k, v, mixt, rl)
@@ -1028,6 +1035,13 @@
         for src, dst in zip((xn_in, raw_in, q_in, k_in, v_in, mixt_in, rl_in), saved)
     ]
     fetched.append(net.local(out_part_in.at[1], out_part.at[1]))
+    needed += [
+        net.local(*pair)
+        for pair in (
+            (dg_in, dg), (dd_in, dd), (wqkv_in, wqkv), (wo_in_, wo),
+            (cos_in, cos), (sin_in, sin), (lk_in, lk),
+        )
+    ]
     sums[...] = jnp.zeros_like(sums)
     gather = [
         gather_ring(net, "z", g.at[m, head_of(me)], sequence_block(g.at[m]), 128) for m in range(2)
@@ -1070,9 +1084,9 @@
     next(gather[1])
     next(gather[0])
     drain(gather[0])
-    next(feed)
     for copy in needed:
         net.settle(copy)
+    next(feed)
     net.settle(fetched[1])
     tables = (cos, sin, lk, lq, sq)
     work = [
@@ -1251,6 +1265,13 @@
         ((2, 2, 1, 1024), F32),
     ]
     sequence = vm((2, 8, 128, width), BF)
+    shared = [
+        vm((2, 8, 2, 32, 512), BF),
+        vm((2, 8, 16, width), BF),
+        vm((2, 1024, HEAD), F32),
+        vm((2, 1024, HEAD), F32),
+        vm((2, 1024, HEAD), jnp.int32),
+    ]
     cos, sin, lk, attended, normed, gain_rows, wqkv, wo, cots, wgu, wds, _, *saved = comm_call(
         front_body,
         RING_Z + RING_X + RING_Y + WEIGHT_PLANE,
@@ -1273,10 +1294,11 @@
         + [sequence, sequence, vm((1024, 256), BF), vm((HEAD, 1024), BF)]
         + [vm((2, 32, 512), BF), vm((16, 16, HEAD), BF), vm((8, 64, 768), BF)]
         + [vm((2, 128, width), BF), vm((2, 128, width), BF)]
-        + reduce_ring_scratch(width) * 2,
+        + reduce_ring_scratch(width) * 2
+        + shared,
         0,
         [True] + [False] * 6 + [True] * 2 + [False] + [None] * 2 + [True] * 3,
-        [True] * 8 + [False] * 11,
+        [False] * 3 + [True] * 3 + [False] * 13,
         160,
         64,
         front_first,
@@ -1297,12 +1319,13 @@
         ],
         [sequence, vm((2, 1024, 384), BF), vm((2, 1024, 768), BF), sequence, sequence]
         + [vm((1024, 768), F32), vm((384, width), F32), vm((2, 128, width), F32)]
+        + [sequence, vm((2, 8, 2, 32, 768), BF), vm((2, 192, width), BF)]
         + reduce_ring_scratch(width) * 2,
         1,
-        [True] * 7,
+        [True] * 3 + [False] * 3 + [True],
         [True] * 5 + [False],
         64,
-        8,
+        12,
     )(normed, attended, cotangent[:, 0], cots, wgu, wds, gain_rows)
     in_sum, out_sum, gain_total, *weights = comm_call(
         back_body,
@@ -1331,12 +1354,14 @@
         + [vm((8, 64, 768), BF), vm((8, 64, 512), BF), vm((8, 32, 512), BF), vm((8, 192, 128), BF)]
         + [vm((24, HEAD), F32), vm((7, 24, HEAD), F32), vm((24, HEAD), F32), vm((15, 24, HEAD), F32)]
         + reduce_ff_scratch()
-        + reduce_ring_scratch(width) * 4,
+        + reduce_ring_scratch(width) * 4
+        + [vm((2, 4, 2, 64, 768), BF), vm((2, 2, 4, 192, 128), BF)]
+        + shared,
         2,
-        [True] * 5 + [False] * 8 + [True] * 8,
+        [True] * 3 + [False] * 12 + [True] + [False] * 3 + [True] * 2,
         [True] * 10,
         224,
-        40,
+        56,
     )(g_attn, tok, gain_sum, dg, dd, out_part, *saved, wqkv, wo, gain_rows, cos, sin, lk, lq, sq)
     output = (attended + out_sum).astype(BF)
     g_in = in_sum.astype(F32)

time: 309 us -> 294 us (0.951)
  Pallas kernels: 278 us -> 264 us
    pallas_call x1, Pallas kernels: 97.3 us -> 86.2 us  [per_device(): comm_call(front_body, RING_Z + RING_X + RING_Y + WEIGHT_PLANE, [((2, 1024...]
    pallas_call x1, Pallas kernels: 51.1 us -> 48 us  [per_device(): comm_call(feed_body, RING_X, [((2, 128, width), F32), ((2, 128, width), B...]
where the time goes in v6:
time: 294 us; the launch traced here: 290 us
  Pallas kernels  264 us (90%)
  other arithmetic  17.6 us (6%)
  local copies, waits for them, and re-layouts  5.84 us (2%)
    pallas_call x1, Pallas kernels, per_device(): comm_call(back_body, RING_Z + RING_X + RING_Y + [{'yl': 1}] + SAMPLE_SHIF...  130 us
    pallas_call x1, Pallas kernels, per_device(): comm_call(front_body, RING_Z + RING_X + RING_Y + WEIGHT_PLANE, [((2, 1024...  86.2 us
    pallas_call x1, Pallas kernels, per_device(): comm_call(feed_body, RING_X, [((2, 128, width), F32), ((2, 128, width), B...  48 us
    convert_element_type x7, other arithmetic, per_device(): w.astype(F32)  9.05 us
  transfers between devices with their start and end apart: 1, of which 0 were waited for; matrix products, arithmetic and copies ran while one was open for 1% of the time, Pallas kernels for 0%

profile of v6, /device:TPU:1, one launch (start us, length us, event | category | flops | bytes accessed | tf_op | source)
XLA Modules:
  0.0 290.4 jit_solution(11355236442859466076)
XLA Ops:
  0.6 0.8 fusion.6
  1.5 0.1 copy.33
  1.6 1.4 collective-permute-start
  3.0 0.7 broadcast_multiply_fusion.1
  3.7 0.1 broadcast_in_dim.78
  3.8 0.1 mul.97
  3.9 0.7 broadcast_select_fusion
  4.6 0.1 select_n.114
  4.7 0.1 select_n.116
  4.8 0.6 maximum_bitcast_fusion.refs_12_
  5.4 0.7 broadcast_select_fusion.3
  6.1 0.7 concatenate.6
  6.8 0.0 collective-permute-done
  6.8 0.7 add_reduce_fusion
  7.5 0.7 compare_select_fusion
  8.1 86.2 %shard_map.246 = (f32[2,1024,128]{2,1,0:T(8,128)}, f32[2,1024,128]{2,1,0:T(8,128)}, s32[2,1024,128]{2,1,0:T(8,128)}, f32[2,128,1024]{2,1,0:T(8,128)}, bf16[2,128...) custom-call(bf16[2,128,1024]{2,1,0:T(8,128)(2,1)} %bitcast.27, ...), custom_call_target="tpu_custom_call" | custom-call | tf_op jit(solution)/shard_map/pallas_call | solution.py:1275
  94.3 0.8 slice.15
  95.1 48.0 %shard_map.247 = (f32[2,128,1024]{2,1,0:T(8,128)}, bf16[2,128,1024]{2,1,0:T(8,128)(2,1)}, f32[8,1024]{1,0:T(8,128)}, bf16[2,4,2,64,768]{4,3,2,1,0:T(8,128)(2,1)}...) custom-call(bf16[2,128,1024]{2,1,0:T(8,128)(2,1)} %get-tuple-element.48.refs_0_, ...), custom_call_target="tpu_custom_call" | custom-call | tf_op jit(solution)/shard_map/pallas_call | solution.py:1309
  143.0 0.0 copy-start
  143.0 130.2 %shard_map.248 = (bf16[2,128,1024]{2,1,0:T(8,128)(2,1)}, f32[2,128,1024]{2,1,0:T(8,128)}, f32[24,128]{1,0:T(8,128)}, bf16[64,2048]{1,0:T(8,128)(2,1)}, bf16[64,1...) custom-call(bf16[2,128,1024]{2,1,0:T(8,128)(2,1)} %get-tuple-element, ...), custom_call_target="tpu_custom_call" | custom-call | tf_op jit(solution)/shard_map/pallas_call | solution.py:1330
  273.3 0.0 copy-start.6
  273.3 0.0 copy-start.5
  273.3 0.0 copy-start.1
  273.3 0.0 copy-start.4
  273.3 0.8 slice_bitcast_fusion
  274.1 0.8 fusion.10
  274.9 0.0 copy-done
  274.9 1.4 fusion
  276.3 0.0 copy-start.2
  276.3 0.0 copy-start.3
  276.3 2.0 convert_element_type.42
  278.4 1.9 convert_element_type.43
  280.3 2.0 convert_element_type.44
  282.3 0.0 copy-done.6
  282.3 0.8 convert_element_type.38
  283.1 0.0 copy-done.5
  283.1 0.8 convert_element_type.41
  283.9 0.0 copy-done.1
  284.0 0.0 copy-done.4
  284.0 0.9 fusion.5
  284.9 0.0 copy-done.8
  284.9 0.7 convert_element_type.39
  285.6 0.7 convert_element_type.40
  286.4 0.6 dynamic_slice.16
  286.9 0.6 dynamic_slice.21
  287.5 0.6 dynamic-slice_bitcast_fusion
  288.1 0.6 dynamic-slice_bitcast_fusion.1
  288.7 1.3 fusion.3
  (11 shorter events, 0.0 us)
Async XLA Ops:
  1.6 5.2 %collective-permute-start = (s32[2,1]{1,0:T(2,128)S(1)}, s32[2,1]{1,0:T(2,128)S(1)}, u32[]{:S(2)}, u32[]{:S(2)}) collective-permute-start(s32[2,1]{1,0:T(2,128)S(1)} %copy.33), channel_id=1, source_target_pairs={{0,1},{1,0},{2,3},{3,2},{4,5},{5,4},{6,7},{7,6},{8,9},{9,8},{10,11... | collective-permute-start | bytes 32 | tf_op jit(solution)/shard_map/ppermute | solution.py:1250
  143.0 131.8 %copy-start = (bf16[2,1,128,1024]{3,2,1,0:T(8,128)(2,1)S(1)}, bf16[2,1,128,1024]{3,2,1,0:T(8,128)(2,1)}, u32[]{:S(2)}) copy-start(bf16[2,1,128,1024]{3,2,1,0:T(8,128)(2,1)} %param.16) | copy-start | bytes 1572868
  273.3 9.0 %copy-start.6 = (bf16[64,2048]{1,0:T(8,128)(2,1)S(1)}, bf16[64,2048]{1,0:T(8,128)(2,1)}, u32[]{:S(2)}) copy-start(bf16[64,2048]{1,0:T(8,128)(2,1)} %get-tuple-element.74) | copy-start | bytes 786436
  273.3 9.8 %copy-start.5 = (bf16[128,1024]{1,0:T(8,128)(2,1)S(1)}, bf16[128,1024]{1,0:T(8,128)(2,1)}, u32[]{:S(2)}) copy-start(bf16[128,1024]{1,0:T(8,128)(2,1)} %get-tuple-element.77) | copy-start | bytes 786436
  273.3 10.7 %copy-start.1 = (f32[2,128,1024]{2,1,0:T(8,128)S(1)}, f32[2,128,1024]{2,1,0:T(8,128)}, u32[]{:S(2)}) copy-start(f32[2,128,1024]{2,1,0:T(8,128)} %get-tuple-element.47.refs_1_) | copy-start | bytes 3145732
  273.3 10.7 %copy-start.4 = (f32[2,128,1024]{2,1,0:T(8,128)S(1)}, f32[2,128,1024]{2,1,0:T(8,128)}, u32[]{:S(2)}) copy-start(f32[2,128,1024]{2,1,0:T(8,128)} %get-tuple-element.70) | copy-start | bytes 3145732
  274.9 10.0 %copy-start.8 = (bf16[64,1024]{1,0:T(8,128)(2,1)S(1)}, bf16[64,1024]{1,0:T(8,128)(2,1)}, u32[]{:S(2)}) copy-start(bf16[64,1024]{1,0:T(8,128)(2,1)} %get-tuple-element.75) | copy-start | bytes 393220
  276.3 9.3 %copy-start.7 = (bf16[64,1024]{1,0:T(8,128)(2,1)S(1)}, bf16[64,1024]{1,0:T(8,128)(2,1)}, u32[]{:S(2)}) copy-start(bf16[64,1024]{1,0:T(8,128)(2,1)} %get-tuple-element.76) | copy-start | bytes 393220
  276.3 12.4 %copy-start.2 = (bf16[2,128,1024]{2,1,0:T(8,128)(2,1)S(1)}, bf16[2,128,1024]{2,1,0:T(8,128)(2,1)}, u32[]{:S(2)}) copy-start(bf16[2,128,1024]{2,1,0:T(8,128)(2,1)} %get-tuple-element.72) | copy-start | bytes 1572868
  276.3 12.4 %copy-start.3 = (f32[2,128,1024]{2,1,0:T(8,128)S(1)}, f32[2,128,1024]{2,1,0:T(8,128)}, u32[]{:S(2)}) copy-start(f32[2,128,1024]{2,1,0:T(8,128)} %get-tuple-element.71) | copy-start | bytes 3145732
